TPU v7x, 32 devices: a whole 2x2x4 slice. The times are simulated.
32 devices in a mesh: dp: 8 (over z, x), tensor: 4 (over y, core).
Axes of the slice: x: 2, y: 2, z: 4, core: 2. Of those that a mesh axis runs over, the one named last changes fastest.
Arguments:
- layer_inputs: bfloat16 [64, 512, 768], P(('dp', 'tensor')), may hold values from -6 to 6
- lengths: int32 [64], P(('dp', 'tensor')), may hold values from 64 to 512, as said below
- first_norm1_gain: float32 [768], replicated, may hold values from 0.1 to 1.9
- second_norm2_gain: float32 [768], replicated, may hold values from 0.1 to 1.9
- router: bfloat16 [768, 10], replicated, may hold values from -0.099609375 to 0.099609375
- query_key_value_weight: bfloat16 [3, 768, 768], P(None, None, 'tensor'), may hold values from -0.078125 to 0.078125
- relative_position_bias: bfloat16 [32, 12], P(None, 'tensor'), may hold values from -4 to 4
- attention_output_weight: bfloat16 [768, 768], P('tensor'), may hold values from -1.75 to 1.75
- input_weight: bfloat16 [768, 3072], P(None, 'tensor'), may hold values from -0.21875 to 0.21875
- output_weight: bfloat16 [3072, 768], P('tensor'), may hold values from -0.109375 to 0.109375
- adapter_down_input: bfloat16 [4, 768, 40], replicated, may hold values from -0.21875 to 0.21875
- adapter_down_attention: bfloat16 [768, 40], replicated, may hold values from -1.75 to 1.75
- adapter_down_output: bfloat16 [3072, 40], replicated, may hold values from -0.109375 to 0.109375
- adapter_up_query_key_value: bfloat16 [3, 40, 768], P(None, None, 'tensor'), may hold values from -3 to 3
- adapter_up_attention: bfloat16 [40, 768], replicated, may hold values from -3 to 3
- adapter_up_input: bfloat16 [40, 3072], P(None, 'tensor'), may hold values from -3 to 3
- adapter_up_output: bfloat16 [40, 768], replicated, may hold values from -3 to 3
- cotangent: bfloat16 [64, 512, 768], P(('dp', 'tensor')), may hold values from -6 to 6
Outputs:
- layer_output: bfloat16 [64, 512, 768], P(('dp', 'tensor'))
- grad_input: float32 [64, 512, 768], P(('dp', 'tensor'))
- grad_router: float32 [768, 10], replicated
- grad_lora_a_in: float32 [4, 768, 40], replicated
- grad_lora_a_o: float32 [768, 40], replicated
- grad_lora_a_out: float32 [3072, 40], replicated
- grad_lora_b_qkv: float32 [3, 40, 768], P(None, None, 'tensor')
- grad_lora_b_o: float32 [40, 768], replicated
- grad_lora_b_in: float32 [40, 3072], P(None, 'tensor')
- grad_lora_b_out: float32 [40, 768], replicated
Inputs may be any that keep to these rules, and one draw needn't show every extreme that they name: `lengths`: each device's first sequence has all 512 tokens.
All inputs are finite; a program needn't handle non-finite values.
Results may differ from a plain program's by a relative error of at most 0.018.
The roundings to bfloat16 on the way count: a program that leaves them out, or rounds other values in their place, can miss the bound.
Values may be sent and summed in bfloat16 or wider, within the bound.
A program may use at most 192 MiB of HBM per device.

v0:
```python
from functools import partial

import jax
import jax.numpy as jnp
import numpy as np
from jax import lax
from jax.sharding import PartitionSpec as P

NB = 32
MAX_DIST = 128


EPSILON = 1e-06
NEGATIVE = -1000000000.0
SINGLE_FLOAT32 = jnp.float32
BRAIN_FLOAT16 = jnp.bfloat16


def bucket_table(seq_length):
    places = np.arange(seq_length)
    relative = places[None, :] - places[:, None]
    half_count = NB // 2
    exact_count = half_count // 2
    distance = np.abs(relative)
    scaled = (
        np.log(np.maximum(distance, 1) / exact_count)
        / np.log(MAX_DIST / exact_count)
        * (half_count - exact_count)
    )
    far_bucket = np.minimum(exact_count + scaled.astype(np.int32), half_count - 1)
    return (
        (relative > 0) * half_count + np.where(distance < exact_count, distance, far_bucket)
    ).astype(np.int32)


def matrix_product(a, b):
    return jnp.dot(a, b, preferred_element_type=SINGLE_FLOAT32)


def matmul_tn(a, b):
    return lax.dot_general(a, b, (((0,), (0,)), ((), ())), preferred_element_type=SINGLE_FLOAT32)


def matrix_product_transposed(a, b):
    return lax.dot_general(
        a, b, (((a.ndim - 1,), (b.ndim - 1,)), ((), ())), preferred_element_type=SINGLE_FLOAT32
    )


def rms_norm(values, gain_vec):
    return (
        values * lax.rsqrt(jnp.mean(values * values, axis=-1, keepdims=True) + EPSILON) * gain_vec
    )


def rms_back(values, gain_vec, upstream):
    inv_rms = lax.rsqrt(jnp.mean(values * values, axis=-1, keepdims=True) + EPSILON)
    scaled_grad = upstream * gain_vec
    return inv_rms * scaled_grad - values * inv_rms**3 * jnp.mean(
        values * scaled_grad, axis=-1, keepdims=True
    )


def gate_grad(d_lowrank, lowrank, experts, rank_size):
    row_count = d_lowrank.shape[0]
    return (d_lowrank * lowrank).reshape(row_count, -1, experts, rank_size).sum(axis=(1, 3))


def masked_scores(q_seq, k_seq, key_valid, bias_all):
    scores = (
        jnp.einsum("qhd,khd->hqk", q_seq, k_seq, preferred_element_type=SINGLE_FLOAT32) + bias_all
    )
    return jnp.where(key_valid[None, None, :] > 0, scores, NEGATIVE)


def attend(inputs, bias_all):
    q_seq, k_seq, v_seq, key_valid = inputs
    masked = masked_scores(q_seq, k_seq, key_valid, bias_all)
    row_max = jnp.max(masked, axis=-1, keepdims=True)
    exp_scores = jnp.exp(masked - row_max)
    exp_total = jnp.sum(exp_scores, axis=-1, keepdims=True)
    attn_probs = exp_scores / exp_total
    context_rows = jnp.einsum(
        "hqk,khd->qhd",
        attn_probs.astype(BRAIN_FLOAT16),
        v_seq,
        preferred_element_type=SINGLE_FLOAT32,
    )
    return (
        context_rows.reshape(q_seq.shape[0], -1).astype(BRAIN_FLOAT16),
        (row_max + jnp.log(exp_total))[..., 0],
    )


def attend_back(inputs, bias_all):
    q_seq, k_seq, v_seq, key_valid, log_total, d_context = inputs
    masked = masked_scores(q_seq, k_seq, key_valid, bias_all)
    attn_probs = jnp.exp(masked - log_total[..., None])
    d_heads = d_context.reshape(q_seq.shape)
    d_value = jnp.einsum(
        "hqk,qhd->khd",
        attn_probs.astype(BRAIN_FLOAT16),
        d_heads,
        preferred_element_type=SINGLE_FLOAT32,
    )
    d_probs = jnp.einsum("qhd,khd->hqk", d_heads, v_seq, preferred_element_type=SINGLE_FLOAT32)
    d_scores = (
        attn_probs * (d_probs - jnp.sum(attn_probs * d_probs, axis=-1, keepdims=True))
    ).astype(BRAIN_FLOAT16)
    d_query = jnp.einsum("hqk,khd->qhd", d_scores, k_seq, preferred_element_type=SINGLE_FLOAT32)
    d_key = jnp.einsum("hqk,qhd->khd", d_scores, q_seq, preferred_element_type=SINGLE_FLOAT32)
    seq_length = q_seq.shape[0]
    return (
        d_query.reshape(seq_length, -1).astype(BRAIN_FLOAT16),
        d_key.reshape(seq_length, -1).astype(BRAIN_FLOAT16),
        d_value.reshape(seq_length, -1).astype(BRAIN_FLOAT16),
    )


def shards(
    layer_inputs,
    lengths,
    first_norm1_gain,
    second_norm2_gain,
    router,
    query_key_value_weight,
    relative_position_bias,
    attention_output_weight,
    input_weight,
    output_weight,
    adapter_down_input,
    adapter_down_attention,
    adapter_down_output,
    adapter_up_query_key_value,
    adapter_up_attention,
    adapter_up_input,
    adapter_up_output,
    cotangent,
):
    groups = lax.axis_size("tensor")
    member = lax.axis_index("tensor")
    seqs_home, seq_length, width_model = layer_inputs.shape
    home_rows = seqs_home * seq_length
    experts = router.shape[1]
    adapter_columns = adapter_down_input.shape[2]
    rank_size = adapter_columns // experts
    inner_total = adapter_down_attention.shape[0]
    feedforward_full = adapter_down_output.shape[0]
    local_inner = inner_total // groups
    local_ffn = feedforward_full // groups
    inner_offset = member * local_inner
    feedforward_start = member * local_ffn
    inner_local = attention_output_weight.shape[0]
    feedforward_local = output_weight.shape[0]
    heads_here = relative_position_bias.shape[1]
    head_dim = inner_local // heads_here
    attn_down_rows = lax.dynamic_slice_in_dim(adapter_down_attention, inner_offset, inner_local, 0)
    output_down_rows = lax.dynamic_slice_in_dim(
        adapter_down_output, feedforward_start, feedforward_local, 0
    )

    def take_home(values):
        picked = lax.dynamic_slice_in_dim(values, member * home_rows, home_rows, 0)
        return picked

    def widen(values, full_size, along, start):
        blank = jnp.zeros(
            values.shape[:along] + (full_size,) + values.shape[along + 1 :], SINGLE_FLOAT32
        )
        widened = lax.dynamic_update_slice_in_dim(blank, values, start, along)
        return widened

    bucket_ids = jnp.asarray(bucket_table(seq_length))
    bias_all = jnp.transpose(
        jnp.take(relative_position_bias, bucket_ids, axis=0).astype(SINGLE_FLOAT32), (2, 0, 1)
    )
    input_local = layer_inputs.reshape(home_rows, width_model).astype(SINGLE_FLOAT32)
    key_valid = (jnp.arange(seq_length)[None, :] < lengths[:, None]).astype(BRAIN_FLOAT16)
    first_normed1 = rms_norm(input_local, first_norm1_gain).astype(BRAIN_FLOAT16)
    rows_first, valid_rows = (
        lax.all_gather(first_normed1, "tensor", axis=0, tiled=True),
        lax.all_gather(key_valid, "tensor", axis=0, tiled=True),
    )
    row_count = rows_first.shape[0]
    seq_count = valid_rows.shape[0]
    gate_probs = jax.nn.softmax(matrix_product(rows_first, router), axis=-1)
    gate_repeated = jnp.repeat(gate_probs, rank_size, axis=1)
    gates_home = take_home(gate_probs)
    rep_home = take_home(gate_repeated)
    down_query_key_value = jnp.transpose(adapter_down_input[:3], (1, 0, 2)).reshape(
        width_model, 3 * adapter_columns
    )
    lowrank_qkv = matrix_product(rows_first, down_query_key_value)
    gated_query_key_value = (
        (lowrank_qkv * jnp.tile(gate_repeated, (1, 3)))
        .astype(BRAIN_FLOAT16)
        .reshape(row_count, 3, adapter_columns)
    )
    projected_rows = jnp.einsum(
        "td,pdc->ptc", rows_first, query_key_value_weight, preferred_element_type=SINGLE_FLOAT32
    )
    projected_rows = (
        projected_rows
        + jnp.einsum(
            "afe,feb->fab",
            gated_query_key_value,
            adapter_up_query_key_value,
            preferred_element_type=SINGLE_FLOAT32,
        )
    ).astype(BRAIN_FLOAT16)
    split_qkv = projected_rows.reshape(3, seq_count, seq_length, heads_here, head_dim)
    context_rows, log_total = lax.map(
        partial(attend, bias_all=bias_all), (split_qkv[0], split_qkv[1], split_qkv[2], valid_rows)
    )
    context_rows = context_rows.reshape(row_count, inner_local)
    part_attn = matrix_product(context_rows, attention_output_weight)
    part_low_o = matrix_product(context_rows, attn_down_rows)
    attention_local, low_o = (
        lax.psum_scatter(part_attn, "tensor", scatter_dimension=0, tiled=True),
        lax.psum_scatter(part_low_o, "tensor", scatter_dimension=0, tiled=True),
    )
    gated_attention = (low_o * rep_home).astype(BRAIN_FLOAT16)
    hidden_first1 = (
        input_local + attention_local + matrix_product(gated_attention, adapter_up_attention)
    )
    second_normed2 = rms_norm(hidden_first1, second_norm2_gain).astype(BRAIN_FLOAT16)
    second_rows = lax.all_gather(second_normed2, "tensor", axis=0, tiled=True)
    lowrank_input = matrix_product(second_rows, adapter_down_input[3])
    gated_input = (lowrank_input * gate_repeated).astype(BRAIN_FLOAT16)
    preactivation = matrix_product(second_rows, input_weight) + matrix_product(
        gated_input, adapter_up_input
    )
    active_flags = jax.nn.silu(preactivation).astype(BRAIN_FLOAT16)
    part_ffn = matrix_product(active_flags, output_weight)
    part_low_out = matrix_product(active_flags, output_down_rows)
    feedforward_home, low_out = (
        lax.psum_scatter(
            part_ffn.astype(jnp.bfloat16), "tensor", scatter_dimension=0, tiled=True
        ).astype(jnp.float32),
        lax.psum_scatter(
            part_low_out.astype(jnp.bfloat16), "tensor", scatter_dimension=0, tiled=True
        ).astype(jnp.float32),
    )
    gated_output = (low_out * rep_home).astype(BRAIN_FLOAT16)
    layer_output = (
        (hidden_first1 + feedforward_home + matrix_product(gated_output, adapter_up_output))
        .astype(BRAIN_FLOAT16)
        .reshape(layer_inputs.shape)
    )
    d_output = cotangent.reshape(home_rows, width_model)
    grad_second_rows = lax.all_gather(d_output, "tensor", axis=0, tiled=True)
    grad_lowrank_output = matrix_product_transposed(grad_second_rows, adapter_up_output)
    d_gated_out = (grad_lowrank_output * gate_repeated).astype(BRAIN_FLOAT16)
    d_active = matrix_product_transposed(
        grad_second_rows, output_weight
    ) + matrix_product_transposed(d_gated_out, output_down_rows)
    sigmoid_pre = jax.nn.sigmoid(preactivation)
    grad_preactivation = (
        d_active * sigmoid_pre * (1.0 + preactivation * (1.0 - sigmoid_pre))
    ).astype(BRAIN_FLOAT16)
    grad_a_out = widen(matmul_tn(active_flags, d_gated_out), feedforward_full, 0, feedforward_start)
    grad_b_in = widen(
        matmul_tn(gated_input, grad_preactivation), feedforward_full, 1, feedforward_start
    )
    part_norm2 = matrix_product_transposed(grad_preactivation, input_weight)
    partial_lowrank_input = matrix_product_transposed(grad_preactivation, adapter_up_input)
    grad_second_normed, d_low_in = (
        lax.psum_scatter(part_norm2, "tensor", scatter_dimension=0, tiled=True),
        lax.psum_scatter(partial_lowrank_input, "tensor", scatter_dimension=0, tiled=True),
    )
    d_gates = gate_grad(take_home(grad_lowrank_output), low_out, experts, rank_size)
    d_gates = d_gates + gate_grad(d_low_in, take_home(lowrank_input), experts, rank_size)
    grad_gated_input = (d_low_in * rep_home).astype(BRAIN_FLOAT16)
    grad_second_normed = grad_second_normed + matrix_product_transposed(
        grad_gated_input, adapter_down_input[3]
    )
    grad_a_ffn = matmul_tn(second_normed2, grad_gated_input)
    grad_b_out = matmul_tn(gated_output, d_output)
    d_hidden1 = d_output.astype(SINGLE_FLOAT32) + rms_back(
        hidden_first1, second_norm2_gain, grad_second_normed
    )
    d_attn = d_hidden1.astype(BRAIN_FLOAT16)
    grad_first_rows = lax.all_gather(d_attn, "tensor", axis=0, tiled=True)
    grad_lowrank_attention = matrix_product_transposed(grad_first_rows, adapter_up_attention)
    d_gated_o = (grad_lowrank_attention * gate_repeated).astype(BRAIN_FLOAT16)
    d_context = (
        matrix_product_transposed(grad_first_rows, attention_output_weight)
        + matrix_product_transposed(d_gated_o, attn_down_rows)
    ).astype(BRAIN_FLOAT16)
    grad_a_o = widen(matmul_tn(context_rows, d_gated_o), inner_total, 0, inner_offset)
    grad_b_o = matmul_tn(gated_attention, d_attn)
    d_gates = d_gates + gate_grad(take_home(grad_lowrank_attention), low_o, experts, rank_size)
    d_query, d_key, d_value = lax.map(
        partial(attend_back, bias_all=bias_all),
        (
            split_qkv[0],
            split_qkv[1],
            split_qkv[2],
            valid_rows,
            log_total,
            d_context.reshape(seq_count, seq_length, inner_local),
        ),
    )
    grad_query_key_value = jnp.stack([d_query, d_key, d_value]).reshape(3, row_count, inner_local)
    grad_b_qkv = widen(
        jnp.einsum(
            "tpr,ptc->prc",
            gated_query_key_value,
            grad_query_key_value,
            preferred_element_type=SINGLE_FLOAT32,
        ),
        inner_total,
        2,
        inner_offset,
    )
    part_norm1 = jnp.einsum(
        "ptc,pdc->td",
        grad_query_key_value,
        query_key_value_weight,
        preferred_element_type=SINGLE_FLOAT32,
    )
    part_low_qkv = jnp.einsum(
        "liz,lsz->ils",
        grad_query_key_value,
        adapter_up_query_key_value,
        preferred_element_type=SINGLE_FLOAT32,
    ).reshape(row_count, 3 * adapter_columns)
    d_normed1, d_low_qkv = (
        lax.psum_scatter(
            part_norm1.astype(jnp.bfloat16), "tensor", scatter_dimension=0, tiled=True
        ).astype(jnp.float32),
        lax.psum_scatter(
            part_low_qkv.astype(jnp.bfloat16), "tensor", scatter_dimension=0, tiled=True
        ).astype(jnp.float32),
    )
    d_gates = d_gates + gate_grad(d_low_qkv, take_home(lowrank_qkv), experts, rank_size)
    d_gated_qkv = (d_low_qkv * jnp.tile(rep_home, (1, 3))).astype(BRAIN_FLOAT16)
    d_normed1 = d_normed1 + matrix_product_transposed(d_gated_qkv, down_query_key_value)
    grad_a_qkv = jnp.transpose(
        matmul_tn(first_normed1, d_gated_qkv).reshape(width_model, 3, adapter_columns), (1, 0, 2)
    )
    d_logits = (
        gates_home * (d_gates - jnp.sum(gates_home * d_gates, axis=-1, keepdims=True))
    ).astype(BRAIN_FLOAT16)
    grad_router = matmul_tn(first_normed1, d_logits)
    d_normed1 = d_normed1 + matrix_product_transposed(d_logits, router)
    grad_input = (d_hidden1 + rms_back(input_local, first_norm1_gain, d_normed1)).reshape(
        layer_inputs.shape
    )
    grad_a_in = jnp.concatenate([grad_a_qkv, grad_a_ffn[None]], axis=0)
    summed = lax.psum(
        (grad_router, grad_a_in, grad_a_o, grad_a_out, grad_b_qkv, grad_b_o, grad_b_in, grad_b_out),
        ("dp", "tensor"),
    )
    qkv_share = lax.dynamic_slice_in_dim(summed[4], member * local_inner, local_inner, 2)
    in_share = lax.dynamic_slice_in_dim(summed[6], member * local_ffn, local_ffn, 1)
    return (
        layer_output,
        grad_input,
        summed[0],
        summed[1],
        summed[2],
        summed[3],
        qkv_share,
        summed[5],
        in_share,
        summed[7],
    )


def solution(mesh):
    placed = (
        P(("dp", "tensor"), None, None),
        P(("dp", "tensor")),
        P(),
        P(),
        P(),
        P(None, None, "tensor"),
        P(None, "tensor"),
        P("tensor", None),
        P(None, "tensor"),
        P("tensor", None),
        P(),
        P(),
        P(),
        P(None, None, "tensor"),
        P(),
        P(None, "tensor"),
        P(),
        P(("dp", "tensor"), None, None),
    )
    return jax.shard_map(
        shards,
        mesh=mesh,
        in_specs=placed,
        out_specs=(
            P(("dp", "tensor"), None, None),
            P(("dp", "tensor"), None, None),
            P(),
            P(),
            P(),
            P(),
            P(None, None, "tensor"),
            P(),
            P(None, "tensor"),
            P(),
        ),
        check_vma=False,
    )
```

profile of v0, /device:TPU:0, one launch (start us, length us, event | category | flops | bytes accessed | tf_op | source)
XLA Modules:
  0.0 1955.8 jit_solution(15148665910465265821)
XLA Ops:
  9.8 3.0 fusion.36
  13.9 913.0 %gather_fusion = bf16[262144,3]{1,0:T(8,128)(2,1)} fusion(bf16[32,3]{1,0:T(8,128)(2,1)S(1)} %copy.66, s32[262144]{0:T(1024)S(1)} %broadcast_clamp_fusion), kind=kCustom, calls=%fused_computation | custom fusion | bytes 4194304 | tf_op jit(solution)/shard_map/jit(_take)/gather | solution.py:175
  927.0 59.5 %copy.67 = f32[512,512,3]{0,1,2:T(8,128)} copy(bf16[512,512,3]{2,1,0:T(8,128)(2,1)} %bitcast.50) | data formatting | bytes 4718592 | tf_op jit(solution)/shard_map/convert_element_type | solution.py:175
  986.6 6.3 all-gather
  992.9 4.5 fusion.69
  1001.6 6.3 fusion.70
  1008.0 3.4 fusion.42
  1020.2 49.1 %while.26 = (s32[]{:T(128)}, bf16[8,512,192]{1,2,0:T(8,128)(2,1)}, f32[8,3,512]{2,1,0:T(4,128)}, bf16[8,512,3,64]{1,3,2,0:T(8,128)(2,1)}, bf16[8,512]{1,0:T(8,12...) while((s32[]{:T(128)}, bf16[8,512,192]{1,2,0:T(8,128)(2,1)}, ...), condition=%wide.region_6.7_spmd, body=%wide.region_3.0_spmd.sunk | while | flops 207716352 | bytes 13818465 | solution.py:212
  1044.7 2.8 fusion.163
  1050.9 2.8 fusion.163
  1074.6 6.4 fusion.71
  1081.7 16.7 reduce-scatter.11.cloned.1.call-done
  1100.1 100.1 %reduce-scatter.9.cloned.1.call-done = f32[1024,768]{1,0:T(8,128)} async-done(((f32[4096,768]{1,0:T(8,128)}), f32[1024,768]{1,0:T(8,128)}) %reduce-scatter.9.cloned.1.call-update) | async-done | bytes 3145744 | tf_op jit(solution)/shard_map/reduce_scatter | solution.py:219
  1206.1 41.9 %all-gather.10.cloned.1.call-done = bf16[4096,768]{1,0:T(8,128)(2,1)} async-done(((bf16[1024,768]{1,0:T(8,128)(2,1)}), bf16[4096,768]{1,0:T(8,128)(2,1)}) %all-gather.10.cloned.1.call-update) | async-done | bytes 6291472 | tf_op jit(solution)/shard_map/all_gather | solution.py:251
  1248.0 10.6 fusion.73
  1258.6 37.8 %all-gather.8.cloned.1.call-done = bf16[4096,768]{1,0:T(8,128)(2,1)} async-done(((bf16[1024,768]{1,0:T(8,128)(2,1)}), bf16[4096,768]{1,0:T(8,128)(2,1)}) %all-gather.8.cloned.1.call-update) | async-done | bytes 6291472 | tf_op jit(solution)/shard_map/all_gather | solution.py:227
  1296.4 4.8 fusion.48
  1301.3 7.4 fusion.72
  1308.8 2.8 multiply_convert_fusion.5
  1311.6 8.3 multiply_convert_fusion.2
  1319.9 10.8 multiply_convert_fusion.1
  1333.3 2.8 fusion.75
  1336.4 10.6 fusion.74
  1347.1 11.7 reduce-scatter.19.cloned.1.call-done
  1360.4 100.1 %reduce-scatter.17.cloned.1.call-done = f32[1024,768]{1,0:T(8,128)} async-done(((f32[4096,768]{1,0:T(8,128)}), f32[1024,768]{1,0:T(8,128)}) %reduce-scatter.17.cloned.1.call-update) | async-done | bytes 3145744 | tf_op jit(solution)/shard_map/reduce_scatter | solution.py:268
  1460.5 3.7 multiply_reduce_fusion.1
  1464.7 2.9 fusion.66
  1467.7 5.5 convolution_convert_fusion.4
  1473.2 41.0 %all-gather.12.cloned.1.call-done = bf16[4096,768]{1,0:T(8,128)(2,1)} async-done(((bf16[1024,768]{1,0:T(8,128)(2,1)}), bf16[4096,768]{1,0:T(8,128)(2,1)}) %all-gather.12.cloned.1.call-update) | async-done | bytes 6291472 | tf_op jit(solution)/shard_map/all_gather | solution.py:283
  1514.2 5.7 multiply_convert_fusion.4
  1527.6 91.4 %while.27 = (s32[]{:T(128)}, bf16[8,512,192]{1,2,0:T(8,128)(2,1)S(1)}, bf16[8,512,192]{1,2,0:T(8,128)(2,1)}, bf16[8,512,192]{1,2,0:T(8,128)(2,1)}, bf16[8,512,3,...) while((s32[]{:T(128)}, ...), condition=%wide.region_17.18_spmd, body=%wide.region_15.17_spmd.sunk | while | flops 510689280 | bytes 42896544 | solution.py:293
  1620.9 3.9 stack.12
  1624.8 2.8 constant_dynamic-update-slice_fusion.6
  1629.6 4.0 stack.13
  1635.6 3.9 stack.14
  1642.7 4.3 convolution_convert_fusion.3
  1647.3 9.7 convolution_convert_fusion.2
  1660.1 3.9 convolution_dynamic-update-slice_fusion
  1665.0 4.6 convolution_dynamic-update-slice_fusion.1
  1677.5 4.8 fusion.80
  1688.8 8.9 bitcast_convert_fusion
  1706.5 26.1 %reduce-scatter.13.cloned.1.call-done = bf16[1024,768]{1,0:T(8,128)(2,1)} async-done(((bf16[4096,768]{1,0:T(8,128)(2,1)}), bf16[1024,768]{1,0:T(8,128)(2,1)}) %reduce-scatter.13.cloned.1.call-update) | async-done | bytes 1572880 | tf_op jit(solution)/shard_map/reduce_scatter | solution.py:237
  1732.6 4.2 add_convert_fusion.1
  1745.1 40.4 %psum.56 = f32[768,10]{0,1:T(8,128)} all-reduce(f32[768,10]{0,1:T(8,128)S(1)} %fusion.78), channel_id=1, replica_groups=mesh['dp'=8,'tensor'=4] {'dp','tensor'}, use_global_device_ids=true, to_apply=%region_26.27 | all-reduce | flops 7680 | bytes 61440 | tf_op jit(solution)/shard_map/psum | solution.py:351
  1785.4 3.3 fusion.77
  1788.8 91.0 %all-reduce.3.cloned.1.call-done = (f32[4,768,40]{1,2,0:T(8,128)}, f32[768,40]{0,1:T(8,128)}, f32[3072,40]{0,1:T(8,128)}, f32[3,40,768]{2,1,0:T(8,128)}, f32[40,...) async-done(((f32[4,768,40]{1,2,0:T(8,128)}, f32[768,40]{0,1:T(8,128)}, f32[3072,40]{0,1:T(8,128)}, f32[3,40,768]{2,1,0:T(8,128)}, f32[40,768]{1,0:T(8,128)}, ...) | async-done | bytes 2211856 | tf_op jit(solution)/shard_map/psum | solution.py:351
  1883.0 56.7 %reduce-scatter.21.cloned.1.call-done = bf16[1024,768]{1,0:T(8,128)(2,1)} async-done(((bf16[4096,768]{1,0:T(8,128)(2,1)}), bf16[1024,768]{1,0:T(8,128)(2,1)}) %reduce-scatter.21.cloned.1.call-update) | async-done | bytes 1572880 | tf_op jit(solution)/shard_map/reduce_scatter | solution.py:329
  1939.7 3.5 fusion.41
  (405 shorter events, 231.0 us)
Async XLA Ops:
  7.2 1294.1 %copy-start = (bf16[768,768]{1,0:T(8,128)(2,1)S(1)}, bf16[768,768]{1,0:T(8,128)(2,1)}, u32[]{:S(2)}) copy-start(bf16[768,768]{1,0:T(8,128)(2,1)} %param.31) | copy-start | bytes 3538948
  7.2 6.6 copy-start.35
  7.2 5.8 copy-start.45
  7.2 6.5 copy-start.66
  7.2 985.6 %all-gather.6.cloned.1.call-start = ((), (), s32[]{:S(2)}) async-start(), calls=%async_computation.8 | async-start | bytes 7864320 | tf_op jit(solution)/shard_map/all_gather | solution.py:181
  12.9 1085.6 %reduce-scatter.11.cloned.1.call-start = ((), (), s32[]{:S(2)}) async-start(), calls=%async_computation.10 | async-start | bytes 819200 | tf_op jit(solution)/shard_map/reduce_scatter | solution.py:220
  927.0 59.5 %copy-start.67 = (s32[2]{0:T(128)S(1)}, s32[2]{0:T(128)}, u32[]{:S(2)}) copy-start(s32[2]{0:T(128)} %param.24) | copy-start | bytes 28
  927.0 65.9 %copy-start.55 = (bf16[768,10]{0,1:T(8,128)(2,1)S(1)}, bf16[768,10]{0,1:T(8,128)(2,1)}, u32[]{:S(2)}) copy-start(bf16[768,10]{0,1:T(8,128)(2,1)} %param.27) | copy-start | bytes 46084
  999.3 8.7 slice-start
  1001.6 6.4 slice-start.1
  1001.6 6.4 copy-start.12
  1001.6 6.4 copy-start.26
  1069.3 11.8 copy-start.54
  1069.3 5.3 copy-start.33
  1072.0 9.0 copy-start.7
  1074.1 126.0 %reduce-scatter.9.cloned.1.call-start = ((), (), s32[]{:S(2)}) async-start(), calls=%async_computation.9 | async-start | bytes 15728640 | tf_op jit(solution)/shard_map/reduce_scatter | solution.py:219
  1081.1 17.4 copy-start.13
  1081.1 119.1 %copy-start.50 = (bf16[40,768]{1,0:T(8,128)(2,1)S(1)}, bf16[40,768]{1,0:T(8,128)(2,1)}, u32[]{:S(2)}) copy-start(bf16[40,768]{1,0:T(8,128)(2,1)} %param.37) | copy-start | bytes 184324
  1081.1 119.1 %copy-start.4 = (bf16[2,512,768]{2,1,0:T(8,128)(2,1)S(1)}, bf16[2,512,768]{2,1,0:T(8,128)(2,1)}, u32[]{:S(2)}) copy-start(bf16[2,512,768]{2,1,0:T(8,128)(2,1)} %param.23) | copy-start | bytes 4718596
  1081.1 166.9 %all-gather.10.cloned.1.call-start = ((), (), s32[]{:S(2)}) async-start(), calls=%async_computation.14 | async-start | bytes 7864320 | tf_op jit(solution)/shard_map/all_gather | solution.py:251
  1081.7 214.7 %all-gather.8.cloned.1.call-start = ((), (), s32[]{:S(2)}) async-start(), calls=%async_computation.11 | async-start | bytes 7864320 | tf_op jit(solution)/shard_map/all_gather | solution.py:227
  1100.1 102.8 %copy-start.37 = (bf16[1024,40]{0,1:T(8,128)(2,1)}, bf16[1024,40]{0,1:T(8,128)(2,1)S(1)}, u32[]{:S(2)}) copy-start(bf16[1024,40]{0,1:T(8,128)(2,1)S(1)} %get-tuple-element.223) | copy-start | bytes 245764
  1204.6 43.4 %copy-start.68 = (bf16[768,768]{1,0:T(8,128)(2,1)S(1)}, bf16[768,768]{1,0:T(8,128)(2,1)}, u32[]{:S(2)}) copy-start(bf16[768,768]{1,0:T(8,128)(2,1)} %param.32) | copy-start | bytes 3538948
  1206.1 152.7 %reduce-scatter.19.cloned.1.call-start = ((), (), s32[]{:S(2)}) async-start(), calls=%async_computation.16 | async-start | bytes 819200 | tf_op jit(solution)/shard_map/reduce_scatter | solution.py:269
  1206.1 90.3 %copy-start.46 = (bf16[4,768,40]{1,2,0:T(8,128)(2,1)S(1)}, bf16[4,768,40]{1,2,0:T(8,128)(2,1)}, u32[]{:S(2)}) copy-start(bf16[4,768,40]{1,2,0:T(8,128)(2,1)} %param.33) | copy-start | bytes 737284
  1296.4 12.3 slice-start.2
  1301.3 7.5 slice-start.3
  1301.3 7.5 copy-start.49
  1311.6 8.3 copy-start.30
  1311.6 8.3 copy-start.28
  1336.1 124.3 %reduce-scatter.17.cloned.1.call-start = ((), (), s32[]{:S(2)}) async-start(), calls=%async_computation.15 | async-start | bytes 15728640 | tf_op jit(solution)/shard_map/reduce_scatter | solution.py:268
  1347.0 11.8 copy-start.21
  1347.0 167.2 %all-gather.12.cloned.1.call-start = ((), (), s32[]{:S(2)}) async-start(), calls=%async_computation.17 | async-start | bytes 7864320 | tf_op jit(solution)/shard_map/all_gather | solution.py:283
  1467.6 201.9 %reduce-scatter.15.cloned.1.call-start = ((), (), s32[]{:S(2)}) async-start(), calls=%async_computation.13 | async-start | bytes 409600 | tf_op jit(solution)/shard_map/reduce_scatter | solution.py:240
  1473.2 46.8 %copy-start.34 = (bf16[192,768]{1,0:T(8,128)(2,1)S(1)}, bf16[192,768]{1,0:T(8,128)(2,1)}, u32[]{:S(2)}) copy-start(bf16[192,768]{1,0:T(8,128)(2,1)} %param.30) | copy-start | bytes 884740
  1473.2 209.8 %reduce-scatter.23.cloned.1.call-start = ((), (), s32[]{:S(2)}) async-start(), calls=%async_computation.19 | async-start | bytes 1228800 | tf_op jit(solution)/shard_map/reduce_scatter | solution.py:332
  1514.2 5.8 copy-start.6
  1620.9 6.7 copy-start.17
  1647.0 85.6 %reduce-scatter.13.cloned.1.call-start = ((), (), s32[]{:S(2)}) async-start(), calls=%async_computation.12 | async-start | bytes 7864320 | tf_op jit(solution)/shard_map/reduce_scatter | solution.py:237
  1657.1 222.6 %all-reduce.3.cloned.1.call-start = ((), (), s32[]{:S(2)}) async-start(), calls=%async_computation.20 | async-start | bytes 4423680 | tf_op jit(solution)/shard_map/psum | solution.py:351
  1669.6 6.1 copy-start.24
  1669.6 6.1 copy-start.8
  1682.4 5.3 copy-start.43
  1688.5 251.2 %reduce-scatter.21.cloned.1.call-start = ((), (), s32[]{:S(2)}) async-start(), calls=%async_computation.18 | async-start | bytes 7864320 | tf_op jit(solution)/shard_map/reduce_scatter | solution.py:329
  1741.6 198.1 %copy-start.56 = (bf16[768,10]{0,1:T(8,128)(2,1)S(1)}, bf16[768,10]{0,1:T(8,128)(2,1)}, u32[]{:S(2)}) copy-start(bf16[768,10]{0,1:T(8,128)(2,1)} %param.27) | copy-start | bytes 46084
  1741.6 198.1 %copy-start.62 = (f32[768]{0:T(1024)S(1)}, f32[768]{0:T(1024)}, u32[]{:S(2)}) copy-start(f32[768]{0:T(1024)} %param.25) | copy-start | bytes 9220
  1883.0 60.2 %copy-start.59 = (f32[1,4,2,128]{3,1,2,0:T(4,128)S(1)}, f32[1,4,2,128]{3,1,2,0:T(4,128)}, u32[]{:S(2)}) copy-start(f32[1,4,2,128]{3,1,2,0:T(4,128)} %copy-done.57) | copy-start | bytes 12292
  1883.0 60.2 %copy-start.65 = (f32[1024]{0:T(1024)S(1)}, f32[1024]{0:T(1024)}, u32[]{:S(2)}) copy-start(f32[1024]{0:T(1024)} %multiply_multiply_fusion) | copy-start | bytes 12292
  (46 other events, 140.7 us)
Sparse Core Ops, SparseCore 0:
  13.0 49.0 all-gather.5
  1074.3 24.1 reduce-scatter.10
  1101.1 99.0 reduce-scatter.8
  1201.6 46.3 all-gather.9
  1250.0 46.3 all-gather.7
  1336.3 22.4 reduce-scatter.18
  1361.4 99.0 reduce-scatter.16
  1467.7 46.3 all-gather.11
  1517.2 20.4 reduce-scatter.14
  1647.2 24.4 reduce-scatter.22
  1674.2 58.3 reduce-scatter.12
  1741.2 138.4 all-reduce.2
  1882.3 57.3 reduce-scatter.20
where the time goes:
time: 1960 us
  local copies, waits for them, and re-layouts  1060 us (54%)
  waiting for transfers between devices  524 us (27%)
  matrix products  254 us (13%)
  other arithmetic  50.3 us (3%)
  blocking collectives  46.7 us (2%)
    gather x1, local copies, waits for them, and re-layouts, shards(): jnp.take(relative_position_bias, bucket_ids, axis=0).astype(SINGLE_FLOAT32)  913 us
    reduce_scatter x1, waiting for transfers between devices, shards(): lax.psum_scatter(part_attn, 'tensor', scatter_dimension=0, tiled=True)  100 us
    reduce_scatter x1, waiting for transfers between devices, shards(): lax.psum_scatter(part_norm2, 'tensor', scatter_dimension=0, tiled=True)  100 us
    psum x1, waiting for transfers between devices, shards(): lax.psum((grad_router, grad_a_in, grad_a_o, grad_a_out, grad_b_qkv, grad_...  91 us
    convert_element_type x1, local copies, waits for them, and re-layouts, shards(): jnp.take(relative_position_bias, bucket_ids, axis=0).astype(SINGLE_FLOAT32)  59.5 us
    dot_general x11, matrix products, matrix_product(): return jnp.dot(a, b, preferred_element_type=SINGLE_FLOAT32)  59.1 us
    dot_general x11, matrix products, matrix_product_transposed(): lax.dot_general(a, b, (((a.ndim - 1,), (b.ndim - 1,)), ((), ())), preferr...  57.5 us
    reduce_scatter x1, waiting for transfers between devices, shards(): lax.psum_scatter(part_norm1.astype(jnp.bfloat16), 'tensor', scatter_dimen...  56.7 us
  transfers between devices with their start and end apart: 13, of which 10 were waited for; matrix products, arithmetic and copies ran while one was open for 62% of the time, Pallas kernels for 0%

commit v1 on v0

v1 whole, which is shorter than its diff:
```python
import jax
import jax.numpy as jnp
import numpy as np
from jax import lax
from jax.experimental import pallas as pl
from jax.experimental.pallas import tpu as pltpu
from jax.sharding import PartitionSpec as P

NB = 32
MAX_DIST = 128
EPS = 1e-06
NEG = -1000000000.0
F32 = jnp.float32
BF16 = jnp.bfloat16
PAD = 64
VMEM_LIMIT = 60 * 1024 * 1024


def nn(a, b):
    return lax.dot_general(a, b, (((1,), (0,)), ((), ())), preferred_element_type=F32)


def nt(a, b):
    return lax.dot_general(a, b, (((1,), (1,)), ((), ())), preferred_element_type=F32)


def tn(a, b):
    return lax.dot_general(a, b, (((0,), (0,)), ((), ())), preferred_element_type=F32)


def bucket_of(relative):
    half = NB // 2
    exact = half // 2
    distance = np.abs(relative)
    scaled = np.log(np.maximum(distance, 1) / exact) / np.log(MAX_DIST / exact) * (half - exact)
    far = np.minimum(exact + scaled.astype(np.int32), half - 1)
    return ((relative > 0) * half + np.where(distance < exact, distance, far)).astype(np.int32)


def bucket_lines(seq):
    m = np.arange(2 * seq)
    rel = seq - 128 - m
    rel = np.where(rel < -seq, rel + 2 * seq, rel)
    rel = np.clip(rel, -(seq - 1), seq - 1)
    ids = bucket_of(rel)
    return (ids[None, :] == np.arange(NB)[:, None]).astype(np.float32)


def attention_forward(
    lens, x_ref, g1_ref, wsm_ref, wqkv_ref, bqkv_ref, rb_ref, oh_ref,
    n1_ref, low_ref, gate_ref, gate_t_ref, gated_ref, qkv_ref, e_ref, r_ref, ctx_ref,
    small, urow, brow,
):
    tokens = x_ref.shape[0]
    groups = wqkv_ref.shape[0]
    inner = wqkv_ref.shape[1] // 3
    seq = e_ref.shape[1]
    seqs = tokens // seq
    heads_here = e_ref.shape[0] // (groups * seqs)
    hd = inner // heads_here
    tb = 256
    experts_rep = 40

    def norm(i, c):
        rows = pl.ds(pl.multiple_of(i * tb, tb), tb)
        x = x_ref[rows, :].astype(F32)
        n1 = (x * lax.rsqrt(jnp.mean(x * x, axis=1, keepdims=True) + EPS) * g1_ref[...]).astype(BF16)
        n1_ref[rows, :] = n1
        small = nt(wsm_ref[...], n1)
        low = small[: 3 * PAD]
        logits = small[3 * PAD :]
        valid = lax.broadcasted_iota(jnp.int32, logits.shape, 0) < experts_rep
        logits = jnp.where(valid, logits, -jnp.inf)
        ex = jnp.exp(logits - jnp.max(logits, axis=0, keepdims=True))
        gate = ex / (jnp.sum(ex, axis=0, keepdims=True) * 0.25)
        low_ref[:, rows] = low
        gate_ref[:, rows] = gate
        gate_t_ref[rows, :] = jnp.concatenate([gate, gate], axis=0).T
        for p in range(3):
            gated_ref[p * PAD : (p + 1) * PAD, rows] = (low[p * PAD : (p + 1) * PAD] * gate).astype(BF16)
        return c

    lax.fori_loop(0, tokens // tb, norm, 0)
    u = nn(rb_ref[...], oh_ref[...])
    for h in range(groups * heads_here):
        urow[h] = u[h : h + 1]

    maskrow = jnp.where(
        lax.broadcasted_iota(jnp.int32, (16, seq), 1) < lens[seqs - 1], 0.0, NEG
    )
    maskrow = jnp.where(lax.broadcasted_iota(jnp.int32, (16, seq), 0) == 0, maskrow, 0.0).astype(BF16)
    onerow = (lax.broadcasted_iota(jnp.int32, (16, seq), 0) == 0).astype(F32).astype(BF16)

    def group(g, c):
        proj = nt(wqkv_ref[g], n1_ref[...])
        for p in range(3):
            up = tn(bqkv_ref[g, p], gated_ref[p * PAD : (p + 1) * PAD, :])
            qkv_ref[g, p] = (proj[p * inner : (p + 1) * inner] + up).astype(BF16)

        def head(h, c):
            gh = g * heads_here + h
            line = jnp.broadcast_to(urow[gh], (128, 2 * seq))
            brow[...] = pltpu.roll(line, 0, 1, stride=1, stride_axis=0)[:, : 2 * seq - 128]
            feats = pl.ds(pl.multiple_of(h * hd, hd), hd)
            for s in range(seqs):
                q = qkv_ref[g, 0, feats, s * seq : (s + 1) * seq]
                k = qkv_ref[g, 1, feats, s * seq : (s + 1) * seq]
                v = qkv_ref[g, 2, feats, s * seq : (s + 1) * seq]
                if s > 0:
                    q = jnp.concatenate([q, onerow], axis=0)
                    k = jnp.concatenate([k, maskrow], axis=0)
                qb = 256
                for b in range(seq // qb):
                    st = tn(k, q[:, b * qb : (b + 1) * qb])
                    bias = jnp.concatenate(
                        [
                            brow[:, seq - 128 - 128 * kb + b * qb : seq - 128 - 128 * kb + (b + 1) * qb]
                            for kb in range(seq // 128)
                        ],
                        axis=0,
                    )
                    st = st + bias
                    ex = jnp.exp(st - jnp.max(st, axis=0, keepdims=True))
                    recip = 1.0 / jnp.sum(ex, axis=0, keepdims=True)
                    eb = ex.astype(BF16)
                    e_ref[gh * seqs + s, :, b * qb : (b + 1) * qb] = eb
                    r_ref[gh, :, s * seq + b * qb : s * seq + (b + 1) * qb] = recip
                    ot = nn(v, eb) * recip
                    ctx_ref[
                        pl.ds(pl.multiple_of(gh * hd, hd), hd), s * seq + b * qb : s * seq + (b + 1) * qb
                    ] = ot.astype(BF16)
            return c

        lax.fori_loop(0, heads_here, head, 0)
        return c

    lax.fori_loop(0, groups, group, 0)


def feed_forward(
    x_ref, c_ref, g2_ref, ctx_ref, gate_ref, wo_ref, ao_ref, bo_ref, ain_ref, bin_ref, aout_ref, bout_ref,
    win_ref, wout_ref,
    y_ref, dh_ref, dctx_ref, z_ref, gao_ref, gaout_ref, gbo_ref, gbin_ref, gbout_ref, gain_ref,
    h1, n2, acc, dn2, low_o, low_in, low_out, d_low_in, gated_in, gated_in_t, dgo, dgo_t, d_low_out,
):
    tokens = x_ref.shape[0]
    groups = win_ref.shape[0]
    tb = 256
    blocks = tokens // tb

    def rows_of(i):
        return pl.ds(pl.multiple_of(i * tb, tb), tb)

    def first(i, c):
        rows = rows_of(i)
        gate = gate_ref[rows, :PAD]
        ctx = ctx_ref[:, rows].T
        lo = nt(ctx, ao_ref[...])
        low_o[rows, :] = lo
        gated_o = (lo * gate).astype(BF16)
        hidden = x_ref[rows, :].astype(F32) + nn(ctx, wo_ref[...]) + nn(gated_o, bo_ref[...])
        h1[rows, :] = hidden
        norm = (
            hidden * lax.rsqrt(jnp.mean(hidden * hidden, axis=1, keepdims=True) + EPS) * g2_ref[...]
        ).astype(BF16)
        n2[rows, :] = norm
        li = nt(norm, ain_ref[...])
        low_in[rows, :] = li
        gi = li * gate
        gated_in[rows, :] = gi.astype(BF16)
        dlo = nt(c_ref[rows, :], bout_ref[...])
        d_low_out[rows, :] = dlo
        dg = dlo * gate
        dgo[rows, :] = dg.astype(BF16)
        both = jnp.concatenate([gi, dg], axis=1).T.astype(BF16)
        gated_in_t[:, rows] = both[:PAD]
        dgo_t[:, rows] = both[PAD:]
        return c

    lax.fori_loop(0, blocks, first, 0)

    def chunk(step, c):
        k = step // blocks
        i = step % blocks
        rows = rows_of(i)
        pre = nn(n2[rows, :], win_ref[k]) + nn(gated_in[rows, :], bin_ref[k])
        da = nt(c_ref[rows, :], wout_ref[k]) + nn(dgo[rows, :], aout_ref[k])
        sig = 1.0 / (1.0 + jnp.exp(-pre))
        active = (pre * sig).astype(BF16)
        dpre = (da * sig * (1.0 + pre * (1.0 - sig))).astype(BF16)
        part = nn(active, wout_ref[k])
        lo = nt(active, aout_ref[k])
        dn = nt(dpre, win_ref[k])
        dl = nt(dpre, bin_ref[k])
        ga = nn(dgo_t[:, rows], active)
        gb = nn(gated_in_t[:, rows], dpre)

        @pl.when(k == 0)
        def _():
            acc[rows, :] = part
            low_out[rows, :] = lo
            dn2[rows, :] = dn
            d_low_in[rows, :] = dl

        @pl.when(k > 0)
        def _():
            acc[rows, :] += part
            low_out[rows, :] += lo
            dn2[rows, :] += dn
            d_low_in[rows, :] += dl

        @pl.when(i == 0)
        def _():
            gaout_ref[k] = ga
            gbin_ref[k] = gb

        @pl.when(i > 0)
        def _():
            gaout_ref[k] += ga
            gbin_ref[k] += gb

        return c

    lax.fori_loop(0, groups * blocks, chunk, 0)

    gbout_ref[...] = jnp.zeros_like(gbout_ref)
    gbo_ref[...] = jnp.zeros_like(gbo_ref)
    gao_ref[...] = jnp.zeros_like(gao_ref)
    gain_ref[...] = jnp.zeros_like(gain_ref)

    def last(i, c):
        rows = rows_of(i)
        gate = gate_ref[rows, :PAD]
        cot = c_ref[rows, :]
        hidden = h1[rows, :]
        go = low_out[rows, :] * gate
        y_ref[rows, :] = (hidden + acc[rows, :] + nn(go.astype(BF16), bout_ref[...])).astype(BF16)
        dli = d_low_in[rows, :]
        dgi = dli * gate
        dn = dn2[rows, :] + nn(dgi.astype(BF16), ain_ref[...])
        both = jnp.concatenate([go, dgi], axis=1).T.astype(BF16)
        gbout_ref[...] += nn(both[:PAD], cot)
        gain_ref[...] += nn(both[PAD:], n2[rows, :])
        inv = lax.rsqrt(jnp.mean(hidden * hidden, axis=1, keepdims=True) + EPS)
        up = dn * g2_ref[...]
        dh = (
            cot.astype(F32)
            + inv * up
            - hidden * (inv * inv * inv) * jnp.mean(hidden * up, axis=1, keepdims=True)
        )
        dh_ref[rows, :] = dh
        da = dh.astype(BF16)
        dlo = nt(da, bo_ref[...])
        lo = low_o[rows, :]
        dg = dlo * gate
        dgb = dg.astype(BF16)
        both = jnp.concatenate([lo * gate, dg], axis=1).T.astype(BF16)
        gbo_ref[...] += nn(both[:PAD], da)
        gao_ref[...] += nt(both[PAD:], ctx_ref[:, rows])
        dctx_ref[:, rows] = (nt(wo_ref[...], da) + tn(ao_ref[...], both[PAD:])).astype(BF16)
        z = dlo * lo + dli * low_in[rows, :] + d_low_out[rows, :] * low_out[rows, :]
        z_ref[:, rows] = jnp.concatenate([z, z], axis=1).T[:PAD]
        return c

    lax.fori_loop(0, blocks, last, 0)


def attention_backward(
    x_ref, g1_ref, wsm_ref, wqkv_ref, bqkv_ref, n1_ref, low_ref, gate_ref, gated_ref, qkv_ref, e_ref, r_ref,
    ctx_ref, dctx_ref, z_ref, dh_ref, sum_ref,
    gx_ref, gsm_ref, gbqkv_ref,
    dqkv, dlow, dn1, dsmall,
):
    tokens = x_ref.shape[0]
    groups = wqkv_ref.shape[0]
    inner = wqkv_ref.shape[1] // 3
    seq = e_ref.shape[1]
    seqs = tokens // seq
    heads_here = e_ref.shape[0] // (groups * seqs)
    hd = inner // heads_here
    qb = 256

    def group(g, c):
        def head(h, c):
            gh = g * heads_here + h
            feats = pl.ds(pl.multiple_of(h * hd, hd), hd)
            full = pl.ds(pl.multiple_of(gh * hd, hd), hd)
            for s in range(seqs):
                cols = slice(s * seq, (s + 1) * seq)
                q = qkv_ref[g, 0, feats, cols]
                k = qkv_ref[g, 1, feats, cols]
                v = qkv_ref[g, 2, feats, cols]
                dk = jnp.zeros((hd, seq), F32)
                dv = jnp.zeros((hd, seq), F32)
                for b in range(seq // qb):
                    part = slice(s * seq + b * qb, s * seq + (b + 1) * qb)
                    do = (dctx_ref[full, part].astype(F32) * r_ref[gh, :, part]).astype(BF16)
                    delta = jnp.sum(do.astype(F32) * ctx_ref[full, part].astype(F32), axis=0, keepdims=True)
                    eb = e_ref[gh * seqs + s, :, b * qb : (b + 1) * qb]
                    dp = tn(v, do)
                    ds = (eb.astype(F32) * (dp - delta)).astype(BF16)
                    dqkv[feats, part] = nn(k, ds).astype(BF16)
                    dk = dk + nt(q[:, b * qb : (b + 1) * qb], ds)
                    dv = dv + nt(do, eb)
                dqkv[pl.ds(pl.multiple_of(inner + h * hd, hd), hd), cols] = dk.astype(BF16)
                dqkv[pl.ds(pl.multiple_of(2 * inner + h * hd, hd), hd), cols] = dv.astype(BF16)
            return c

        lax.fori_loop(0, heads_here, head, 0)
        dn = tn(wqkv_ref[g], dqkv[...])

        @pl.when(g == 0)
        def _():
            dn1[...] = dn

        @pl.when(g > 0)
        def _():
            dn1[...] += dn

        for p in range(3):
            d = dqkv[p * inner : (p + 1) * inner, :]
            dl = nn(bqkv_ref[g, p], d)

            @pl.when(g == 0)
            def _():
                dlow[p * PAD : (p + 1) * PAD, :] = dl

            @pl.when(g > 0)
            def _():
                dlow[p * PAD : (p + 1) * PAD, :] += dl

            gbqkv_ref[g, p] = nt(gated_ref[p * PAD : (p + 1) * PAD, :], d)
        return c

    lax.fori_loop(0, groups, group, 0)
    gate = gate_ref[...]
    z = z_ref[...]
    for p in range(3):
        part = slice(p * PAD, (p + 1) * PAD)
        z = z + dlow[part, :] * low_ref[part, :]
        dsmall[part, :] = (dlow[part, :] * gate).astype(BF16)
    zh = z.astype(BF16)
    zl = (z - zh.astype(F32)).astype(BF16)
    dgate = nn(sum_ref[...], zh) + nn(sum_ref[...], zl)
    total = jnp.sum(gate * z, axis=0, keepdims=True)
    dlogit = gate * (dgate - total)
    row = lax.broadcasted_iota(jnp.int32, dlogit.shape, 0)
    keep = jnp.logical_and(row % 4 == 0, row < 40)
    dsmall[3 * PAD :, :] = jnp.where(keep, dlogit, 0.0).astype(BF16)
    gsm_ref[...] = nn(dsmall[...], n1_ref[...])

    tb = 256

    def finish(i, c):
        rows = pl.ds(pl.multiple_of(i * tb, tb), tb)
        dn = (dn1[:, rows] + tn(wsm_ref[...], dsmall[:, rows])).T
        x = x_ref[rows, :].astype(F32)
        inv = lax.rsqrt(jnp.mean(x * x, axis=1, keepdims=True) + EPS)
        up = dn * g1_ref[...]
        gx_ref[rows, :] = (
            dh_ref[rows, :] + inv * up - x * (inv * inv * inv) * jnp.mean(x * up, axis=1, keepdims=True)
        )
        return c

    lax.fori_loop(0, tokens // tb, finish, 0)


def call(body, name, outs, scratch, args, smem=0):
    specs = [pl.BlockSpec(memory_space=pltpu.SMEM)] * smem
    specs += [pl.BlockSpec(memory_space=pltpu.VMEM)] * (len(args) - smem)
    return pl.pallas_call(
        body,
        name=name,
        out_shape=[jax.ShapeDtypeStruct(s, d) for s, d in outs],
        in_specs=specs,
        out_specs=[pl.BlockSpec(memory_space=pltpu.VMEM)] * len(outs),
        scratch_shapes=[pltpu.VMEM(s, d) for s, d in scratch],
        compiler_params=pltpu.CompilerParams(vmem_limit_bytes=VMEM_LIMIT),
    )(*args)


def pad_rows(a):
    width = [(0, 0)] * (a.ndim - 2) + [(0, PAD - a.shape[-2]), (0, 0)]
    return jnp.pad(a, width)


def shards(
    layer_inputs, lengths, first_gain, second_gain, router, wqkv, bias_table, wo, win, wout,
    a_in, a_o, a_out, b_qkv, b_o, b_in, b_out, cotangent,
):
    groups = lax.axis_size("tensor")
    member = lax.axis_index("tensor")
    seqs, seq, width = layer_inputs.shape
    tokens = seqs * seq
    inner = wo.shape[0]
    heads_here = bias_table.shape[1]
    heads = heads_here * groups
    hd = inner // heads_here
    hidden = win.shape[1]
    experts = router.shape[1]
    cols = a_in.shape[2]
    rank = cols // experts

    def gather(v):
        return lax.all_gather(v, "tensor", axis=0)

    x = layer_inputs.reshape(tokens, width)
    cot = cotangent.reshape(tokens, width)
    g1 = first_gain.reshape(1, width)
    g2 = second_gain.reshape(1, width)
    at = jnp.swapaxes(a_in, 1, 2)
    rrep = jnp.repeat(router.T, rank, axis=0)
    wsm = pad_rows(jnp.concatenate([at[:3], rrep[None]], axis=0)).reshape(4 * PAD, width)
    wqkv_all = gather(jnp.swapaxes(wqkv, 1, 2).reshape(3 * inner, width))
    bqkv_all = pad_rows(gather(b_qkv))
    rb = gather(bias_table.T).reshape(heads, NB)
    rb = jnp.pad(rb, ((0, 16 - heads % 16), (0, 0)))
    wo_all = gather(wo).reshape(groups * inner, width)
    win_all = gather(win)
    wout_all = gather(wout)
    bin_all = pad_rows(gather(b_in))
    ao = pad_rows(a_o.T)
    ain = pad_rows(at[3])
    aout = pad_rows(jnp.swapaxes(a_out.T.reshape(cols, groups, hidden), 0, 1))
    bo = pad_rows(b_o)
    bout = pad_rows(b_out)
    onehot = jnp.asarray(bucket_lines(seq), BF16)

    n1, low, gate, gate_t, gated, qkv, e, r, ctx = call(
        attention_forward,
        "attention_forward",
        [
            ((tokens, width), BF16),
            ((3 * PAD, tokens), F32),
            ((PAD, tokens), F32),
            ((tokens, 2 * PAD), F32),
            ((3 * PAD, tokens), BF16),
            ((groups, 3, inner, tokens), BF16),
            ((heads * seqs, seq, seq), BF16),
            ((heads, 1, tokens), F32),
            ((groups * inner, tokens), BF16),
        ],
        [
            ((8, 128), F32),
            ((heads, 1, 2 * seq), F32),
            ((128, 2 * seq - 128), F32),
        ],
        (lengths, x, g1, wsm, wqkv_all, bqkv_all, rb, onehot),
        smem=1,
    )
    y, dh, dctx, z, gao, gaout, gbo, gbin, gbout, gain = call(
        feed_forward,
        "feed_forward",
        [
            ((tokens, width), BF16),
            ((tokens, width), F32),
            ((groups * inner, tokens), BF16),
            ((PAD, tokens), F32),
            ((PAD, groups * inner), F32),
            ((groups, PAD, hidden), F32),
            ((PAD, width), F32),
            ((groups, PAD, hidden), F32),
            ((PAD, width), F32),
            ((PAD, width), F32),
        ],
        [
            ((tokens, width), F32),
            ((tokens, width), BF16),
            ((tokens, width), F32),
            ((tokens, width), F32),
            ((tokens, PAD), F32),
            ((tokens, PAD), F32),
            ((tokens, PAD), F32),
            ((tokens, PAD), F32),
            ((tokens, PAD), BF16),
            ((PAD, tokens), BF16),
            ((tokens, PAD), BF16),
            ((PAD, tokens), BF16),
            ((tokens, PAD), F32),
        ],
        (x, cot, g2, ctx, gate_t, wo_all, ao, bo, ain, bin_all, aout, bout, win_all, wout_all),
    )
    c = np.arange(PAD)
    same = (c[:, None] // rank == c[None, :] // rank) & (c[None, :] < cols)
    gx, gsm, gbqkv = call(
        attention_backward,
        "attention_backward",
        [
            ((tokens, width), F32),
            ((4 * PAD, width), F32),
            ((groups, 3, PAD, inner), F32),
        ],
        [
            ((3 * inner, tokens), BF16),
            ((3 * PAD, tokens), F32),
            ((width, tokens), F32),
            ((4 * PAD, tokens), BF16),
        ],
        (x, g1, wsm, wqkv_all, bqkv_all, n1, low, gate, gated, qkv, e, r, ctx, dctx, z, dh, jnp.asarray(same, BF16)),
    )
    g_in = jnp.concatenate([gsm.reshape(4, PAD, width)[:3, :cols], gain[None, :cols]], axis=0)
    g_router = gsm.reshape(4, PAD, width)[3, :cols:rank]
    summed = lax.psum(
        (g_router, g_in, gao[:cols], gaout[:, :cols], gbqkv[:, :, :cols], gbo[:cols], gbin[:, :cols], gbout[:cols]),
        ("dp", "tensor"),
    )
    return (
        y.reshape(layer_inputs.shape),
        gx.reshape(layer_inputs.shape),
        summed[0].T,
        jnp.swapaxes(summed[1], 1, 2),
        summed[2].T,
        jnp.swapaxes(summed[3], 0, 1).reshape(cols, groups * hidden).T,
        lax.dynamic_index_in_dim(summed[4], member, 0, keepdims=False),
        summed[5],
        lax.dynamic_index_in_dim(summed[6], member, 0, keepdims=False),
        summed[7],
    )


def solution(mesh):
    rows = P(("dp", "tensor"), None, None)
    placed = (
        rows, P(("dp", "tensor")), P(), P(), P(), P(None, None, "tensor"), P(None, "tensor"), P("tensor", None),
        P(None, "tensor"), P("tensor", None), P(), P(), P(), P(None, None, "tensor"), P(), P(None, "tensor"), P(), rows,
    )
    return jax.shard_map(
        shards,
        mesh=mesh,
        in_specs=placed,
        out_specs=(rows, rows, P(), P(), P(), P(), P(None, None, "tensor"), P(), P(None, "tensor"), P()),
        check_vma=False,
    )
```

time: 1960 us -> 407 us (0.21)
  local copies, waits for them, and re-layouts: 1060 us -> 22.3 us
  waiting for transfers between devices: 524 us -> 163 us
  matrix products: 254 us -> 0 us
  Pallas kernels: 0 us -> 144 us
  other arithmetic: 50.3 us -> 1.6 us
    gather x1 -> x0, local copies, waits for them, and re-layouts: 913 us -> none  [shards(): jnp.take(relative_position_bias, bucket_ids, axis=0).astype(SINGLE_FLOAT32)]
    reduce_scatter x8 -> x0, waiting for transfers between devices: 312 us -> none  [the longest x1 100 us: shards(): lax.psum_scatter(part_attn, 'tensor', scatter_dimension=0, tiled=True)]
    dot_general x90 -> x0, matrix products: 247 us -> none  [the longest x11 59.1 us: matrix_product(): return jnp.dot(a, b, preferred_element_type=SINGLE_FLOAT32)]
    pallas_call x0 -> x3, Pallas kernels: none -> 144 us  [call(): pl.pallas_call(body, name=name, out_shape=[jax.ShapeDtypeStruct(s, d) for...]
    convert_element_type x1 -> x0, local copies, waits for them, and re-layouts: 59.5 us -> none  [shards(): jnp.take(relative_position_bias, bucket_ids, axis=0).astype(SINGLE_FLOAT32)]
    all_gather x4, waiting for transfers between devices: 121 us -> 63.9 us  [gather(): return lax.all_gather(v, 'tensor', axis=0)]
  transfers between devices with their start and end apart: 13 -> 5, of which waited for: 10 -> 4; matrix products, arithmetic and copies ran while one was open for 62% -> 2% of each run, Pallas kernels for 0% -> 10%
where the time goes in v1:
time: 407 us
  waiting for transfers between devices  163 us (40%)
  Pallas kernels  144 us (35%)
  blocking collectives  61.4 us (15%)
  local copies, waits for them, and re-layouts  22.3 us (5%)
  between operations  14 us (3%)
    pallas_call x3, Pallas kernels, call(): pl.pallas_call(body, name=name, out_shape=[jax.ShapeDtypeStruct(s, d) for...  144 us
    psum x1, waiting for transfers between devices, shards(): lax.psum((g_router, g_in, gao[:cols], gaout[:, :cols], gbqkv[:, :, :cols]...  97 us
    all_gather x4, waiting for transfers between devices, gather(): return lax.all_gather(v, 'tensor', axis=0)  63.9 us
    psum x1, blocking collectives, shards(): lax.psum((g_router, g_in, gao[:cols], gaout[:, :cols], gbqkv[:, :, :cols]...  40.6 us
    all_gather x3, blocking collectives, gather(): return lax.all_gather(v, 'tensor', axis=0)  20.9 us
  transfers between devices with their start and end apart: 5, of which 4 were waited for; matrix products, arithmetic and copies ran while one was open for 2% of the time, Pallas kernels for 10%

profile of v1, /device:TPU:0, one launch (start us, length us, event | category | flops | bytes accessed | tf_op | source)
XLA Modules:
  0.0 406.5 jit_solution(9106719614990282186)
XLA Ops:
  7.2 0.0 all-gather.12.cloned.1.call-start
  7.2 0.7 all-gather.12.cloned.1.call-update
  8.0 0.0 all-gather.14.cloned.1.call-start
  8.0 0.7 all-gather.14.cloned.1.call-update
  8.7 0.0 all-gather.16.cloned.1.call-start
  8.7 0.7 all-gather.16.cloned.1.call-update
  9.4 0.0 all-gather.18.cloned.1.call-start
  9.5 0.5 all-gather.18.cloned.1.call-update
  10.0 0.0 all-reduce.12.cloned.1.call-start
  10.2 0.6 reshape.60.g1_ref
  10.8 6.0 %all-gather.6 = bf16[4,3,32]{2,1,0:T(4,128)(2,1)S(1)} all-gather(bf16[1,3,32]{2,1,0:T(4,128)(2,1)S(1)} %bitcast.69), channel_id=3, replica_groups=mesh['dp'=8,'tensor'=4] {'tensor'}, dimensions={0}, use_global_device_ids=true | all-gather | bytes 960 | tf_op jit(solution)/shard_map/all_gather | solution.py:405
  16.8 6.2 %all-gather = bf16[12,40,192]{2,1,0:T(8,128)(2,1)S(1)} all-gather(bf16[3,40,192]{2,1,0:T(8,128)(2,1)S(1)} %copy-done.12), channel_id=2, replica_groups=mesh['dp'=8,'tensor'=4] {'tensor'}, dimensions={0}, use_global_device_ids=true | all-gather | bytes 230400 | tf_op jit(solution)/shard_map/all_gather | solution.py:405
  23.0 0.8 pad.32.bqkv_ref
  23.8 0.6 pad.33.rb_ref
  24.4 0.6 pad.36.ain_ref
  25.0 8.7 %all-gather.3 = bf16[160,768]{1,0:T(8,128)(2,1)S(1)} all-gather(bf16[40,768]{1,0:T(8,128)(2,1)S(1)} %copy-done.13), channel_id=5, replica_groups=mesh['dp'=8,'tensor'=4] {'tensor'}, dimensions={0}, use_global_device_ids=true | all-gather | bytes 307200 | tf_op jit(solution)/shard_map/all_gather | solution.py:405
  33.7 0.8 pad.37.bin_ref
  34.5 0.8 pad.38.aout_ref
  35.3 0.6 pad.34.ao_ref
  36.0 0.6 pad.35.bo_ref
  36.6 0.6 pad.39.bout_ref
  37.3 0.6 reshape.59.g2_ref
  37.8 0.8 fusion.2
  38.6 5.8 %all-gather.12.cloned.1.call-done.wqkv_ref = bf16[4,576,768]{2,1,0:T(8,128)(2,1)} async-done(((bf16[1,576,768]{2,1,0:T(8,128)(2,1)}), bf16[4,576,768]{2,1,0:T(8,128)(2,1)}) %all-gather.12.cloned.1.call-update) | async-done | bytes 3538960 | tf_op jit(solution)/shard_map/all_gather | solution.py:405
  44.4 39.8 %attention_forward.1 = (bf16[1024,768]{1,0:T(8,128)(2,1)}, f32[192,1024]{1,0:T(8,128)}, f32[64,1024]{1,0:T(8,128)}, f32[1024,128]{1,0:T(8,128)}, bf16[192,1024]{...) custom-call(s32[2]{0:T(128)} %lens.1, ...), custom_call_target="tpu_custom_call" | custom-call | tf_op jit(solution)/shard_map/attention_forward/pallas_call | solution.py:371
  84.2 19.2 %all-gather.16.cloned.1.call-done = bf16[3072,768]{1,0:T(8,128)(2,1)} async-done(((bf16[768,768]{1,0:T(8,128)(2,1)}), bf16[3072,768]{1,0:T(8,128)(2,1)}) %all-gather.16.cloned.1.call-update) | async-done | bytes 4718608 | tf_op jit(solution)/shard_map/all_gather | solution.py:405
  103.5 38.9 %all-gather.18.cloned.1.call-done = bf16[3072,768]{1,0:T(8,128)(2,1)} async-done(((bf16[768,768]{1,0:T(8,128)(2,1)}), bf16[3072,768]{1,0:T(8,128)(2,1)}) %all-gather.18.cloned.1.call-update) | async-done | bytes 4718608 | tf_op jit(solution)/shard_map/all_gather | solution.py:405
  142.4 54.7 %feed_forward.1 = (bf16[1024,768]{1,0:T(8,128)(2,1)}, f32[1024,768]{1,0:T(8,128)}, bf16[768,1024]{1,0:T(8,128)(2,1)}, f32[64,1024]{1,0:T(8,128)}, f32[64,768]{1,...) custom-call(bf16[1024,768]{1,0:T(8,128)(2,1)} %bitcast.49, ...), custom_call_target="tpu_custom_call" | custom-call | tf_op jit(solution)/shard_map/feed_forward/pallas_call | solution.py:371
  197.1 49.0 %attention_backward.1 = (f32[1024,768]{1,0:T(8,128)}, f32[256,768]{1,0:T(8,128)}, f32[4,3,64,192]{3,2,1,0:T(8,128)}) custom-call(bf16[1024,768]{1,0:T(8,128)(2,1)} %bitcast.50, f32[1,768]{1,0:T(1,128)} %reshape.60.g1_ref, bf16[256,768]{1,0:T(8,128)(2,1)} %bitcast.54, bf16[4,576,768]{2,1,0:T(8,128)(2,1)} %all-gather.12.cloned.1.call-done.wqkv_ref, ...), custom_call_target="tpu_custom_call" | custom-call | tf_op jit(solution)/shard_map/attention_backward/pallas_call | solution.py:371
  246.2 1.1 slice.46
  247.3 1.9 slice.40
  249.2 0.8 copy.35
  250.1 0.8 slice.42
  250.9 0.7 slice.41
  251.6 0.7 slice.43
  252.2 0.7 slice_bitcast_fusion.1
  252.9 0.8 maximum_bitcast_fusion
  253.7 0.0 all-reduce.12.cloned.1.call-update
  253.7 0.9 slice.35
  254.7 40.6 %psum.56 = f32[768,10]{0,1:T(8,128)} all-reduce(f32[768,10]{0,1:T(8,128)S(1)} %bitcast.66), channel_id=1, replica_groups=mesh['dp'=8,'tensor'=4] {'dp','tensor'}, use_global_device_ids=true, to_apply=%region_0.1 | all-reduce | flops 7680 | bytes 61440 | tf_op jit(solution)/shard_map/psum | solution.py:503
  295.3 97.0 %all-reduce.12.cloned.1.call-done = (f32[4,768,40]{1,2,0:T(8,128)}, f32[768,40]{0,1:T(8,128)}, f32[3072,40]{0,1:T(8,128)}, f32[4,3,40,192]{3,2,1,0:T(8,128)}, f3...) async-done(((f32[4,768,40]{1,2,0:T(8,128)}, f32[768,40]{0,1:T(8,128)}, f32[3072,40]{0,1:T(8,128)}, f32[4,3,40,192]{3,2,1,0:T(8,128)}, f32[40,768]{1,0:T(8,128)}, ...) | async-done | bytes 2211856 | tf_op jit(solution)/shard_map/psum | solution.py:503
  392.2 1.6 dynamic-slice_bitcast_fusion
  393.9 1.6 dynamic-slice_bitcast_fusion.1
  395.4 1.8 copy.45
  397.3 0.6 copy.46
  397.9 0.8 copy.47
  398.7 0.6 copy.48
  399.4 0.6 copy.49
  (51 shorter events, 0.2 us)
Async XLA Ops:
  7.2 37.2 %all-gather.12.cloned.1.call-start = ((), (), s32[]{:S(2)}) async-start(), calls=%async_computation | async-start | bytes 4423680 | tf_op jit(solution)/shard_map/all_gather | solution.py:405
  7.2 2.9 copy-start.3
  7.9 2.2 copy-start.17
  7.9 2.3 copy-start.18
  7.9 2.8 copy-start.20
  7.9 8.9 %copy-start.12 = (bf16[3,40,192]{2,1,0:T(8,128)(2,1)S(1)}, bf16[3,40,192]{2,1,0:T(8,128)(2,1)}, u32[]{:S(2)}) copy-start(bf16[3,40,192]{2,1,0:T(8,128)(2,1)} %param.33) | copy-start | bytes 138244
  8.0 76.3 %all-gather.14.cloned.1.call-start = ((), (), s32[]{:S(2)}) async-start(), calls=%async_computation.1 | async-start | bytes 1474560 | tf_op jit(solution)/shard_map/all_gather | solution.py:405
  8.7 94.8 %all-gather.16.cloned.1.call-start = ((), (), s32[]{:S(2)}) async-start(), calls=%async_computation.2 | async-start | bytes 5898240 | tf_op jit(solution)/shard_map/all_gather | solution.py:405
  9.4 15.6 %copy-start.13 = (bf16[40,768]{1,0:T(8,128)(2,1)S(1)}, bf16[40,768]{1,0:T(8,128)(2,1)}, u32[]{:S(2)}) copy-start(bf16[40,768]{1,0:T(8,128)(2,1)} %param.35) | copy-start | bytes 184324
  9.4 132.9 %all-gather.18.cloned.1.call-start = ((), (), s32[]{:S(2)}) async-start(), calls=%async_computation.3 | async-start | bytes 5898240 | tf_op jit(solution)/shard_map/all_gather | solution.py:405
  10.0 24.5 %copy-start.4 = (bf16[3072,40]{0,1:T(8,128)(2,1)S(1)}, bf16[3072,40]{0,1:T(8,128)(2,1)}, u32[]{:S(2)}) copy-start(bf16[3072,40]{0,1:T(8,128)(2,1)} %param.32) | copy-start | bytes 737284
  10.0 382.2 %all-reduce.12.cloned.1.call-start = ((), (), s32[]{:S(2)}) async-start(), calls=%async_computation.4 | async-start | bytes 4669440 | tf_op jit(solution)/shard_map/psum | solution.py:503
  23.0 12.3 %copy-start.14 = (bf16[768,40]{0,1:T(8,128)(2,1)S(1)}, bf16[768,40]{0,1:T(8,128)(2,1)}, u32[]{:S(2)}) copy-start(bf16[768,40]{0,1:T(8,128)(2,1)} %param.31) | copy-start | bytes 184324
  23.0 13.0 %copy-start.15 = (bf16[40,768]{1,0:T(8,128)(2,1)S(1)}, bf16[40,768]{1,0:T(8,128)(2,1)}, u32[]{:S(2)}) copy-start(bf16[40,768]{1,0:T(8,128)(2,1)} %param.34) | copy-start | bytes 184324
  23.0 13.6 %copy-start.16 = (bf16[40,768]{1,0:T(8,128)(2,1)S(1)}, bf16[40,768]{1,0:T(8,128)(2,1)}, u32[]{:S(2)}) copy-start(bf16[40,768]{1,0:T(8,128)(2,1)} %param.36) | copy-start | bytes 184324
  23.8 13.5 %copy-start.19 = (f32[768]{0:T(1024)S(1)}, f32[768]{0:T(1024)}, u32[]{:S(2)}) copy-start(f32[768]{0:T(1024)} %param.23) | copy-start | bytes 9220
  197.1 50.2 %copy-start.11 = (f32[64,768]{1,0:T(8,128)S(1)}, f32[64,768]{1,0:T(8,128)}, u32[]{:S(2)}) copy-start(f32[64,768]{1,0:T(8,128)} %get-tuple-element.47) | copy-start | bytes 589828
  246.1 3.0 copy-start.2
  247.3 2.8 copy-start.1
  249.2 1.7 copy-start.10
  249.2 2.4 copy-start.9
  249.2 3.0 copy-start.8
  392.2 5.0 %copy-start.7 = (f32[768,40]{0,1:T(8,128)S(1)}, f32[768,40]{0,1:T(8,128)}, u32[]{:S(2)}) copy-start(f32[768,40]{0,1:T(8,128)} %get-tuple-element.65) | copy-start | bytes 368644
  392.2 5.7 %copy-start = (f32[3072,40]{0,1:T(8,128)S(1)}, f32[3072,40]{0,1:T(8,128)}, u32[]{:S(2)}) copy-start(f32[3072,40]{0,1:T(8,128)} %get-tuple-element.66) | copy-start | bytes 1474564
  392.2 6.5 %copy-start.6 = (f32[40,768]{1,0:T(8,128)S(1)}, f32[40,768]{1,0:T(8,128)}, u32[]{:S(2)}) copy-start(f32[40,768]{1,0:T(8,128)} %get-tuple-element.68) | copy-start | bytes 368644
  392.2 7.1 %copy-start.5 = (f32[40,768]{1,0:T(8,128)S(1)}, f32[40,768]{1,0:T(8,128)}, u32[]{:S(2)}) copy-start(f32[40,768]{1,0:T(8,128)} %get-tuple-element.70) | copy-start | bytes 368644
Sparse Core Ops, SparseCore 0:
  9.6 34.7 all-gather.11
  45.9 18.4 all-gather.13
  66.0 37.4 all-gather.15
  104.9 37.4 all-gather.17
  253.9 138.3 all-reduce.11

commit v2 on v1

--- a/solution.py
+++ b/solution.py
@@ -28,6 +28,74 @@
     return lax.dot_general(a, b, (((0,), (0,)), ((), ())), preferred_element_type=F32)
 
 
+def flip(index, bit):
+    return index + (1 - 2 * ((index // bit) % 2)) * bit
+
+
+def group_at(member, step):
+    high = (member // 2 + step // 2) % 2
+    low = (member % 2 + step % 2) % 2
+    return 2 * high + low
+
+
+class Links:
+    def __init__(self, send, recv):
+        self.send, self.recv, self.count, self.waiting = send, recv, 0, []
+
+    def __call__(self, src, dst, device):
+        n = self.count
+        self.count += 1
+        return pltpu.make_async_remote_copy(
+            src_ref=src, dst_ref=dst, send_sem=self.send.at[n], recv_sem=self.recv.at[n],
+            device_id=device, device_id_type=pl.DeviceIdType.MESH,
+        )
+
+
+def greet(devices):
+    barrier = pltpu.get_barrier_semaphore()
+    for device in devices:
+        pl.semaphore_signal(barrier, inc=1, device_id=device, device_id_type=pl.DeviceIdType.MESH)
+    pl.semaphore_wait(barrier, len(devices))
+
+
+class Places:
+    def __init__(self):
+        d, t = lax.axis_index("dp"), lax.axis_index("tensor")
+        self.d, self.t = d, t
+        self.half = d % 2
+        self.core = (d, flip(t, 1))
+        self.y = (d, flip(t, 2))
+        self.across = (d, flip(flip(t, 1), 2))
+        self.x = (flip(d, 1), t)
+        self.y_group = flip(t, 2)
+
+
+def spread(links, places, own, whole, chunks):
+    g, g2 = places.t, places.y_group
+    total = own.shape[0]
+    rows = total // 2 // chunks
+    out = {"core": links(own, whole.at[g], places.core), "y": [], "x": [], "near": [], "far": []}
+    for j in range(chunks):
+        mine = pl.ds(pl.multiple_of(places.half * (total // 2) + j * rows, 16), rows)
+        other = pl.ds(pl.multiple_of((1 - places.half) * (total // 2) + j * rows, 16), rows)
+        out["y"].append(links(own.at[mine], whole.at[g, mine], places.y))
+        out["x"].append(links(whole.at[g2, mine], whole.at[g2, mine], places.x))
+        out["near"].append(links(whole.at[g2, mine], whole.at[g2, mine], places.core))
+        out["far"].append(links(whole.at[g2, other], whole.at[g2, other], places.core))
+    return out
+
+
+def relay(item, j):
+    item["y"][j].wait_recv()
+    item["x"][j].start()
+    item["near"][j].start()
+
+
+def close(item, j):
+    item["x"][j].wait_recv()
+    item["far"][j].start()
+
+
 def bucket_of(relative):
     half = NB // 2
     exact = half // 2
@@ -47,10 +115,84 @@
 
 
 def attention_forward(
-    lens, x_ref, g1_ref, wsm_ref, wqkv_ref, bqkv_ref, rb_ref, oh_ref,
+    lens, x_ref, g1_ref, wsm_ref, oh_ref, wqkv_own, bqkv_own, rb_own, wo_own, win_own, bin_own,
     n1_ref, low_ref, gate_ref, gate_t_ref, gated_ref, qkv_ref, e_ref, r_ref, ctx_ref,
-    small, urow, brow,
+    wqkv_all, bqkv_all, wo_all, win_all, bin_all,
+    wqkv_ref, bqkv_ref, rb_ref, urow, brow, send, recv, local,
 ):
+    places = Places()
+    t = places.t
+    greet([places.core, places.y, places.across, places.x])
+    links = Links(send, recv)
+    moves = {
+        "qkv": spread(links, places, wqkv_own, wqkv_ref, 2),
+        "o": spread(links, places, wo_own, wo_all, 1),
+        "in": spread(links, places, win_own, win_all, 2),
+    }
+    small = {
+        who: [
+            links(rb_own, rb_ref.at[t], device),
+            links(bqkv_own, bqkv_ref.at[t], device),
+            links(bin_own, bin_all.at[t], device),
+        ]
+        for who, device in (("core", places.core), ("y", places.y), ("across", places.across))
+    }
+    own = [
+        pltpu.make_async_copy(a, b.at[t], local.at[i])
+        for i, (a, b) in enumerate(
+            (
+                (wqkv_own, wqkv_ref), (bqkv_own, bqkv_ref), (rb_own, rb_ref),
+                (wo_own, wo_all), (win_own, win_all), (bin_own, bin_all),
+            )
+        )
+    ]
+    for copy in own[:3]:
+        copy.start()
+    moves["qkv"]["y"][0].start()
+    moves["qkv"]["core"].start()
+    for who in ("core", "y", "across"):
+        small[who][0].start()
+        small[who][1].start()
+    moves["qkv"]["y"][1].start()
+    for copy in own[3:]:
+        copy.start()
+
+    def at_step(step):
+        if step == 1:
+            relay(moves["qkv"], 0)
+            moves["o"]["y"][0].start()
+            moves["o"]["core"].start()
+        if step == 2:
+            relay(moves["qkv"], 1)
+            moves["in"]["y"][0].start()
+            moves["in"]["core"].start()
+        if step == 3:
+            close(moves["qkv"], 0)
+            moves["qkv"]["core"].wait_recv()
+            small["core"][0].wait_recv()
+            small["core"][1].wait_recv()
+        if step == 4:
+            relay(moves["o"], 0)
+            close(moves["qkv"], 1)
+            moves["in"]["y"][1].start()
+            for who in ("core", "y", "across"):
+                small[who][2].start()
+        if step == 6:
+            relay(moves["in"], 0)
+            close(moves["o"], 0)
+            small["y"][0].wait_recv()
+            small["y"][1].wait_recv()
+        if step == 9:
+            relay(moves["in"], 1)
+            close(moves["in"], 0)
+            for j in range(2):
+                moves["qkv"]["near"][j].wait_recv()
+                moves["qkv"]["far"][j].wait_recv()
+            small["across"][0].wait_recv()
+            small["across"][1].wait_recv()
+        if step == 11:
+            close(moves["in"], 1)
+
     tokens = x_ref.shape[0]
     groups = wqkv_ref.shape[0]
     inner = wqkv_ref.shape[1] // 3
@@ -81,9 +223,11 @@
         return c
 
     lax.fori_loop(0, tokens // tb, norm, 0)
-    u = nn(rb_ref[...], oh_ref[...])
-    for h in range(groups * heads_here):
-        urow[h] = u[h : h + 1]
+    for copy in own[:3]:
+        copy.wait()
+
+    def keep(k, g):
+        return pltpu.make_async_copy(wqkv_ref.at[g], wqkv_all.at[g], local.at[6 + k])
 
     maskrow = jnp.where(
         lax.broadcasted_iota(jnp.int32, (16, seq), 1) < lens[seqs - 1], 0.0, NEG
@@ -91,58 +235,122 @@
     maskrow = jnp.where(lax.broadcasted_iota(jnp.int32, (16, seq), 0) == 0, maskrow, 0.0).astype(BF16)
     onerow = (lax.broadcasted_iota(jnp.int32, (16, seq), 0) == 0).astype(F32).astype(BF16)
 
-    def group(g, c):
-        proj = nt(wqkv_ref[g], n1_ref[...])
-        for p in range(3):
-            up = tn(bqkv_ref[g, p], gated_ref[p * PAD : (p + 1) * PAD, :])
-            qkv_ref[g, p] = (proj[p * inner : (p + 1) * inner] + up).astype(BF16)
-
-        def head(h, c):
-            gh = g * heads_here + h
-            line = jnp.broadcast_to(urow[gh], (128, 2 * seq))
-            brow[...] = pltpu.roll(line, 0, 1, stride=1, stride_axis=0)[:, : 2 * seq - 128]
-            feats = pl.ds(pl.multiple_of(h * hd, hd), hd)
-            for s in range(seqs):
-                q = qkv_ref[g, 0, feats, s * seq : (s + 1) * seq]
-                k = qkv_ref[g, 1, feats, s * seq : (s + 1) * seq]
-                v = qkv_ref[g, 2, feats, s * seq : (s + 1) * seq]
-                if s > 0:
-                    q = jnp.concatenate([q, onerow], axis=0)
-                    k = jnp.concatenate([k, maskrow], axis=0)
-                qb = 256
-                for b in range(seq // qb):
-                    st = tn(k, q[:, b * qb : (b + 1) * qb])
-                    bias = jnp.concatenate(
-                        [
-                            brow[:, seq - 128 - 128 * kb + b * qb : seq - 128 - 128 * kb + (b + 1) * qb]
-                            for kb in range(seq // 128)
-                        ],
-                        axis=0,
-                    )
-                    st = st + bias
-                    ex = jnp.exp(st - jnp.max(st, axis=0, keepdims=True))
-                    recip = 1.0 / jnp.sum(ex, axis=0, keepdims=True)
-                    eb = ex.astype(BF16)
-                    e_ref[gh * seqs + s, :, b * qb : (b + 1) * qb] = eb
-                    r_ref[gh, :, s * seq + b * qb : s * seq + (b + 1) * qb] = recip
-                    ot = nn(v, eb) * recip
-                    ctx_ref[
-                        pl.ds(pl.multiple_of(gh * hd, hd), hd), s * seq + b * qb : s * seq + (b + 1) * qb
-                    ] = ot.astype(BF16)
-            return c
-
-        lax.fori_loop(0, heads_here, head, 0)
+    def head(gh, c):
+        for step in (1, 2, 3, 4, 6, 9, 11):
+            pl.when(gh == step)(lambda step=step: at_step(step))
+        k = gh // heads_here
+        h = gh % heads_here
+        g = group_at(t, k)
+
+        @pl.when(h == 0)
+        def _():
+            keep(k, g).start()
+            u = nn(rb_ref[g], oh_ref[...])
+            for i in range(heads_here):
+                urow[i] = u[i : i + 1]
+            proj = nt(wqkv_ref[g], n1_ref[...])
+            for p in range(3):
+                up = tn(bqkv_ref[g, p * PAD : (p + 1) * PAD], gated_ref[p * PAD : (p + 1) * PAD, :])
+                qkv_ref[k, p] = (proj[p * inner : (p + 1) * inner] + up).astype(BF16)
+
+        line = jnp.broadcast_to(urow[h], (128, 2 * seq))
+        brow[...] = pltpu.roll(line, 0, 1, stride=1, stride_axis=0)[:, : 2 * seq - 128]
+        feats = pl.ds(pl.multiple_of(h * hd, hd), hd)
+        full = pl.ds(pl.multiple_of(g * inner + h * hd, hd), hd)
+        for s in range(seqs):
+            q = qkv_ref[k, 0, feats, s * seq : (s + 1) * seq]
+            key = qkv_ref[k, 1, feats, s * seq : (s + 1) * seq]
+            v = qkv_ref[k, 2, feats, s * seq : (s + 1) * seq]
+            if s > 0:
+                q = jnp.concatenate([q, onerow], axis=0)
+                key = jnp.concatenate([key, maskrow], axis=0)
+            qb = 256
+            for b in range(seq // qb):
+                part = slice(s * seq + b * qb, s * seq + (b + 1) * qb)
+                st = tn(key, q[:, b * qb : (b + 1) * qb])
+                bias = jnp.concatenate(
+                    [
+                        brow[:, seq - 128 - 128 * kb + b * qb : seq - 128 - 128 * kb + (b + 1) * qb]
+                        for kb in range(seq // 128)
+                    ],
+                    axis=0,
+                )
+                st = st + bias
+                ex = jnp.exp(st - jnp.max(st, axis=0, keepdims=True))
+                recip = 1.0 / jnp.sum(ex, axis=0, keepdims=True)
+                eb = ex.astype(BF16)
+                e_ref[gh * seqs + s, :, b * qb : (b + 1) * qb] = eb
+                r_ref[gh, :, part] = recip
+                ctx_ref[full, part] = (nn(v, eb) * recip).astype(BF16)
         return c
 
-    lax.fori_loop(0, groups, group, 0)
+    lax.fori_loop(0, groups * heads_here, head, 0)
+    for k in range(groups):
+        keep(k, group_at(t, k)).wait()
+    bqkv_all[...] = bqkv_ref[...]
+    for copy in own[3:]:
+        copy.wait()
+    for j in range(1):
+        moves["o"]["near"][j].wait_recv()
+        moves["o"]["far"][j].wait_recv()
+    for j in range(2):
+        moves["in"]["near"][j].wait_recv()
+        moves["in"]["far"][j].wait_recv()
+    moves["o"]["core"].wait_recv()
+    moves["in"]["core"].wait_recv()
+    for who in small:
+        small[who][2].wait_recv()
+        for copy in small[who]:
+            copy.wait_send()
+    for item in moves.values():
+        item["core"].wait_send()
+        for kind in ("y", "x", "near", "far"):
+            for copy in item[kind]:
+                copy.wait_send()
 
 
 def feed_forward(
     x_ref, c_ref, g2_ref, ctx_ref, gate_ref, wo_ref, ao_ref, bo_ref, ain_ref, bin_ref, aout_ref, bout_ref,
-    win_ref, wout_ref,
+    win_all, wout_own,
     y_ref, dh_ref, dctx_ref, z_ref, gao_ref, gaout_ref, gbo_ref, gbin_ref, gbout_ref, gain_ref,
     h1, n2, acc, dn2, low_o, low_in, low_out, d_low_in, gated_in, gated_in_t, dgo, dgo_t, d_low_out,
+    win_ref, wout_ref, send, recv, local,
 ):
+    places = Places()
+    t = places.t
+    greet([places.core, places.y, places.x])
+    out = spread(Links(send, recv), places, wout_own, wout_ref, 3)
+    own = pltpu.make_async_copy(wout_own, wout_ref.at[t], local.at[0])
+    for j in range(3):
+        out["y"][j].start()
+    out["core"].start()
+    own.start()
+
+    def win_copy(k, g):
+        return pltpu.make_async_copy(win_all.at[g], win_ref.at[g], local.at[1 + k])
+
+    for k in range(4):
+        win_copy(k, group_at(t, k)).start()
+
+    def at_step(step):
+        if step == 0:
+            own.wait()
+            relay(out, 0)
+        if step == 2:
+            relay(out, 1)
+        if step == 4:
+            relay(out, 2)
+            close(out, 0)
+            out["core"].wait_recv()
+        if step == 6:
+            close(out, 1)
+        if step == 8:
+            close(out, 2)
+        if step == 12:
+            for j in range(3):
+                out["near"][j].wait_recv()
+                out["far"][j].wait_recv()
+
     tokens = x_ref.shape[0]
     groups = win_ref.shape[0]
     tb = 256
@@ -180,9 +388,17 @@
     lax.fori_loop(0, blocks, first, 0)
 
     def chunk(step, c):
-        k = step // blocks
+        for point in (0, 2, 4, 6, 8, 12):
+            pl.when(step == point)(lambda point=point: at_step(point))
+        n = step // blocks
         i = step % blocks
         rows = rows_of(i)
+        k = group_at(t, n)
+
+        @pl.when(i == 0)
+        def _():
+            win_copy(n, k).wait()
+
         pre = nn(n2[rows, :], win_ref[k]) + nn(gated_in[rows, :], bin_ref[k])
         da = nt(c_ref[rows, :], wout_ref[k]) + nn(dgo[rows, :], aout_ref[k])
         sig = 1.0 / (1.0 + jnp.exp(-pre))
@@ -195,14 +411,14 @@
         ga = nn(dgo_t[:, rows], active)
         gb = nn(gated_in_t[:, rows], dpre)
 
-        @pl.when(k == 0)
+        @pl.when(n == 0)
         def _():
             acc[rows, :] = part
             low_out[rows, :] = lo
             dn2[rows, :] = dn
             d_low_in[rows, :] = dl
 
-        @pl.when(k > 0)
+        @pl.when(n > 0)
         def _():
             acc[rows, :] += part
             low_out[rows, :] += lo
@@ -263,6 +479,10 @@
         return c
 
     lax.fori_loop(0, blocks, last, 0)
+    out["core"].wait_send()
+    for kind in ("y", "x", "near", "far"):
+        for copy in out[kind]:
+            copy.wait_send()
 
 
 def attention_backward(
@@ -280,16 +500,20 @@
     hd = inner // heads_here
     qb = 256
 
-    def group(g, c):
+    t = lax.axis_index("tensor")
+
+    def group(n, c):
+        g = group_at(t, n)
+
         def head(h, c):
-            gh = g * heads_here + h
+            gh = n * heads_here + h
             feats = pl.ds(pl.multiple_of(h * hd, hd), hd)
-            full = pl.ds(pl.multiple_of(gh * hd, hd), hd)
+            full = pl.ds(pl.multiple_of(g * inner + h * hd, hd), hd)
             for s in range(seqs):
                 cols = slice(s * seq, (s + 1) * seq)
-                q = qkv_ref[g, 0, feats, cols]
-                k = qkv_ref[g, 1, feats, cols]
-                v = qkv_ref[g, 2, feats, cols]
+                q = qkv_ref[n, 0, feats, cols]
+                k = qkv_ref[n, 1, feats, cols]
+                v = qkv_ref[n, 2, feats, cols]
                 dk = jnp.zeros((hd, seq), F32)
                 dv = jnp.zeros((hd, seq), F32)
                 for b in range(seq // qb):
@@ -309,23 +533,23 @@
         lax.fori_loop(0, heads_here, head, 0)
         dn = tn(wqkv_ref[g], dqkv[...])
 
-        @pl.when(g == 0)
+        @pl.when(n == 0)
         def _():
             dn1[...] = dn
 
-        @pl.when(g > 0)
+        @pl.when(n > 0)
         def _():
             dn1[...] += dn
 
         for p in range(3):
             d = dqkv[p * inner : (p + 1) * inner, :]
-            dl = nn(bqkv_ref[g, p], d)
-
-            @pl.when(g == 0)
+            dl = nn(bqkv_ref[g, p * PAD : (p + 1) * PAD], d)
+
+            @pl.when(n == 0)
             def _():
                 dlow[p * PAD : (p + 1) * PAD, :] = dl
 
-            @pl.when(g > 0)
+            @pl.when(n > 0)
             def _():
                 dlow[p * PAD : (p + 1) * PAD, :] += dl
 
@@ -365,17 +589,23 @@
     lax.fori_loop(0, tokens // tb, finish, 0)
 
 
-def call(body, name, outs, scratch, args, smem=0):
-    specs = [pl.BlockSpec(memory_space=pltpu.SMEM)] * smem
-    specs += [pl.BlockSpec(memory_space=pltpu.VMEM)] * (len(args) - smem)
+ANY = "any"
+SEM = "semaphores"
+
+
+def call(body, name, outs, scratch, args, kinds, collective=None):
+    def spec(kind):
+        return pl.BlockSpec(memory_space={"s": pltpu.SMEM, "v": pltpu.VMEM, "a": pl.ANY}[kind])
+
+    extra = {} if collective is None else {"collective_id": collective, "has_side_effects": True}
     return pl.pallas_call(
         body,
         name=name,
-        out_shape=[jax.ShapeDtypeStruct(s, d) for s, d in outs],
-        in_specs=specs,
-        out_specs=[pl.BlockSpec(memory_space=pltpu.VMEM)] * len(outs),
-        scratch_shapes=[pltpu.VMEM(s, d) for s, d in scratch],
-        compiler_params=pltpu.CompilerParams(vmem_limit_bytes=VMEM_LIMIT),
+        out_shape=[jax.ShapeDtypeStruct(o[0], o[1]) for o in outs],
+        in_specs=[spec(k) for k in kinds],
+        out_specs=[spec("a" if len(o) > 2 else "v") for o in outs],
+        scratch_shapes=[pltpu.SemaphoreType.DMA((n[1],)) if n[0] == SEM else pltpu.VMEM(*n) for n in scratch],
+        compiler_params=pltpu.CompilerParams(vmem_limit_bytes=VMEM_LIMIT, **extra),
     )(*args)
 
 
@@ -401,9 +631,6 @@
     cols = a_in.shape[2]
     rank = cols // experts
 
-    def gather(v):
-        return lax.all_gather(v, "tensor", axis=0)
-
     x = layer_inputs.reshape(tokens, width)
     cot = cotangent.reshape(tokens, width)
     g1 = first_gain.reshape(1, width)
@@ -411,14 +638,10 @@
     at = jnp.swapaxes(a_in, 1, 2)
     rrep = jnp.repeat(router.T, rank, axis=0)
     wsm = pad_rows(jnp.concatenate([at[:3], rrep[None]], axis=0)).reshape(4 * PAD, width)
-    wqkv_all = gather(jnp.swapaxes(wqkv, 1, 2).reshape(3 * inner, width))
-    bqkv_all = pad_rows(gather(b_qkv))
-    rb = gather(bias_table.T).reshape(heads, NB)
-    rb = jnp.pad(rb, ((0, 16 - heads % 16), (0, 0)))
-    wo_all = gather(wo).reshape(groups * inner, width)
-    win_all = gather(win)
-    wout_all = gather(wout)
-    bin_all = pad_rows(gather(b_in))
+    wqkv_own = jnp.swapaxes(wqkv, 1, 2).reshape(3 * inner, width)
+    bqkv_own = pad_rows(b_qkv).reshape(3 * PAD, inner)
+    rb_own = jnp.pad(bias_table.T, ((0, 16 - heads_here), (0, 0)))
+    bin_own = pad_rows(b_in)
     ao = pad_rows(a_o.T)
     ain = pad_rows(at[3])
     aout = pad_rows(jnp.swapaxes(a_out.T.reshape(cols, groups, hidden), 0, 1))
@@ -426,7 +649,7 @@
     bout = pad_rows(b_out)
     onehot = jnp.asarray(bucket_lines(seq), BF16)
 
-    n1, low, gate, gate_t, gated, qkv, e, r, ctx = call(
+    n1, low, gate, gate_t, gated, qkv, e, r, ctx, wqkv_all, bqkv_all, wo_all, win_all, bin_all = call(
         attention_forward,
         "attention_forward",
         [
@@ -439,15 +662,27 @@
             ((heads * seqs, seq, seq), BF16),
             ((heads, 1, tokens), F32),
             ((groups * inner, tokens), BF16),
+            ((groups, 3 * inner, width), BF16, ANY),
+            ((groups, 3 * PAD, inner), BF16),
+            ((groups, inner, width), BF16, ANY),
+            ((groups, width, hidden), BF16, ANY),
+            ((groups, PAD, hidden), BF16, ANY),
         ],
         [
-            ((8, 128), F32),
-            ((heads, 1, 2 * seq), F32),
+            ((groups, 3 * inner, width), BF16),
+            ((groups, 3 * PAD, inner), BF16),
+            ((groups, 16, NB), BF16),
+            ((heads_here, 1, 2 * seq), F32),
             ((128, 2 * seq - 128), F32),
+            (SEM, 32),
+            (SEM, 32),
+            (SEM, 10),
         ],
-        (lengths, x, g1, wsm, wqkv_all, bqkv_all, rb, onehot),
-        smem=1,
+        (lengths, x, g1, wsm, onehot, wqkv_own, bqkv_own, rb_own, wo, win, bin_own),
+        "svvvvaaaaaa",
+        collective=0,
     )
+    wo_all = wo_all.reshape(groups * inner, width)
     y, dh, dctx, z, gao, gaout, gbo, gbin, gbout, gain = call(
         feed_forward,
         "feed_forward",
@@ -477,8 +712,15 @@
             ((tokens, PAD), BF16),
             ((PAD, tokens), BF16),
             ((tokens, PAD), F32),
+            ((groups, width, hidden), BF16),
+            ((groups, hidden, width), BF16),
+            (SEM, 16),
+            (SEM, 16),
+            (SEM, 5),
         ],
-        (x, cot, g2, ctx, gate_t, wo_all, ao, bo, ain, bin_all, aout, bout, win_all, wout_all),
+        (x, cot, g2, ctx, gate_t, wo_all, ao, bo, ain, bin_all, aout, bout, win_all, wout),
+        "v" * 12 + "aa",
+        collective=1,
     )
     c = np.arange(PAD)
     same = (c[:, None] // rank == c[None, :] // rank) & (c[None, :] < cols)
@@ -497,6 +739,7 @@
             ((4 * PAD, tokens), BF16),
         ],
         (x, g1, wsm, wqkv_all, bqkv_all, n1, low, gate, gated, qkv, e, r, ctx, dctx, z, dh, jnp.asarray(same, BF16)),
+        "v" * 17,
     )
     g_in = jnp.concatenate([gsm.reshape(4, PAD, width)[:3, :cols], gain[None, :cols]], axis=0)
     g_router = gsm.reshape(4, PAD, width)[3, :cols:rank]

time: 407 us -> 351 us (0.86)
  waiting for transfers between devices: 163 us -> 97.2 us
  Pallas kernels: 144 us -> 168 us
  blocking collectives: 61.4 us -> 40.8 us
  local copies, waits for them, and re-layouts: 22.3 us -> 28.7 us
    all_gather x4 -> x0, waiting for transfers between devices: 63.9 us -> none  [gather(): return lax.all_gather(v, 'tensor', axis=0)]
    pallas_call x3, Pallas kernels: 144 us -> 168 us  [call(): pl.pallas_call(body, name=name, out_shape=[jax.ShapeDtypeStruct(o[0], o[1...]
    all_gather x3 -> x0, blocking collectives: 20.9 us -> none  [gather(): return lax.all_gather(v, 'tensor', axis=0)]
  transfers between devices with their start and end apart: 5 -> 1, of which waited for: 4 -> 1; matrix products, arithmetic and copies ran while one was open for 2% -> 0% of each run, Pallas kernels for 10% -> 0%
where the time goes in v2:
time: 351 us; the launch traced here: 350 us
  Pallas kernels  168 us (48%)
  waiting for transfers between devices  97.2 us (28%)
  blocking collectives  40.8 us (12%)
  local copies, waits for them, and re-layouts  28.7 us (8%)
  between operations  14.2 us (4%)
    pallas_call x3, Pallas kernels, call(): pl.pallas_call(body, name=name, out_shape=[jax.ShapeDtypeStruct(o[0], o[1...  168 us
    psum x1, waiting for transfers between devices, shards(): lax.psum((g_router, g_in, gao[:cols], gaout[:, :cols], gbqkv[:, :, :cols]...  97.1 us
    psum x1, blocking collectives, shards(): lax.psum((g_router, g_in, gao[:cols], gaout[:, :cols], gbqkv[:, :, :cols]...  40.8 us
  transfers between devices with their start and end apart: 1, of which 1 were waited for; matrix products, arithmetic and copies ran while one was open for 0% of the time, Pallas kernels for 0%

profile of v2, /device:TPU:0, one launch (start us, length us, event | category | flops | bytes accessed | tf_op | source)
XLA Modules:
  0.0 350.3 jit_solution(17996146084705586575)
XLA Ops:
  7.2 0.0 copy-start.12
  7.2 0.0 copy-start.13
  7.2 0.0 copy-start.14
  7.2 0.0 all-reduce.12.cloned.1.call-start
  7.3 1.0 slice.44
  8.2 0.8 slice_bitcast_fusion.3
  9.1 0.8 broadcast_in_dim.6
  9.8 1.3 reshape.63.g1_ref
  11.1 1.5 pad.32
  12.6 1.5 pad.34.bin_own
  14.1 1.3 pad.33.rb_own
  15.3 0.6 pad.37.ain_ref
  16.0 1.0 copy.35
  17.0 0.8 pad.38.aout_ref
  17.7 0.6 pad.35.ao_ref
  18.4 0.0 copy-done.13
  18.4 0.6 pad.36.bo_ref
  19.0 0.6 pad.39.bout_ref
  19.7 0.6 reshape.62.g2_ref
  20.3 0.8 fusion.2
  21.0 61.6 %attention_forward.1 = (bf16[1024,768]{1,0:T(8,128)(2,1)}, f32[192,1024]{1,0:T(8,128)}, f32[64,1024]{1,0:T(8,128)}, f32[1024,128]{1,0:T(8,128)}, bf16[192,1024]{...) custom-call(s32[2]{0:T(128)} %lens.1, ...), custom_call_target="tpu_custom_call" | custom-call | tf_op jit(solution)/shard_map/attention_forward/pallas_call | solution.py:601
  82.7 57.4 %feed_forward.1 = (bf16[1024,768]{1,0:T(8,128)(2,1)}, f32[1024,768]{1,0:T(8,128)}, bf16[768,1024]{1,0:T(8,128)(2,1)}, f32[64,1024]{1,0:T(8,128)}, f32[64,768]{1,...) custom-call(bf16[1024,768]{1,0:T(8,128)(2,1)} %bitcast.45, ...), custom_call_target="tpu_custom_call" | custom-call | tf_op jit(solution)/shard_map/feed_forward/pallas_call | solution.py:601
  140.0 48.9 %attention_backward.1 = (f32[1024,768]{1,0:T(8,128)}, f32[256,768]{1,0:T(8,128)}, f32[4,3,64,192]{3,2,1,0:T(8,128)}) custom-call(bf16[1024,768]{1,0:T(8,128)(2,1)} %bitcast.46, f32[1,768]{1,0:T(1,128)} %reshape.63.g1_ref, bf16[256,768]{1,0:T(8,128)(2,1)} %bitcast.48, bf16[4,576,768]{2,1,0:T(8,128)(2,1)} %get-tuple-element.43.wqkv_ref, ...), custom_call_target="tpu_custom_call" | custom-call | tf_op jit(solution)/shard_map/attention_backward/pallas_call | solution.py:601
  188.9 1.1 slice.46
  190.1 1.9 slice.40
  192.0 0.8 copy.33
  192.9 0.8 slice.42
  193.7 0.7 slice.41
  194.3 0.7 slice.43
  195.0 0.7 slice_bitcast_fusion.1
  195.7 0.8 maximum_bitcast_fusion
  196.5 0.0 all-reduce.12.cloned.1.call-update
  196.5 1.0 slice.35
  197.6 40.8 %psum.56 = f32[768,10]{0,1:T(8,128)} all-reduce(f32[768,10]{0,1:T(8,128)S(1)} %bitcast.61), channel_id=1, replica_groups=mesh['dp'=8,'tensor'=4] {'dp','tensor'}, use_global_device_ids=true, to_apply=%region_0.1 | all-reduce | flops 7680 | bytes 61440 | tf_op jit(solution)/shard_map/psum | solution.py:746
  238.3 97.1 %all-reduce.12.cloned.1.call-done = (f32[4,768,40]{1,2,0:T(8,128)}, f32[768,40]{0,1:T(8,128)}, f32[3072,40]{0,1:T(8,128)}, f32[4,3,40,192]{3,2,1,0:T(8,128)}, f3...) async-done(((f32[4,768,40]{1,2,0:T(8,128)}, f32[768,40]{0,1:T(8,128)}, f32[3072,40]{0,1:T(8,128)}, f32[4,3,40,192]{3,2,1,0:T(8,128)}, f32[40,768]{1,0:T(8,128)}, ...) | async-done | bytes 2211856 | tf_op jit(solution)/shard_map/psum | solution.py:746
  335.5 1.6 dynamic-slice_bitcast_fusion
  337.0 1.6 dynamic-slice_bitcast_fusion.1
  338.6 1.1 copy.44
  339.7 0.2 copy-done.2
  339.9 0.8 copy.45
  340.7 0.0 copy-done.7
  340.7 0.6 copy.46
  341.3 0.0 copy-done.1
  341.3 0.8 copy.47
  342.1 0.0 copy-done.6
  342.1 0.6 copy.48
  342.8 0.0 copy-done.5
  342.8 0.6 copy.49
  (26 shorter events, 0.1 us)
Async XLA Ops:
  7.2 10.6 %copy-start.12 = (bf16[768,40]{0,1:T(8,128)(2,1)S(1)}, bf16[768,40]{0,1:T(8,128)(2,1)}, u32[]{:S(2)}) copy-start(bf16[768,40]{0,1:T(8,128)(2,1)} %param.31) | copy-start | bytes 184324
  7.2 11.2 %copy-start.13 = (bf16[40,768]{1,0:T(8,128)(2,1)S(1)}, bf16[40,768]{1,0:T(8,128)(2,1)}, u32[]{:S(2)}) copy-start(bf16[40,768]{1,0:T(8,128)(2,1)} %param.34) | copy-start | bytes 184324
  7.2 11.8 %copy-start.14 = (bf16[40,768]{1,0:T(8,128)(2,1)S(1)}, bf16[40,768]{1,0:T(8,128)(2,1)}, u32[]{:S(2)}) copy-start(bf16[40,768]{1,0:T(8,128)(2,1)} %param.36) | copy-start | bytes 184324
  7.2 12.5 %copy-start.15 = (f32[768]{0:T(1024)S(1)}, f32[768]{0:T(1024)}, u32[]{:S(2)}) copy-start(f32[768]{0:T(1024)} %param.23) | copy-start | bytes 9220
  7.2 328.2 %all-reduce.12.cloned.1.call-start = ((), (), s32[]{:S(2)}) async-start(), calls=%async_computation | async-start | bytes 4669440 | tf_op jit(solution)/shard_map/psum | solution.py:746
  140.0 50.0 %copy-start.11 = (f32[64,768]{1,0:T(8,128)S(1)}, f32[64,768]{1,0:T(8,128)}, u32[]{:S(2)}) copy-start(f32[64,768]{1,0:T(8,128)} %get-tuple-element.57) | copy-start | bytes 589828
  188.9 3.1 copy-start.4
  190.0 2.8 copy-start.3
  192.0 1.7 copy-start.10
  192.0 2.4 copy-start.9
  192.0 3.0 copy-start.8
  196.5 142.1 %copy-start = (bf16[1024,768]{1,0:T(8,128)(2,1)S(1)}, bf16[1024,768]{1,0:T(8,128)(2,1)}, u32[]{:S(2)}) copy-start(bf16[1024,768]{1,0:T(8,128)(2,1)} %get-tuple-element.42) | copy-start | bytes 4718596
  338.6 1.3 copy-start.2
  338.6 2.1 copy-start.7
  338.6 2.7 copy-start.1
  339.9 2.2 copy-start.6
  339.9 2.9 copy-start.5
Sparse Core Ops, SparseCore 0:
  196.6 138.7 all-reduce.11

commit v3 on v2

--- a/solution.py
+++ b/solution.py
@@ -14,6 +14,11 @@
 BF16 = jnp.bfloat16
 PAD = 64
 VMEM_LIMIT = 60 * 1024 * 1024
+
+
+def padded(a):
+    wide = jnp.concatenate([a.astype(F32), jnp.zeros((PAD - a.shape[0], a.shape[1]), F32)], axis=0)
+    return wide.astype(a.dtype)
 
 
 def nn(a, b):
@@ -115,13 +120,19 @@
 
 
 def attention_forward(
-    lens, x_ref, g1_ref, wsm_ref, oh_ref, wqkv_own, bqkv_own, rb_own, wo_own, win_own, bin_own,
+    lens, x_ref, g1_ref, at_ref, router_ref, oh_ref, bqkv_own, rb_own, bin_own, wqkv_own, wo_own, win_own,
     n1_ref, low_ref, gate_ref, gate_t_ref, gated_ref, qkv_ref, e_ref, r_ref, ctx_ref,
-    wqkv_all, bqkv_all, wo_all, win_all, bin_all,
-    wqkv_ref, bqkv_ref, rb_ref, urow, brow, send, recv, local,
+    wqkv_all, bqkv_ref, wo_all, win_all, bin_ref, wsm_ref,
+    wqkv_ref, rb_ref, urow, brow, send, recv, local,
 ):
     places = Places()
     t = places.t
+    for p in range(3):
+        bqkv_ref[t, p * PAD : (p + 1) * PAD] = padded(bqkv_own[p])
+    pick = lax.broadcasted_iota(jnp.int32, (16, rb_own.shape[0]), 0)
+    pick = pick == lax.broadcasted_iota(jnp.int32, (16, rb_own.shape[0]), 1)
+    rb_ref[t] = nn(pick.astype(F32).astype(BF16), rb_own[...]).astype(BF16)
+    bin_ref[t] = padded(bin_own[...])
     greet([places.core, places.y, places.across, places.x])
     links = Links(send, recv)
     moves = {
@@ -131,31 +142,33 @@
     }
     small = {
         who: [
-            links(rb_own, rb_ref.at[t], device),
-            links(bqkv_own, bqkv_ref.at[t], device),
-            links(bin_own, bin_all.at[t], device),
+            links(rb_ref.at[t], rb_ref.at[t], device),
+            links(bqkv_ref.at[t], bqkv_ref.at[t], device),
+            links(bin_ref.at[t], bin_ref.at[t], device),
         ]
         for who, device in (("core", places.core), ("y", places.y), ("across", places.across))
     }
     own = [
         pltpu.make_async_copy(a, b.at[t], local.at[i])
         for i, (a, b) in enumerate(
-            (
-                (wqkv_own, wqkv_ref), (bqkv_own, bqkv_ref), (rb_own, rb_ref),
-                (wo_own, wo_all), (win_own, win_all), (bin_own, bin_all),
-            )
+            ((wqkv_own, wqkv_ref), (wo_own, wo_all), (win_own, win_all))
         )
     ]
-    for copy in own[:3]:
-        copy.start()
+    own[0].start()
     moves["qkv"]["y"][0].start()
     moves["qkv"]["core"].start()
     for who in ("core", "y", "across"):
         small[who][0].start()
         small[who][1].start()
     moves["qkv"]["y"][1].start()
-    for copy in own[3:]:
-        copy.start()
+    own[1].start()
+    own[2].start()
+    for p in range(3):
+        wsm_ref[p * PAD : (p + 1) * PAD, :] = padded(at_ref[p])
+    experts = router_ref.shape[0]
+    spots = lax.broadcasted_iota(jnp.int32, (PAD, experts), 0) // 4
+    spots = spots == lax.broadcasted_iota(jnp.int32, (PAD, experts), 1)
+    wsm_ref[3 * PAD :, :] = nn(spots.astype(F32).astype(BF16), router_ref[...]).astype(BF16)
 
     def at_step(step):
         if step == 1:
@@ -206,7 +219,7 @@
     def norm(i, c):
         rows = pl.ds(pl.multiple_of(i * tb, tb), tb)
         x = x_ref[rows, :].astype(F32)
-        n1 = (x * lax.rsqrt(jnp.mean(x * x, axis=1, keepdims=True) + EPS) * g1_ref[...]).astype(BF16)
+        n1 = (x * lax.rsqrt(jnp.mean(x * x, axis=1, keepdims=True) + EPS) * g1_ref[...].reshape(1, x_ref.shape[1])).astype(BF16)
         n1_ref[rows, :] = n1
         small = nt(wsm_ref[...], n1)
         low = small[: 3 * PAD]
@@ -223,11 +236,10 @@
         return c
 
     lax.fori_loop(0, tokens // tb, norm, 0)
-    for copy in own[:3]:
-        copy.wait()
+    own[0].wait()
 
     def keep(k, g):
-        return pltpu.make_async_copy(wqkv_ref.at[g], wqkv_all.at[g], local.at[6 + k])
+        return pltpu.make_async_copy(wqkv_ref.at[g], wqkv_all.at[g], local.at[3 + k])
 
     maskrow = jnp.where(
         lax.broadcasted_iota(jnp.int32, (16, seq), 1) < lens[seqs - 1], 0.0, NEG
@@ -287,9 +299,8 @@
     lax.fori_loop(0, groups * heads_here, head, 0)
     for k in range(groups):
         keep(k, group_at(t, k)).wait()
-    bqkv_all[...] = bqkv_ref[...]
-    for copy in own[3:]:
-        copy.wait()
+    own[1].wait()
+    own[2].wait()
     for j in range(1):
         moves["o"]["near"][j].wait_recv()
         moves["o"]["far"][j].wait_recv()
@@ -310,11 +321,11 @@
 
 
 def feed_forward(
-    x_ref, c_ref, g2_ref, ctx_ref, gate_ref, wo_ref, ao_ref, bo_ref, ain_ref, bin_ref, aout_ref, bout_ref,
+    x_ref, c_ref, g2_ref, ctx_ref, gate_ref, wo_ref, ao_raw, bo_raw, at_raw, bin_ref, aout_raw, bout_raw,
     win_all, wout_own,
-    y_ref, dh_ref, dctx_ref, z_ref, gao_ref, gaout_ref, gbo_ref, gbin_ref, gbout_ref, gain_ref,
+    y_ref, dh_ref, dctx_ref, z_ref, part_ref,
     h1, n2, acc, dn2, low_o, low_in, low_out, d_low_in, gated_in, gated_in_t, dgo, dgo_t, d_low_out,
-    win_ref, wout_ref, send, recv, local,
+    win_ref, wout_ref, ao_ref, bo_ref, ain_ref, aout_ref, bout_ref, send, recv, local,
 ):
     places = Places()
     t = places.t
@@ -356,6 +367,16 @@
     tb = 256
     blocks = tokens // tb
 
+    hidden_here = aout_ref.shape[2]
+    cols = ao_raw.shape[0]
+    ao_ref[...] = padded(ao_raw[...])
+    bo_ref[...] = padded(bo_raw[...])
+    ain_ref[...] = padded(at_raw[3])
+    bout_ref[...] = padded(bout_raw[...])
+    for j in range(groups):
+        aout_ref[j] = padded(aout_raw[:, j * hidden_here : (j + 1) * hidden_here])
+    part_ref[...] = jnp.zeros_like(part_ref)
+
     def rows_of(i):
         return pl.ds(pl.multiple_of(i * tb, tb), tb)
 
@@ -369,7 +390,7 @@
         hidden = x_ref[rows, :].astype(F32) + nn(ctx, wo_ref[...]) + nn(gated_o, bo_ref[...])
         h1[rows, :] = hidden
         norm = (
-            hidden * lax.rsqrt(jnp.mean(hidden * hidden, axis=1, keepdims=True) + EPS) * g2_ref[...]
+            hidden * lax.rsqrt(jnp.mean(hidden * hidden, axis=1, keepdims=True) + EPS) * g2_ref[...].reshape(1, x_ref.shape[1])
         ).astype(BF16)
         n2[rows, :] = norm
         li = nt(norm, ain_ref[...])
@@ -425,24 +446,11 @@
             dn2[rows, :] += dn
             d_low_in[rows, :] += dl
 
-        @pl.when(i == 0)
-        def _():
-            gaout_ref[k] = ga
-            gbin_ref[k] = gb
-
-        @pl.when(i > 0)
-        def _():
-            gaout_ref[k] += ga
-            gbin_ref[k] += gb
-
+        part_ref[k, :cols] += ga[:cols]
+        part_ref[k, 2 * cols : 3 * cols] += gb[:cols]
         return c
 
     lax.fori_loop(0, groups * blocks, chunk, 0)
-
-    gbout_ref[...] = jnp.zeros_like(gbout_ref)
-    gbo_ref[...] = jnp.zeros_like(gbo_ref)
-    gao_ref[...] = jnp.zeros_like(gao_ref)
-    gain_ref[...] = jnp.zeros_like(gain_ref)
 
     def last(i, c):
         rows = rows_of(i)
@@ -455,10 +463,10 @@
         dgi = dli * gate
         dn = dn2[rows, :] + nn(dgi.astype(BF16), ain_ref[...])
         both = jnp.concatenate([go, dgi], axis=1).T.astype(BF16)
-        gbout_ref[...] += nn(both[:PAD], cot)
-        gain_ref[...] += nn(both[PAD:], n2[rows, :])
+        part_ref[2, cols : 2 * cols] += nn(both[:PAD], cot)[:cols]
+        part_ref[3, cols : 2 * cols] += nn(both[PAD:], n2[rows, :])[:cols]
         inv = lax.rsqrt(jnp.mean(hidden * hidden, axis=1, keepdims=True) + EPS)
-        up = dn * g2_ref[...]
+        up = dn * g2_ref[...].reshape(1, x_ref.shape[1])
         dh = (
             cot.astype(F32)
             + inv * up
@@ -471,8 +479,8 @@
         dg = dlo * gate
         dgb = dg.astype(BF16)
         both = jnp.concatenate([lo * gate, dg], axis=1).T.astype(BF16)
-        gbo_ref[...] += nn(both[:PAD], da)
-        gao_ref[...] += nt(both[PAD:], ctx_ref[:, rows])
+        part_ref[1, cols : 2 * cols] += nn(both[:PAD], da)[:cols]
+        part_ref[0, cols : 2 * cols] += nt(both[PAD:], ctx_ref[:, rows])[:cols]
         dctx_ref[:, rows] = (nt(wo_ref[...], da) + tn(ao_ref[...], both[PAD:])).astype(BF16)
         z = dlo * lo + dli * low_in[rows, :] + d_low_out[rows, :] * low_out[rows, :]
         z_ref[:, rows] = jnp.concatenate([z, z], axis=1).T[:PAD]
@@ -487,10 +495,91 @@
 
 def attention_backward(
     x_ref, g1_ref, wsm_ref, wqkv_ref, bqkv_ref, n1_ref, low_ref, gate_ref, gated_ref, qkv_ref, e_ref, r_ref,
-    ctx_ref, dctx_ref, z_ref, dh_ref, sum_ref,
-    gx_ref, gsm_ref, gbqkv_ref,
-    dqkv, dlow, dn1, dsmall,
+    ctx_ref, dctx_ref, z_ref, dh_ref, part_ref,
+    gx_ref, grouter_ref, gin_ref, gao_ref, gaout_ref, gbqkv_out, gbo_ref, gbin_ref, gbout_ref,
+    dqkv, dlow, dn1, dsmall, gsm_ref, gbqkv_ref,
+    core_out, core_in, y_out, y_in, x_out, x_in, held, z_all, full,
+    small_out, small_in, small_z, small_full, b_out, b_in, b_z, b_full, send, recv,
 ):
+    places = Places()
+    t, d, half = places.t, places.d, places.half
+    zs = z_all.shape[0]
+    z = d // 2
+    z_peers = [((z + i) % zs, ((z + i) % zs * 2 + half, t)) for i in range(1, zs)]
+    tens = [(flip(t, 1), places.core), (places.y_group, places.y), (flip(places.y_group, 1), places.across)]
+    block_peers = [(half * 4 + j, dev) for j, dev in tens]
+    block_peers += [((1 - half) * 4 + j, (flip(d, 1), dev[1])) for j, dev in tens]
+    block_peers += [((1 - half) * 4 + t, places.x)]
+    me = half * 4 + t
+    greet([dev for _, dev in block_peers] + [dev for _, dev in z_peers])
+    links = Links(send, recv)
+    partner, y_group, far_group = flip(t, 1), places.y_group, flip(places.y_group, 1)
+    rows_half = x_out.shape[0]
+    mine = pl.ds(pl.multiple_of(half * rows_half, rows_half), rows_half)
+    other = pl.ds(pl.multiple_of((1 - half) * rows_half, rows_half), rows_half)
+    shared = 2 * gao_ref.shape[0]
+    cols = gao_ref.shape[0]
+    to_core = links(core_out, core_in, places.core)
+    to_y = links(y_out, y_in, places.y)
+    to_x = links(x_out, x_in, places.x)
+    to_z = [links(z_all.at[z], z_all.at[z], dev) for _, dev in z_peers]
+    all_x = links(full.at[t, mine], full.at[t, mine], places.x)
+    all_y = links(full.at[t, :shared], full.at[t, :shared], places.y)
+    all_core = [
+        links(full.at[t, :shared], full.at[t, :shared], places.core),
+        links(full.at[y_group, :shared], full.at[y_group, :shared], places.core),
+    ]
+    share = small_in.shape[1]
+    b_share = b_in.shape[1]
+    give = []
+    for j, dev in block_peers:
+        there = pl.ds(pl.multiple_of(j * share, 16), share)
+        there_b = pl.ds(pl.multiple_of((j // 4) * b_share, 16), b_share)
+        give.append(links(small_out.at[there], small_in.at[me], dev))
+        give.append(links(b_out.at[j % 4, there_b], b_in.at[me], dev))
+    cross = []
+    for _, dev in z_peers:
+        cross.append(links(small_z.at[z], small_z.at[z], dev))
+        cross.append(links(b_z.at[z], b_z.at[z], dev))
+    back = [links(small_full.at[me], small_full.at[me], dev) for _, dev in block_peers]
+    back.append(links(b_full.at[half], b_full.at[half], places.x))
+
+    def at_step(step):
+        if step == 0:
+            core_out[0] = part_ref[partner].astype(BF16)
+            core_out[1] = part_ref[far_group].astype(BF16)
+            to_core.start()
+        if step == 1:
+            to_core.wait_recv()
+            y_out[...] = (part_ref[y_group] + core_in[1].astype(F32)).astype(BF16)
+            to_y.start()
+            held[...] = part_ref[t] + core_in[0].astype(F32)
+        if step == 3:
+            to_y.wait_recv()
+            held[...] += y_in[...].astype(F32)
+            x_out[...] = held[other, :].astype(BF16)
+            to_x.start()
+        if step == 5:
+            to_x.wait_recv()
+            z_all[z] = (held[mine, :] + x_in[...].astype(F32)).astype(BF16)
+            for copy in to_z:
+                copy.start()
+        if step == 8:
+            for copy in to_z:
+                copy.wait_recv()
+            total = z_all[0].astype(F32)
+            for i in range(1, zs):
+                total = total + z_all[i].astype(F32)
+            full[t, mine] = total.astype(BF16)
+            all_x.start()
+        if step == 9:
+            all_x.wait_recv()
+            all_y.start()
+            all_core[0].start()
+        if step == 11:
+            all_y.wait_recv()
+            all_core[1].start()
+
     tokens = x_ref.shape[0]
     groups = wqkv_ref.shape[0]
     inner = wqkv_ref.shape[1] // 3
@@ -500,13 +589,13 @@
     hd = inner // heads_here
     qb = 256
 
-    t = lax.axis_index("tensor")
-
     def group(n, c):
         g = group_at(t, n)
 
         def head(h, c):
             gh = n * heads_here + h
+            for point in (0, 1, 3, 5, 8, 9, 11):
+                pl.when(gh == point)(lambda point=point: at_step(point))
             feats = pl.ds(pl.multiple_of(h * hd, hd), hd)
             full = pl.ds(pl.multiple_of(g * inner + h * hd, hd), hd)
             for s in range(seqs):
@@ -558,20 +647,38 @@
 
     lax.fori_loop(0, groups, group, 0)
     gate = gate_ref[...]
-    z = z_ref[...]
+    prod = z_ref[...]
     for p in range(3):
         part = slice(p * PAD, (p + 1) * PAD)
-        z = z + dlow[part, :] * low_ref[part, :]
+        prod = prod + dlow[part, :] * low_ref[part, :]
         dsmall[part, :] = (dlow[part, :] * gate).astype(BF16)
-    zh = z.astype(BF16)
-    zl = (z - zh.astype(F32)).astype(BF16)
-    dgate = nn(sum_ref[...], zh) + nn(sum_ref[...], zl)
-    total = jnp.sum(gate * z, axis=0, keepdims=True)
+    high = prod.astype(BF16)
+    low = (prod - high.astype(F32)).astype(BF16)
+    same = lax.broadcasted_iota(jnp.int32, (PAD, PAD), 0) // 4 == lax.broadcasted_iota(jnp.int32, (PAD, PAD), 1) // 4
+    same = jnp.logical_and(same, lax.broadcasted_iota(jnp.int32, (PAD, PAD), 1) < cols).astype(F32).astype(BF16)
+    dgate = nn(same, high) + nn(same, low)
+    total = jnp.sum(gate * prod, axis=0, keepdims=True)
     dlogit = gate * (dgate - total)
     row = lax.broadcasted_iota(jnp.int32, dlogit.shape, 0)
     keep = jnp.logical_and(row % 4 == 0, row < 40)
     dsmall[3 * PAD :, :] = jnp.where(keep, dlogit, 0.0).astype(BF16)
     gsm_ref[...] = nn(dsmall[...], n1_ref[...])
+    lines = [gsm_ref[p * PAD : p * PAD + cols, :] for p in range(3)]
+    lines.append(jnp.concatenate([gsm_ref[3 * PAD + 4 * e : 3 * PAD + 4 * e + 1, :] for e in range(16)], axis=0))
+    count = 3 * cols + 16
+    tall = -(-count // 16) * 16
+    lines.append(jnp.zeros((tall - count, gsm_ref.shape[1]), F32))
+    lines = jnp.concatenate(lines, axis=0).astype(BF16)
+    wide = gsm_ref.shape[1] // 128
+    for i in range(wide):
+        small_out[i * tall : (i + 1) * tall, :] = lines[:, i * 128 : (i + 1) * 128]
+    small_out[wide * tall :, :] = jnp.zeros((small_out.shape[0] - wide * tall, 128), BF16)
+    for j in range(groups):
+        block = [gbqkv_ref[j, p, :cols] for p in range(3)]
+        block.append(jnp.zeros((b_out.shape[1] - 3 * cols, inner), F32))
+        b_out[j] = jnp.concatenate(block, axis=0).astype(BF16)
+    for copy in give:
+        copy.start()
 
     tb = 256
 
@@ -580,13 +687,60 @@
         dn = (dn1[:, rows] + tn(wsm_ref[...], dsmall[:, rows])).T
         x = x_ref[rows, :].astype(F32)
         inv = lax.rsqrt(jnp.mean(x * x, axis=1, keepdims=True) + EPS)
-        up = dn * g1_ref[...]
+        up = dn * g1_ref[...].reshape(1, x_ref.shape[1])
         gx_ref[rows, :] = (
             dh_ref[rows, :] + inv * up - x * (inv * inv * inv) * jnp.mean(x * up, axis=1, keepdims=True)
         )
         return c
 
-    lax.fori_loop(0, tokens // tb, finish, 0)
+    lax.fori_loop(0, tokens // tb // 2, finish, 0)
+    for copy in give:
+        copy.wait_recv()
+    small_in[me] = small_out[pl.ds(pl.multiple_of(me * share, 16), share), :]
+    b_in[me] = b_out[t, pl.ds(pl.multiple_of(half * b_share, 16), b_share), :]
+    total = small_in[0].astype(F32)
+    total_b = b_in[0].astype(F32)
+    for i in range(1, 8):
+        total = total + small_in[i].astype(F32)
+        total_b = total_b + b_in[i].astype(F32)
+    small_z[z] = total.astype(BF16)
+    b_z[z] = total_b.astype(BF16)
+    for copy in cross:
+        copy.start()
+    lax.fori_loop(tokens // tb // 2, tokens // tb, finish, 0)
+    for copy in cross:
+        copy.wait_recv()
+    total = small_z[0].astype(F32)
+    total_b = b_z[0].astype(F32)
+    for i in range(1, zs):
+        total = total + small_z[i].astype(F32)
+        total_b = total_b + b_z[i].astype(F32)
+    small_full[me] = total.astype(BF16)
+    b_full[half] = total_b.astype(BF16)
+    for copy in back:
+        copy.start()
+    for copy in all_core:
+        copy.wait_recv()
+    gbin_ref[...] = full[t].astype(F32)[2 * cols : 3 * cols]
+    hidden = gaout_ref.shape[1] // groups
+    for j in range(groups):
+        block = full[j].astype(F32)
+        gaout_ref[:, j * hidden : (j + 1) * hidden] = block[:cols]
+        target = (gao_ref, gbo_ref, gbout_ref, gin_ref.at[3])[j]
+        target[...] = block[cols : 2 * cols]
+    for copy in back:
+        copy.wait_recv()
+    flat = small_full[...].reshape(8 * share, 128)
+    for i in range(wide):
+        block = flat[i * tall : (i + 1) * tall].astype(F32)
+        for p in range(3):
+            gin_ref[p, :, i * 128 : (i + 1) * 128] = block[p * cols : (p + 1) * cols]
+        grouter_ref[:, i * 128 : (i + 1) * 128] = block[3 * cols : 3 * cols + grouter_ref.shape[0]]
+    block = b_full[...].reshape(2 * b_share, inner).astype(F32)
+    for p in range(3):
+        gbqkv_out[p] = block[p * cols : (p + 1) * cols]
+    for copy in [to_core, to_y, to_x, *to_z, all_x, all_y, *all_core, *give, *cross, *back]:
+        copy.wait_send()
 
 
 ANY = "any"
@@ -609,17 +763,11 @@
     )(*args)
 
 
-def pad_rows(a):
-    width = [(0, 0)] * (a.ndim - 2) + [(0, PAD - a.shape[-2]), (0, 0)]
-    return jnp.pad(a, width)
-
-
 def shards(
     layer_inputs, lengths, first_gain, second_gain, router, wqkv, bias_table, wo, win, wout,
     a_in, a_o, a_out, b_qkv, b_o, b_in, b_out, cotangent,
 ):
     groups = lax.axis_size("tensor")
-    member = lax.axis_index("tensor")
     seqs, seq, width = layer_inputs.shape
     tokens = seqs * seq
     inner = wo.shape[0]
@@ -629,27 +777,15 @@
     hidden = win.shape[1]
     experts = router.shape[1]
     cols = a_in.shape[2]
-    rank = cols // experts
 
     x = layer_inputs.reshape(tokens, width)
     cot = cotangent.reshape(tokens, width)
-    g1 = first_gain.reshape(1, width)
-    g2 = second_gain.reshape(1, width)
     at = jnp.swapaxes(a_in, 1, 2)
-    rrep = jnp.repeat(router.T, rank, axis=0)
-    wsm = pad_rows(jnp.concatenate([at[:3], rrep[None]], axis=0)).reshape(4 * PAD, width)
     wqkv_own = jnp.swapaxes(wqkv, 1, 2).reshape(3 * inner, width)
-    bqkv_own = pad_rows(b_qkv).reshape(3 * PAD, inner)
-    rb_own = jnp.pad(bias_table.T, ((0, 16 - heads_here), (0, 0)))
-    bin_own = pad_rows(b_in)
-    ao = pad_rows(a_o.T)
-    ain = pad_rows(at[3])
-    aout = pad_rows(jnp.swapaxes(a_out.T.reshape(cols, groups, hidden), 0, 1))
-    bo = pad_rows(b_o)
-    bout = pad_rows(b_out)
     onehot = jnp.asarray(bucket_lines(seq), BF16)
-
-    n1, low, gate, gate_t, gated, qkv, e, r, ctx, wqkv_all, bqkv_all, wo_all, win_all, bin_all = call(
+    zs = lax.axis_size("dp") // 2
+
+    n1, low, gate, gate_t, gated, qkv, e, r, ctx, wqkv_all, bqkv_all, wo_all, win_all, bin_all, wsm = call(
         attention_forward,
         "attention_forward",
         [
@@ -666,24 +802,24 @@
             ((groups, 3 * PAD, inner), BF16),
             ((groups, inner, width), BF16, ANY),
             ((groups, width, hidden), BF16, ANY),
-            ((groups, PAD, hidden), BF16, ANY),
+            ((groups, PAD, hidden), BF16),
+            ((4 * PAD, width), BF16),
         ],
         [
             ((groups, 3 * inner, width), BF16),
-            ((groups, 3 * PAD, inner), BF16),
             ((groups, 16, NB), BF16),
             ((heads_here, 1, 2 * seq), F32),
             ((128, 2 * seq - 128), F32),
             (SEM, 32),
             (SEM, 32),
-            (SEM, 10),
+            (SEM, 7),
         ],
-        (lengths, x, g1, wsm, onehot, wqkv_own, bqkv_own, rb_own, wo, win, bin_own),
-        "svvvvaaaaaa",
+        (lengths, x, first_gain, at, router.T, onehot, b_qkv, bias_table.T, b_in, wqkv_own, wo, win),
+        "s" + "v" * 8 + "aaa",
         collective=0,
     )
     wo_all = wo_all.reshape(groups * inner, width)
-    y, dh, dctx, z, gao, gaout, gbo, gbin, gbout, gain = call(
+    y, dh, dctx, z, part = call(
         feed_forward,
         "feed_forward",
         [
@@ -691,12 +827,7 @@
             ((tokens, width), F32),
             ((groups * inner, tokens), BF16),
             ((PAD, tokens), F32),
-            ((PAD, groups * inner), F32),
-            ((groups, PAD, hidden), F32),
-            ((PAD, width), F32),
-            ((groups, PAD, hidden), F32),
-            ((PAD, width), F32),
-            ((PAD, width), F32),
+            ((groups, 128, width), F32),
         ],
         [
             ((tokens, width), F32),
@@ -714,50 +845,77 @@
             ((tokens, PAD), F32),
             ((groups, width, hidden), BF16),
             ((groups, hidden, width), BF16),
+            ((PAD, width), BF16),
+            ((PAD, width), BF16),
+            ((PAD, width), BF16),
+            ((groups, PAD, hidden), BF16),
+            ((PAD, width), BF16),
             (SEM, 16),
             (SEM, 16),
             (SEM, 5),
         ],
-        (x, cot, g2, ctx, gate_t, wo_all, ao, bo, ain, bin_all, aout, bout, win_all, wout),
+        (x, cot, second_gain, ctx, gate_t, wo_all, a_o.T, b_o, at, bin_all, a_out.T, b_out, win_all, wout),
         "v" * 12 + "aa",
         collective=1,
     )
-    c = np.arange(PAD)
-    same = (c[:, None] // rank == c[None, :] // rank) & (c[None, :] < cols)
-    gx, gsm, gbqkv = call(
+    copies = 7 + 3 * (zs - 1) + 22
+    outs = call(
         attention_backward,
         "attention_backward",
         [
             ((tokens, width), F32),
-            ((4 * PAD, width), F32),
-            ((groups, 3, PAD, inner), F32),
+            ((experts, width), F32),
+            ((4, cols, width), F32),
+            ((cols, width), F32),
+            ((cols, groups * hidden), F32),
+            ((3, cols, inner), F32),
+            ((cols, width), F32),
+            ((cols, hidden), F32),
+            ((cols, width), F32),
         ],
         [
             ((3 * inner, tokens), BF16),
             ((3 * PAD, tokens), F32),
             ((width, tokens), F32),
             ((4 * PAD, tokens), BF16),
+            ((4 * PAD, width), F32),
+            ((groups, 3, PAD, inner), F32),
+            ((2, 128, width), BF16),
+            ((2, 128, width), BF16),
+            ((128, width), BF16),
+            ((128, width), BF16),
+            ((64, width), BF16),
+            ((64, width), BF16),
+            ((128, width), F32),
+            ((zs, 64, width), BF16),
+            ((groups, 128, width), BF16),
+            ((896, 128), BF16),
+            ((8, 112, 128), BF16),
+            ((zs, 112, 128), BF16),
+            ((8, 112, 128), BF16),
+            ((groups, 128, inner), BF16),
+            ((8, 64, inner), BF16),
+            ((zs, 64, inner), BF16),
+            ((2, 64, inner), BF16),
+            (SEM, copies),
+            (SEM, copies),
         ],
-        (x, g1, wsm, wqkv_all, bqkv_all, n1, low, gate, gated, qkv, e, r, ctx, dctx, z, dh, jnp.asarray(same, BF16)),
+        (x, first_gain, wsm, wqkv_all, bqkv_all, n1, low, gate, gated, qkv, e, r, ctx, dctx, z, dh, part),
         "v" * 17,
+        collective=2,
     )
-    g_in = jnp.concatenate([gsm.reshape(4, PAD, width)[:3, :cols], gain[None, :cols]], axis=0)
-    g_router = gsm.reshape(4, PAD, width)[3, :cols:rank]
-    summed = lax.psum(
-        (g_router, g_in, gao[:cols], gaout[:, :cols], gbqkv[:, :, :cols], gbo[:cols], gbin[:, :cols], gbout[:cols]),
-        ("dp", "tensor"),
-    )
+    gx, g_router, g_in, g_ao, g_aout, g_bqkv, g_bo, g_bin, g_bout = outs
     return (
         y.reshape(layer_inputs.shape),
         gx.reshape(layer_inputs.shape),
-        summed[0].T,
-        jnp.swapaxes(summed[1], 1, 2),
-        summed[2].T,
-        jnp.swapaxes(summed[3], 0, 1).reshape(cols, groups * hidden).T,
-        lax.dynamic_index_in_dim(summed[4], member, 0, keepdims=False),
-        summed[5],
-        lax.dynamic_index_in_dim(summed[6], member, 0, keepdims=False),
-        summed[7],
+        g_router.T,
+        jnp.swapaxes(g_in, 1, 2),
+        g_ao.T,
+        g_aout.T,
+        g_bqkv,
+        g_bo,
+        g_bin,
+        g_bout,
     )
 
 

time: 351 us -> 196 us (0.56)
  waiting for transfers between devices: 97.2 us -> 0 us
  blocking collectives: 40.8 us -> 0 us
  local copies, waits for them, and re-layouts: 28.7 us -> 9.57 us
  Pallas kernels: 168 us -> 186 us
  between operations: 14.2 us -> 0.72 us
    psum x1 -> x0, waiting for transfers between devices: 97.1 us -> none  [shards(): lax.psum((g_router, g_in, gao[:cols], gaout[:, :cols], gbqkv[:, :, :cols]...]
    psum x1 -> x0, blocking collectives: 40.8 us -> none  [shards(): lax.psum((g_router, g_in, gao[:cols], gaout[:, :cols], gbqkv[:, :, :cols]...]
    pallas_call x3, Pallas kernels: 168 us -> 186 us  [call(): pl.pallas_call(body, name=name, out_shape=[jax.ShapeDtypeStruct(o[0], o[1...]
    pad x8 -> x0, local copies, waits for them, and re-layouts: 7.6 us -> none  [the longest x7 6.32 us: pad_rows(): return jnp.pad(a, width)]
    slice x7 -> x0, local copies, waits for them, and re-layouts: 7.14 us -> none  [the longest x1 1.92 us: shards(): gbqkv[:, :, :cols]]
    unnamed x39 -> x30, local copies, waits for them, and re-layouts: 4.9 us -> 9.57 us
    squeeze x3 -> x0, local copies, waits for them, and re-layouts: 3.95 us -> none  [the longest x1 1.56 us: shards(): lax.dynamic_index_in_dim(summed[6], member, 0, keepdims=False)]
    reshape x4 -> x0, local copies, waits for them, and re-layouts: 3.63 us -> none  [the longest x1 1.27 us: shards(): g1 = first_gain.reshape(1, width)]
  transfers between devices with their start and end apart: 1 -> 0, of which waited for: 1 -> 0; matrix products, arithmetic and copies ran while one was open for 0% -> 0% of each run, Pallas kernels for 0% -> 0%
where the time goes in v3:
time: 196 us
  Pallas kernels  186 us (95%)
  local copies, waits for them, and re-layouts  9.57 us (5%)
    pallas_call x3, Pallas kernels, call(): pl.pallas_call(body, name=name, out_shape=[jax.ShapeDtypeStruct(o[0], o[1...  186 us
    unnamed x30, local copies, waits for them, and re-layouts  9.57 us

profile of v3, /device:TPU:0, one launch (start us, length us, event | category | flops | bytes accessed | tf_op | source)
XLA Modules:
  0.0 196.1 jit_solution(4014514498218522134)
XLA Ops:
  0.6 58.9 %attention_forward.1 = (bf16[1024,768]{1,0:T(8,128)(2,1)}, f32[192,1024]{1,0:T(8,128)}, f32[64,1024]{1,0:T(8,128)}, f32[1024,128]{1,0:T(8,128)}, bf16[192,1024]{...) custom-call(s32[2]{0:T(128)} %lens.1, ...), custom_call_target="tpu_custom_call" | custom-call | tf_op jit(solution)/shard_map/attention_forward/pallas_call | solution.py:755
  59.6 56.5 %feed_forward.1 = (bf16[1024,768]{1,0:T(8,128)(2,1)}, f32[1024,768]{1,0:T(8,128)}, bf16[768,1024]{1,0:T(8,128)(2,1)}, f32[64,1024]{1,0:T(8,128)}, f32[4,128,768]{2,1,0:T(8,128)}) custom-call(bf16[1024,768]{1,0:T(8,128)(2,1)} %bitcast.18, bf16[1024,768]{1,0:T(8,128)(2,1)} %bitcast.22, f32[768]{0:T(1024)} %g2_ref.1, ...), custom_call_target="tpu_custom_call" | custom-call | tf_op jit(solution)/shard_map/feed_forward/pallas_call | solution.py:755
  116.1 0.0 copy-start.1
  116.1 70.4 %attention_backward.1 = (f32[1024,768]{1,0:T(8,128)}, f32[10,768]{1,0:T(8,128)}, f32[4,40,768]{2,1,0:T(8,128)}, f32[40,768]{1,0:T(8,128)}, f32[40,3072]{1,0:T(8,...) custom-call(bf16[1024,768]{1,0:T(8,128)(2,1)} %bitcast.19, ...), custom_call_target="tpu_custom_call" | custom-call | tf_op jit(solution)/shard_map/attention_backward/pallas_call | solution.py:755
  186.5 0.0 copy-done.1
  186.5 0.0 copy-start
  186.5 1.1 copy.39
  187.7 1.3 copy-done
  189.0 0.0 copy-start.9
  189.0 0.0 copy-start.3
  189.0 0.0 copy-start.8
  189.0 1.7 copy.40
  190.6 0.0 copy-done.9
  190.6 0.0 copy-start.2
  190.6 0.0 copy-start.7
  190.6 0.0 copy-start.6
  190.7 0.0 copy-start.5
  190.7 0.0 copy-start.4
  190.7 0.6 copy.41
  191.3 0.0 copy-done.3
  191.3 0.8 copy.42
  192.1 0.0 copy-done.8
  192.1 0.6 copy.43
  192.7 0.0 copy-done.2
  192.7 0.8 copy.44
  193.5 0.0 copy-done.7
  193.5 0.6 copy.45
  194.2 0.0 copy-done.6
  194.2 0.6 copy.46
  194.8 0.0 copy-done.5
  194.8 0.6 copy.47
  195.5 0.0 copy-done.4
  195.5 0.6 copy.48
Async XLA Ops:
  116.1 70.4 %copy-start.1 = (bf16[1024,768]{1,0:T(8,128)(2,1)S(1)}, bf16[1024,768]{1,0:T(8,128)(2,1)}, u32[]{:S(2)}) copy-start(bf16[1024,768]{1,0:T(8,128)(2,1)} %get-tuple-element.44) | copy-start | bytes 4718596
  186.5 2.5 %copy-start = (f32[1024,768]{1,0:T(8,128)S(1)}, f32[1024,768]{1,0:T(8,128)}, u32[]{:S(2)}) copy-start(f32[1024,768]{1,0:T(8,128)} %get-tuple-element.59) | copy-start | bytes 9437188
  189.0 1.7 copy-start.9
  189.0 2.3 %copy-start.3 = (f32[4,40,768]{2,1,0:T(8,128)S(1)}, f32[4,40,768]{2,1,0:T(8,128)}, u32[]{:S(2)}) copy-start(f32[4,40,768]{2,1,0:T(8,128)} %get-tuple-element.61) | copy-start | bytes 1474564
  189.0 3.1 %copy-start.8 = (f32[40,768]{1,0:T(8,128)S(1)}, f32[40,768]{1,0:T(8,128)}, u32[]{:S(2)}) copy-start(f32[40,768]{1,0:T(8,128)} %get-tuple-element.62) | copy-start | bytes 368644
  190.6 2.1 %copy-start.2 = (f32[40,3072]{1,0:T(8,128)S(1)}, f32[40,3072]{1,0:T(8,128)}, u32[]{:S(2)}) copy-start(f32[40,3072]{1,0:T(8,128)} %get-tuple-element.63) | copy-start | bytes 1474564
  190.6 2.9 %copy-start.7 = (f32[3,40,192]{2,1,0:T(8,128)S(1)}, f32[3,40,192]{2,1,0:T(8,128)}, u32[]{:S(2)}) copy-start(f32[3,40,192]{2,1,0:T(8,128)} %get-tuple-element.84) | copy-start | bytes 276484
  190.6 3.5 %copy-start.6 = (f32[40,768]{1,0:T(8,128)S(1)}, f32[40,768]{1,0:T(8,128)}, u32[]{:S(2)}) copy-start(f32[40,768]{1,0:T(8,128)} %get-tuple-element.85) | copy-start | bytes 368644
  190.7 4.2 %copy-start.5 = (f32[40,768]{1,0:T(8,128)S(1)}, f32[40,768]{1,0:T(8,128)}, u32[]{:S(2)}) copy-start(f32[40,768]{1,0:T(8,128)} %get-tuple-element.86) | copy-start | bytes 368644
  190.7 4.8 %copy-start.4 = (f32[40,768]{1,0:T(8,128)S(1)}, f32[40,768]{1,0:T(8,128)}, u32[]{:S(2)}) copy-start(f32[40,768]{1,0:T(8,128)} %get-tuple-element.87) | copy-start | bytes 368644

commit v4 on v1

v4 whole, which is shorter than its diff:
```python
import jax
import jax.numpy as jnp
import numpy as np
from jax import lax
from jax.experimental import pallas as pl
from jax.experimental.pallas import tpu as pltpu
from jax.sharding import PartitionSpec as P

NB = 32
MAX_DIST = 128
EPS = 1e-06
NEG = -1000000000.0
LOG2E = 1.4426950408889634
F32 = jnp.float32
BF16 = jnp.bfloat16
PAD = 64
RANK_PAD = 48
VMEM_LIMIT = 63 * 1024 * 1024
MESH = pl.DeviceIdType.MESH


def filled(a, rows):
    wide = jnp.concatenate([a.astype(F32), jnp.zeros((rows - a.shape[0], a.shape[1]), F32)], axis=0)
    return wide.astype(a.dtype)


def nn(a, b):
    return lax.dot_general(a, b, (((1,), (0,)), ((), ())), preferred_element_type=F32)


def nt(a, b):
    return lax.dot_general(a, b, (((1,), (1,)), ((), ())), preferred_element_type=F32)


def tn(a, b):
    return lax.dot_general(a, b, (((0,), (0,)), ((), ())), preferred_element_type=F32)


def ds(start, size):
    return pl.ds(pl.multiple_of(start, 16), size)


def flip(index, bit):
    return index + (1 - 2 * ((index // bit) % 2)) * bit


def group_at(member, step):
    high = (member // 2 + step // 2) % 2
    low = (member % 2 + step % 2) % 2
    return 2 * high + low


class Links:
    def __init__(self, send, recv):
        self.send, self.recv, self.made = send, recv, []

    def __call__(self, src, dst, device):
        n = len(self.made)
        copy = pltpu.make_async_remote_copy(
            src_ref=src, dst_ref=dst, send_sem=self.send.at[n], recv_sem=self.recv.at[n],
            device_id=device, device_id_type=MESH,
        )
        self.made.append(copy)
        return copy


class Places:
    def __init__(self):
        d, t = lax.axis_index("dp"), lax.axis_index("tensor")
        self.d, self.t = d, t
        self.half = d % 2
        self.quarter = d % 4
        self.core_t, self.y_t = flip(t, 1), flip(t, 2)
        self.far_t = flip(self.core_t, 2)
        self.core = (d, self.core_t)
        self.y = (d, self.y_t)
        self.across = (d, self.far_t)
        self.x = (flip(d, 1), t)
        self.z = (flip(d, 2), t)


class Chunk:
    def __init__(self, links, places, own, whole, first, base, rows, over_x):
        part = rows // 4
        q = places.quarter
        qx, qz = flip(q, 1), flip(q, 2)
        qd = flip(qx, 2)
        g, g2 = places.t, places.y_t

        def at(group, quarter):
            return whole.at[ds(first(group) + base + quarter * part, part)]

        def pass_on(quarter, device):
            return links(at(g2, quarter), at(g2, quarter), device)

        self.y = links(own.at[ds(base + q * part, part)], at(g, q), places.y)
        self.one = [pass_on(q, places.x), pass_on(q, places.z), pass_on(q, places.core)]
        self.two = [pass_on(qz, places.x) if over_x else pass_on(qx, places.z)]
        self.two += [pass_on(qx, places.core), pass_on(qz, places.core)]
        self.three = pass_on(qd, places.core)

    def start(self):
        self.y.start()

    def relay(self):
        self.y.wait_recv()
        for copy in self.one:
            copy.start()

    def forward(self):
        self.one[0].wait_recv()
        self.one[1].wait_recv()
        for copy in self.two:
            copy.start()

    def close(self):
        self.two[0].wait_recv()
        self.three.start()

    def whole_here(self):
        for copy in (self.one[2], self.two[1], self.two[2], self.three):
            copy.wait_recv()


def bucket_of(relative):
    half = NB // 2
    exact = half // 2
    distance = np.abs(relative)
    scaled = np.log(np.maximum(distance, 1) / exact) / np.log(MAX_DIST / exact) * (half - exact)
    far = np.minimum(exact + scaled.astype(np.int32), half - 1)
    return ((relative > 0) * half + np.where(distance < exact, distance, far)).astype(np.int32)


def bucket_lines(seq):
    m = np.arange(2 * seq)
    rel = seq - 128 - m
    rel = np.where(rel < -seq, rel + 2 * seq, rel)
    rel = np.clip(rel, -(seq - 1), seq - 1)
    ids = bucket_of(rel)
    return (ids[None, :] == np.arange(NB)[:, None]).astype(np.float32)


class Names:
    def __init__(self, **refs):
        self.__dict__.update(refs)


def layer(names, sizes, *refs):
    r = Names(**dict(zip(names, refs)))
    tokens, width, seq, seqs, groups, inner, heads_here, hd, hidden, cols, experts, zs = sizes
    heads = groups * heads_here
    span = 3 * hd
    rank = cols // experts
    places = Places()
    t, d, half = places.t, places.d, places.half
    z = d // 2
    links = Links(r.send, r.recv)

    def gb_rows(g, p):
        return ds(4 * PAD + (g * 3 + p) * PAD, PAD)

    r.zed = r.low_in
    r.dsmall = r.dctx.at[: 4 * PAD]
    r.d_low = [r.low_out, r.d_low_in, r.d_low_out]
    r.core_out = [r.cot.at[:128], r.cot.at[128:256]]
    r.y_out, r.x_out, r.z_out = r.cot.at[256:384], r.cot.at[384:448], r.cot.at[448:512]
    batch = min(zs, 4)
    r.z_in = r.cot.at[512 : 512 + 64 * batch]

    local = [0]

    def here(src, dst):
        local[0] += 1
        return pltpu.make_async_copy(src, dst, r.local.at[local[0] - 1])

    get_x = here(r.x, r.xy)
    get_c = here(r.c, r.cot)
    get_qkv = [
        here(
            r.wqkv_own.at[p, h * hd : (h + 1) * hd],
            r.wqkv.at[ds(t * heads_here * span + h * span + p * hd, hd)],
        )
        for h in range(heads_here)
        for p in range(3)
    ]
    get_x.start()
    for copy in get_qkv:
        copy.start()

    z_peers = [((z + i) % zs * 2 + half, t) for i in range(1, zs)]
    same_x = [(half * 4 + j, (d, j)) for j in (places.core_t, places.y_t, places.far_t)]
    other_x = [((1 - half) * 4 + j, (flip(d, 1), j)) for j in (places.core_t, places.y_t, places.far_t, t)]
    block_peers = same_x + other_x
    barrier = pltpu.get_barrier_semaphore()
    known = [dev for _, dev in block_peers] + z_peers
    for dev in known:
        pl.semaphore_signal(barrier, inc=1, device_id=dev, device_id_type=MESH)

    def quarter_of(ref, g, rows):
        return ref.at[ds(g * rows, rows)]

    def qkv_row(g):
        return g * heads_here * span

    qkv_chunks = [
        Chunk(links, places, quarter_of(r.wqkv, t, heads_here * span), r.wqkv, qkv_row, h * span, span, h % 2 == 0)
        for h in range(heads_here)
    ]
    o_chunk = Chunk(links, places, r.wo_own, r.wo, lambda g: g * inner, 0, inner, False)
    in_chunks = [
        Chunk(links, places, r.win_own, r.win_all, lambda g: g * width, j * width // 2, width // 2, j == 0)
        for j in range(2)
    ]
    out_chunks = [
        Chunk(links, places, r.wout_own, r.wout, lambda g: g * hidden, j * hidden // 2, hidden // 2, j == 1)
        for j in range(2)
    ]

    own_qkv = quarter_of(r.wqkv, t, heads_here * span)
    core_qkv = links(own_qkv, own_qkv, places.core)
    core_o = links(r.wo_own, quarter_of(r.wo, t, inner), places.core)
    core_in = links(r.win_own, quarter_of(r.win_all, t, width), places.core)
    core_out = links(r.wout_own, quarter_of(r.wout, t, hidden), places.core)
    small = [r.bq, r.rb, r.bin]
    small_y = [links(a.at[t], a.at[t], places.y) for a in small]
    small_core = [links(a.at[t], a.at[t], places.core) for a in small]
    small_far = [links(a.at[places.y_t], a.at[places.y_t], places.core) for a in small]
    keep = [
        here(r.wo_own, quarter_of(r.wo, t, inner)),
        here(r.win_own, quarter_of(r.win_all, t, width)),
        here(r.wout_own, quarter_of(r.wout, t, hidden)),
    ]

    for p in range(3):
        r.bq[t, p * RANK_PAD : (p + 1) * RANK_PAD] = filled(r.b_qkv[p], RANK_PAD)
    pick = lax.broadcasted_iota(jnp.int32, (16, heads_here), 0)
    pick = pick == lax.broadcasted_iota(jnp.int32, (16, heads_here), 1)
    r.rb[t] = nn(pick.astype(F32).astype(BF16), r.table[...]).astype(BF16)
    r.bin[t] = filled(r.b_in[...], PAD)
    for copy in get_qkv:
        copy.wait()
    pl.semaphore_wait(barrier, len(known))
    qkv_chunks[0].start()
    core_qkv.start()
    small_core[0].start()
    small_core[1].start()
    qkv_chunks[1].start()
    small_y[0].start()
    small_y[1].start()
    qkv_chunks[2].start()
    get_c.start()
    keep[0].start()
    keep[1].start()
    for p in range(3):
        r.wsm[p * PAD : (p + 1) * PAD, :] = filled(r.at[p], PAD)
    spots = lax.broadcasted_iota(jnp.int32, (PAD, experts), 0) // rank
    spots = spots == lax.broadcasted_iota(jnp.int32, (PAD, experts), 1)
    r.wsm[3 * PAD :, :] = nn(spots.astype(F32).astype(BF16), r.router[...]).astype(BF16)
    r.ao[...] = filled(r.a_o[...], PAD)
    r.bo[...] = filled(r.b_o[...], PAD)
    r.ain[...] = filled(r.at[3], PAD)
    r.bout[...] = filled(r.b_out[...], PAD)
    for j in range(groups):
        r.aout[j] = filled(r.a_out[:, j * hidden : (j + 1) * hidden], PAD)
    g1 = r.g1[...].reshape(1, width)
    g2 = r.g2[...].reshape(1, width)

    tb = 256
    get_x.wait()

    def norm(i, c):
        rows = ds(i * tb, tb)
        x = r.xy[rows, :].astype(F32)
        n1 = (x * lax.rsqrt(jnp.mean(x * x, axis=1, keepdims=True) + EPS) * g1).astype(BF16)
        r.n1[rows, :] = n1
        lines = nt(r.wsm[...], n1)
        low = lines[: 3 * PAD]
        logits = lines[3 * PAD :]
        valid = lax.broadcasted_iota(jnp.int32, logits.shape, 0) < cols
        logits = jnp.where(valid, logits, -jnp.inf)
        ex = jnp.exp(logits - jnp.max(logits, axis=0, keepdims=True))
        gate = ex / (jnp.sum(ex, axis=0, keepdims=True) * (1.0 / rank))
        r.low[:, rows] = low
        r.gate[:, rows] = gate
        for p in range(3):
            r.gated[p * PAD : (p + 1) * PAD, rows] = (low[p * PAD : (p + 1) * PAD] * gate).astype(BF16)
        return c

    lax.fori_loop(0, tokens // tb, norm, 0)

    maskrow = jnp.where(lax.broadcasted_iota(jnp.int32, (16, seq), 1) < r.lens[seqs - 1], 0.0, NEG)
    maskrow = jnp.where(lax.broadcasted_iota(jnp.int32, (16, seq), 0) == 0, maskrow, 0.0).astype(BF16)
    onerow = (lax.broadcasted_iota(jnp.int32, (16, seq), 0) == 0).astype(F32).astype(BF16)

    def head_row(n):
        return (group_at(t, n // heads_here) * heads_here + n % heads_here) * span

    def next_group(k):
        g = group_at(t, k)
        u = nn(r.rb[g], r.onehot[...]) * LOG2E
        for h in range(heads_here):
            r.urow[k * heads_here + h] = u[h : h + 1]
            for p in range(3):
                block = r.bq[g, p * RANK_PAD : (p + 1) * RANK_PAD, h * hd : (h + 1) * hd]
                r.bh[h, p * PAD : p * PAD + RANK_PAD, :] = block

    def project(n):
        row = head_row(n)
        h = n % heads_here
        out = nt(r.wqkv[ds(row, span), :], r.n1[...])
        for p in range(3):
            up = tn(r.bh[h, p * PAD : p * PAD + RANK_PAD, :], r.gated[p * PAD : p * PAD + RANK_PAD, :])
            r.qkv[ds(row + p * hd, hd), :] = (out[p * hd : (p + 1) * hd] + up).astype(BF16)

    def spread_bias(n):
        line = jnp.broadcast_to(r.urow[n], (128, 2 * seq))
        r.brow[n % 2] = pltpu.roll(line, 0, 1, stride=1, stride_axis=0)[:, : 2 * seq - 128]

    qb = 256
    parts = seq // qb

    def score_place(i):
        return slice((i % 2) * seq, (i % 2 + 1) * seq), slice((i // 2 % 3) * qb, (i // 2 % 3 + 1) * qb)

    def attend(n):
        row = head_row(n)
        full = ds(row // 3, hd)
        blocks = [(s, b) for s in range(seqs) for b in range(parts)]
        made, tops = {}, {}

        def score(i):
            s, b = blocks[i]
            token = slice(s * seq, (s + 1) * seq)
            if b == 0:
                q = r.qkv[ds(row, hd), token]
                k = r.qkv[ds(row + hd, hd), token].astype(F32) * LOG2E
                high = k.astype(BF16)
                keys = [high, (k - high.astype(F32)).astype(BF16)]
                queries = [q, q]
                if s > 0:
                    keys.append(maskrow)
                    queries.append(onerow)
                v = jnp.concatenate([r.qkv[ds(row + 2 * hd, hd), token], onerow], axis=0)
                made[s] = jnp.concatenate(keys, axis=0), jnp.concatenate(queries, axis=0), v
            keys, queries, v = made[s]
            top = None
            rows, lanes = score_place(i)
            for kc in range(seq // 256):
                st = tn(keys[:, kc * 256 : (kc + 1) * 256], queries[:, b * qb : (b + 1) * qb])
                for kk in range(2):
                    kb = kc * 2 + kk
                    shift = seq - 128 - 128 * kb + b * qb
                    st_b = st[kk * 128 : (kk + 1) * 128] + r.brow[n % 2, :, shift : shift + qb]
                    r.acc[rows.start + kb * 128 : rows.start + (kb + 1) * 128, lanes] = st_b
                    peak = jnp.max(st_b, axis=0, keepdims=True)
                    top = peak if top is None else jnp.maximum(top, peak)
            tops[i] = top

        def soft(i):
            s, b = blocks[i]
            v = made[s][2]
            rows, lanes = score_place(i)
            token = slice(s * seq + b * qb, s * seq + (b + 1) * qb)
            for kb in range(seq // 128):
                st = r.acc[rows.start + kb * 128 : rows.start + (kb + 1) * 128, lanes]
                r.e[n * seqs + s, kb * 128 : (kb + 1) * 128, b * qb : (b + 1) * qb] = jnp.exp2(st - tops[i]).astype(
                    BF16
                )
            o = nn(v, r.e[n * seqs + s, :, b * qb : (b + 1) * qb])
            recip = 1.0 / o[hd : hd + 1]
            r.recip[n, :, token] = recip
            r.ctx[full, token] = (o[:hd] * recip).astype(BF16)

        ahead = 3
        for i in range(ahead):
            score(i)
        for i in range(len(blocks)):
            if i + ahead < len(blocks):
                score(i + ahead)
            soft(i)

    def forward_step(step):
        if step == 1:
            qkv_chunks[0].relay()
        if step == 2:
            core_qkv.wait_recv()
            small_core[0].wait_recv()
            small_core[1].wait_recv()
            o_chunk.start()
            core_o.start()
        if step == 3:
            qkv_chunks[0].forward()
            qkv_chunks[1].relay()
            small_y[0].wait_recv()
            small_y[1].wait_recv()
            small_far[0].start()
            small_far[1].start()
        if step == 4:
            in_chunks[0].start()
            core_in.start()
            qkv_chunks[2].relay()
        if step == 5:
            qkv_chunks[0].close()
            qkv_chunks[1].forward()
        if step == 6:
            qkv_chunks[1].close()
            qkv_chunks[2].forward()
        if step == 7:
            qkv_chunks[2].close()
            o_chunk.relay()
            in_chunks[1].start()
        if step == 8:
            small_far[0].wait_recv()
            small_far[1].wait_recv()
            for chunk in qkv_chunks:
                chunk.whole_here()
        if step == 9:
            in_chunks[0].relay()
            o_chunk.forward()
            out_chunks[0].start()
            core_out.start()
            keep[2].start()
            small_y[2].start()
            small_core[2].start()
        if step == 11:
            in_chunks[1].relay()
            o_chunk.close()
            out_chunks[1].start()

    next_group(0)
    project(0)
    spread_bias(0)

    def forward_head(n, c):
        for step in (1, 2, 3, 4, 5, 6, 7, 8, 9, 11):
            pl.when(n == step)(lambda step=step: forward_step(step))
        last = heads - 1
        follow = jnp.minimum(n + 1, last)

        @pl.when(jnp.logical_and((n + 1) % heads_here == 0, n < last))
        def _():
            next_group((n + 1) // heads_here)

        attend(n)
        project(follow)
        spread_bias(follow)
        return c

    lax.fori_loop(0, heads, forward_head, 0)

    core_o.wait_recv()
    keep[0].wait()
    o_chunk.whole_here()
    get_c.wait()
    keep[1].wait()
    win_first = here(quarter_of(r.win_all, t, width), r.win.at[0])
    win_first.start()

    def first(i, c):
        for j in range(2):
            rows = ds((2 * i + j) * tb, tb)
            gate = r.gate[:, rows]
            ctx = r.ctx[:, rows]
            low = nn(r.ao[...], ctx)
            r.low_o[:, rows] = low
            gated = (low * gate).astype(BF16)
            h1 = r.xy[rows, :].astype(F32) + tn(ctx, r.wo[...]) + tn(gated, r.bo[...])
            r.h1[rows, :] = h1
            n2 = (h1 * lax.rsqrt(jnp.mean(h1 * h1, axis=1, keepdims=True) + EPS) * g2).astype(BF16)
            r.n2[rows, :] = n2
            low = nt(r.ain[...], n2)
            r.low_in[:, rows] = low
            r.gin[:, rows] = (low * gate).astype(BF16)
            low = nt(r.bout[...], r.cot[rows, :])
            r.d_low_out[:, rows] = low
            r.dgo[:, rows] = (low * gate).astype(BF16)
        return c

    lax.fori_loop(0, tokens // tb // 2, first, 0)
    r.acc[...] = jnp.zeros_like(r.acc)
    r.dn2[...] = jnp.zeros_like(r.dn2)
    r.low_out[...] = jnp.zeros_like(r.low_out)
    r.d_low_in[...] = jnp.zeros_like(r.d_low_in)
    r.part[...] = jnp.zeros_like(r.part)

    wide = 512
    blocks = tokens // wide
    win_next = [here(quarter_of(r.win_all, group_at(t, k), width), r.win.at[k % 2]) for k in range(1, groups)]

    def feed_step(step):
        if step == 0:
            keep[2].wait()
            out_chunks[0].relay()
            in_chunks[0].forward()
            win_first.wait()
        if step == 1:
            in_chunks[1].forward()
            out_chunks[1].relay()
            small_y[2].wait_recv()
            small_far[2].start()
            core_in.wait_recv()
            win_next[0].start()
        if step == 2:
            in_chunks[0].close()
            out_chunks[0].forward()
            core_out.wait_recv()
            small_core[2].wait_recv()
            win_next[0].wait()
        if step == 3:
            in_chunks[1].close()
            out_chunks[1].forward()
            win_next[1].start()
        if step == 4:
            out_chunks[0].close()
            out_chunks[1].close()
            win_next[1].wait()
        if step == 5:
            for chunk in in_chunks:
                chunk.whole_here()
            small_far[2].wait_recv()
            win_next[2].start()
        if step == 6:
            for chunk in out_chunks:
                chunk.whole_here()
            win_next[2].wait()

    active, d_pre = r.xy.at[:wide], r.xy.at[wide : 2 * wide]
    third = hidden // 3

    def chunk(step, c):
        for point in range(7):
            pl.when(step == point)(lambda point=point: feed_step(point))
        n = step // blocks
        rows = ds((step % blocks) * wide, wide)
        g = group_at(t, n)
        slot = n % 2
        gin, dgo = r.gin[:, rows], r.dgo[:, rows]
        for j in range(3):
            cs = slice(j * third, (j + 1) * third)
            pre = nn(r.n2[rows, :], r.win[slot, :, cs]) + tn(gin, r.bin[g, :, cs])
            da = nt(r.cot[rows, :], r.wout[ds(g * hidden + j * third, third), :]) + tn(dgo, r.aout[g, :, cs])
            sig = 1.0 / (1.0 + jnp.exp(-pre))
            act = pre * sig
            active[:, cs] = act.astype(BF16)
            d_pre[:, cs] = (da * (sig + act * (1.0 - sig))).astype(BF16)
        r.acc[rows, :] += nn(active[...], r.wout[ds(g * hidden, hidden), :])
        r.dn2[rows, :] += nt(d_pre[...], r.win[slot])
        r.low_out[:, rows] += nt(r.aout[g], active[...])
        r.d_low_in[:, rows] += nt(r.bin[g], d_pre[...])
        r.part[g, :cols] += nn(dgo, active[...])[:cols]
        r.part[g, 2 * cols : 3 * cols] += nn(gin, d_pre[...])[:cols]
        return c

    lax.fori_loop(0, groups * blocks, chunk, 0)

    def last(i, c):
        for j in range(2):
            rows = ds((2 * i + j) * tb, tb)
            gate = r.gate[:, rows]
            cot, n2, ctx, h1 = r.cot[rows, :], r.n2[rows, :], r.ctx[:, rows], r.h1[rows, :]
            low_out, d_low_in = r.low_out[:, rows], r.d_low_in[:, rows]
            go = (low_out * gate).astype(BF16)
            r.xy[rows, :] = (h1 + r.acc[rows, :] + tn(go, r.bout[...])).astype(BF16)
            dgi = (d_low_in * gate).astype(BF16)
            up = (r.dn2[rows, :] + tn(dgi, r.ain[...])) * g2
            r.part[2, cols : 2 * cols] += nn(go, cot)[:cols]
            r.part[3, cols : 2 * cols] += nn(dgi, n2)[:cols]
            inv = lax.rsqrt(jnp.mean(h1 * h1, axis=1, keepdims=True) + EPS)
            dh = cot.astype(F32) + inv * up - h1 * (inv * inv * inv * jnp.mean(h1 * up, axis=1, keepdims=True))
            r.h1[rows, :] = dh
            da = dh.astype(BF16)
            d_low = nt(r.bo[...], da)
            low = r.low_o[:, rows]
            dgo = (d_low * gate).astype(BF16)
            r.part[1, cols : 2 * cols] += nn((low * gate).astype(BF16), da)[:cols]
            r.part[0, cols : 2 * cols] += nt(dgo, ctx)[:cols]
            r.dctx[:, rows] = (nt(r.wo[...], da) + tn(r.ao[...], dgo)).astype(BF16)
            r.zed[:, rows] = d_low * low + d_low_in * r.low_in[:, rows] + r.d_low_out[:, rows] * low_out
        return c

    lax.fori_loop(0, tokens // tb // 2, last, 0)
    put_y = here(r.xy, r.y)
    put_y.start()

    rows_half = 64
    mine, other = ds(half * rows_half, rows_half), ds((1 - half) * rows_half, rows_half)
    shared = 2 * cols
    to_core = links(r.cot.at[:256], r.core_in, places.core)
    to_y = links(r.y_out, r.y_in, places.y)
    to_x = links(r.x_out, r.x_in, places.x)
    to_z = [links(r.z_out, r.z_all.at[ds(z * 64, 64)], dev) for dev in z_peers]
    keep_z = here(r.z_out, r.z_all.at[ds(z * 64, 64)])
    get_z = [here(r.z_all.at[i * 64 : (i + batch) * 64], r.z_in) for i in range(0, zs, batch)]
    all_x = links(r.full.at[t, mine], r.full.at[t, mine], places.x)
    all_y = links(r.full.at[t, :shared], r.full.at[t, :shared], places.y)
    all_core = [
        links(r.full.at[j, :shared], r.full.at[j, :shared], places.core) for j in (t, places.y_t)
    ]
    share = r.small_in.shape[1]
    b_share = r.b_in_sum.shape[1]
    me = half * 4 + t
    give = []
    for j, dev in block_peers:
        give.append(links(r.small_out.at[ds(j * share, share)], r.small_in.at[me], dev))
        give.append(links(r.b_all.at[j % 4, ds(j // 4 * b_share, b_share)], r.b_in_sum.at[me], dev))
    cross = []
    for dev in z_peers:
        cross.append(links(r.small_z.at[z], r.small_z.at[z], dev))
        cross.append(links(r.b_z.at[z], r.b_z.at[z], dev))
    back = [links(r.small_full.at[me], r.small_full.at[me], dev) for _, dev in block_peers]
    back.append(links(r.b_full.at[half], r.b_full.at[half], places.x))

    def sum_step(step):
        if step == 0:
            r.core_out[0][...] = r.part[places.core_t].astype(BF16)
            r.core_out[1][...] = r.part[places.far_t].astype(BF16)
            to_core.start()
        if step == 2:
            to_core.wait_recv()
            r.y_out[...] = (r.part[places.y_t] + r.core_in[128:].astype(F32)).astype(BF16)
            to_y.start()
            r.part[t] += r.core_in[:128].astype(F32)
            put_y.wait()
            get_x_again.start()
        if step == 5:
            to_y.wait_recv()
            r.part[t] += r.y_in[...].astype(F32)
            r.x_out[...] = r.part[t, other, :].astype(BF16)
            to_x.start()
        if step == 7:
            to_x.wait_recv()
            r.z_out[...] = (r.part[t, mine, :] + r.x_in[...].astype(F32)).astype(BF16)
            keep_z.start()
            for copy in to_z:
                copy.start()

    def sum_z():
        for copy in to_z:
            copy.wait_recv()
        keep_z.wait()
        total = None
        for copy in get_z:
            copy.start()
            copy.wait()
            for i in range(batch):
                term = r.z_in[i * 64 : (i + 1) * 64].astype(F32)
                total = term if total is None else total + term
        r.full[t, mine] = total.astype(BF16)
        all_x.start()

    get_x_again = here(r.x, r.xy)

    def attend_back(n):
        row = head_row(n)
        full = ds(row // 3, hd)
        blocks = [(s, b) for s in range(seqs) for b in range(parts)]
        sent, sums = {}, {}

        def ds_place(i):
            return slice((i % 2) * seq, (i % 2 + 1) * seq), slice((i // 2 % 3) * qb, (i // 2 % 3 + 1) * qb)

        def score(i):
            s, b = blocks[i]
            token = slice(s * seq + b * qb, s * seq + (b + 1) * qb)
            do = (r.dctx[full, token].astype(F32) * r.recip[n, :, token]).astype(BF16)
            delta = jnp.sum(do.astype(F32) * r.ctx[full, token].astype(F32), axis=0, keepdims=True)
            sent[i] = do
            v = r.qkv[ds(row + 2 * hd, hd), s * seq : (s + 1) * seq]
            rows, lanes = ds_place(i)
            for kc in range(seq // 256):
                keys = slice(kc * 256, (kc + 1) * 256)
                dp = tn(v[:, keys], do)
                e = r.e[n * seqs + s, keys, b * qb : (b + 1) * qb].astype(F32)
                r.n2[rows.start + kc * 256 : rows.start + (kc + 1) * 256, lanes] = (e * (dp - delta)).astype(BF16)

        def grads(i):
            s, b = blocks[i]
            token = slice(s * seq + b * qb, s * seq + (b + 1) * qb)
            whole = slice(s * seq, (s + 1) * seq)
            k = r.qkv[ds(row + hd, hd), whole]
            q = r.qkv[ds(row, hd), token]
            rows, lanes = ds_place(i)
            dsc = r.n2[rows, lanes]
            dk = nt(q, dsc)
            dv = nt(sent[i], r.e[n * seqs + s, :, b * qb : (b + 1) * qb])
            r.qkv[ds(row, hd), token] = nn(k, dsc).astype(BF16)
            if b > 0:
                dk, dv = sums[s][0] + dk, sums[s][1] + dv
            sums[s] = dk, dv
            if b == parts - 1:
                r.qkv[ds(row + hd, hd), whole] = dk.astype(BF16)
                r.qkv[ds(row + 2 * hd, hd), whole] = dv.astype(BF16)

        ahead = 2
        for i in range(ahead):
            score(i)
        for i in range(len(blocks)):
            if i + ahead < len(blocks):
                score(i + ahead)
            grads(i)

    def backward_head(n, c):
        for step in (0, 2, 5, 7):
            pl.when(n == step)(lambda step=step: sum_step(step))
        attend_back(n)
        return c

    lax.fori_loop(0, heads, backward_head, 0)
    sum_z()

    gsm = r.acc.at[: 4 * PAD]

    def adapters(g, c):
        for p in range(3):
            dp = [
                r.qkv[ds((g * heads_here + h) * span + p * hd, hd), :] for h in range(heads_here)
            ]
            dp = jnp.concatenate(dp, axis=0)
            low = nn(r.bq[g, p * RANK_PAD : (p + 1) * RANK_PAD], dp)
            r.d_low[p][:RANK_PAD, :] += low
            r.acc[gb_rows(g, p), :inner] = nt(r.gated[p * PAD : (p + 1) * PAD, :], dp)
        return c

    for p in range(3):
        r.d_low[p][...] = jnp.zeros(r.d_low[p].shape, F32)
    lax.fori_loop(0, groups, adapters, 0)
    gate = r.gate[...]
    prod = r.zed[...]
    for p in range(3):
        part = slice(p * PAD, (p + 1) * PAD)
        prod = prod + r.d_low[p][...] * r.low[part, :]
        r.dsmall[part, :] = (r.d_low[p][...] * gate).astype(BF16)
    high = prod.astype(BF16)
    low = (prod - high.astype(F32)).astype(BF16)
    same = lax.broadcasted_iota(jnp.int32, (PAD, PAD), 0) // rank
    same = same == lax.broadcasted_iota(jnp.int32, (PAD, PAD), 1) // rank
    same = jnp.logical_and(same, lax.broadcasted_iota(jnp.int32, (PAD, PAD), 1) < cols).astype(F32).astype(BF16)
    d_gate = nn(same, high) + nn(same, low)
    d_logit = gate * (d_gate - jnp.sum(gate * prod, axis=0, keepdims=True))
    row = lax.broadcasted_iota(jnp.int32, d_logit.shape, 0)
    chosen = jnp.logical_and(row % rank == 0, row < cols)
    r.dsmall[3 * PAD :, :] = jnp.where(chosen, d_logit, 0.0).astype(BF16)
    gsm[...] = nn(r.dsmall[...], r.n1[...])
    lines = [gsm[p * PAD : p * PAD + cols, :] for p in range(3)]
    lines.append(jnp.concatenate([gsm[3 * PAD + rank * e : 3 * PAD + rank * e + 1, :] for e in range(16)], axis=0))
    count = 3 * cols + 16
    tall = -(-count // 16) * 16
    lines.append(jnp.zeros((tall - count, width), F32))
    lines = jnp.concatenate(lines, axis=0).astype(BF16)
    strips = width // 128
    for i in range(strips):
        r.small_out[i * tall : (i + 1) * tall, :] = lines[:, i * 128 : (i + 1) * 128]
    r.small_out[strips * tall :, :] = jnp.zeros((r.small_out.shape[0] - strips * tall, 128), BF16)
    for j in range(groups):
        block = [r.acc[gb_rows(j, p), :inner][:cols] for p in range(3)]
        block.append(jnp.zeros((r.b_all.shape[1] - 3 * cols, inner), F32))
        r.b_all[j] = jnp.concatenate(block, axis=0).astype(BF16)
    for copy in give:
        copy.start()
    all_x.wait_recv()
    all_y.start()
    all_core[0].start()
    get_x_again.wait()

    def finish(i, c):
        rows = ds(i * tb, tb)
        dn = tn(r.qkv[:, rows], r.wqkv[...]) + tn(r.dsmall[:, rows], r.wsm[...])
        x = r.xy[rows, :].astype(F32)
        inv = lax.rsqrt(jnp.mean(x * x, axis=1, keepdims=True) + EPS)
        up = dn * g1
        r.h1[rows, :] += inv * up - x * (inv * inv * inv * jnp.mean(x * up, axis=1, keepdims=True))
        return c

    part_rows = tokens // 2
    put_x = [here(r.h1.at[i * part_rows : (i + 1) * part_rows], r.gx.at[i * part_rows : (i + 1) * part_rows]) for i in range(2)]
    lax.fori_loop(0, tokens // tb // 2, finish, 0)
    put_x[0].start()
    all_y.wait_recv()
    all_core[1].start()
    for copy in give:
        copy.wait_recv()
    r.small_in[me] = r.small_out[ds(me * share, share), :]
    r.b_in_sum[me] = r.b_all[t, ds(half * b_share, b_share), :]
    total = r.small_in[0].astype(F32)
    total_b = r.b_in_sum[0].astype(F32)
    for i in range(1, 8):
        total = total + r.small_in[i].astype(F32)
        total_b = total_b + r.b_in_sum[i].astype(F32)
    r.small_z[z] = total.astype(BF16)
    r.b_z[z] = total_b.astype(BF16)
    for copy in cross:
        copy.start()
    lax.fori_loop(tokens // tb // 2, tokens // tb, finish, 0)
    put_x[1].start()
    for copy in cross:
        copy.wait_recv()
    total = r.small_z[0].astype(F32)
    total_b = r.b_z[0].astype(F32)
    for i in range(1, zs):
        total = total + r.small_z[i].astype(F32)
        total_b = total_b + r.b_z[i].astype(F32)
    r.small_full[me] = total.astype(BF16)
    r.b_full[half] = total_b.astype(BF16)
    for copy in back:
        copy.start()
    for copy in all_core:
        copy.wait_recv()
    r.g_b_in[...] = r.full[t].astype(F32)[2 * cols : 3 * cols]
    for j in range(groups):
        block = r.full[j].astype(F32)
        r.g_a_out[:, j * hidden : (j + 1) * hidden] = block[:cols]
        target = (r.g_a_o, r.g_b_o, r.g_b_out, r.g_a_in.at[3])[j]
        target[...] = block[cols : 2 * cols]
    for copy in back:
        copy.wait_recv()
    flat = r.small_full[...].reshape(8 * share, 128)
    for i in range(strips):
        block = flat[i * tall : (i + 1) * tall].astype(F32)
        lanes = slice(i * 128, (i + 1) * 128)
        for p in range(3):
            r.g_a_in[p, :, lanes] = block[p * cols : (p + 1) * cols]
        r.g_router[:, lanes] = block[3 * cols : 3 * cols + experts]
    block = r.b_full[...].reshape(2 * b_share, inner).astype(F32)
    for p in range(3):
        r.g_b_qkv[p] = block[p * cols : (p + 1) * cols]
    for copy in put_x:
        copy.wait()
    for copy in links.made:
        copy.wait_send()


def shards(
    layer_inputs, lengths, first_gain, second_gain, router, wqkv, bias_table, wo, win, wout,
    a_in, a_o, a_out, b_qkv, b_o, b_in, b_out, cotangent,
):
    groups = lax.axis_size("tensor")
    zs = lax.axis_size("dp") // 2
    seqs, seq, width = layer_inputs.shape
    tokens = seqs * seq
    inner = wo.shape[0]
    heads_here = bias_table.shape[1]
    heads = heads_here * groups
    hd = inner // heads_here
    hidden = win.shape[1]
    experts = router.shape[1]
    cols = a_in.shape[2]
    sizes = (tokens, width, seq, seqs, groups, inner, heads_here, hd, hidden, cols, experts, zs)
    ins = {
        "lens": (lengths, pltpu.SMEM),
        "g1": (first_gain, pltpu.VMEM),
        "g2": (second_gain, pltpu.VMEM),
        "at": (jnp.swapaxes(a_in, 1, 2), pltpu.VMEM),
        "router": (router.T, pltpu.VMEM),
        "onehot": (jnp.asarray(bucket_lines(seq), BF16), pltpu.VMEM),
        "b_qkv": (b_qkv, pltpu.VMEM),
        "table": (bias_table.T, pltpu.VMEM),
        "b_in": (b_in, pltpu.VMEM),
        "a_o": (a_o.T, pltpu.VMEM),
        "b_o": (b_o, pltpu.VMEM),
        "a_out": (a_out.T, pltpu.VMEM),
        "b_out": (b_out, pltpu.VMEM),
        "x": (layer_inputs.reshape(tokens, width), pl.ANY),
        "c": (cotangent.reshape(tokens, width), pl.ANY),
        "wqkv_own": (jnp.swapaxes(wqkv, 1, 2), pl.ANY),
        "wo_own": (wo, pl.ANY),
        "win_own": (win, pl.ANY),
        "wout_own": (wout, pl.ANY),
    }
    outs = {
        "y": ((tokens, width), BF16, pl.ANY),
        "gx": ((tokens, width), F32, pl.ANY),
        "g_router": ((experts, width), F32, pltpu.VMEM),
        "g_a_in": ((4, cols, width), F32, pltpu.VMEM),
        "g_a_o": ((cols, width), F32, pltpu.VMEM),
        "g_a_out": ((cols, groups * hidden), F32, pltpu.VMEM),
        "g_b_qkv": ((3, cols, inner), F32, pltpu.VMEM),
        "g_b_o": ((cols, width), F32, pltpu.VMEM),
        "g_b_in": ((cols, hidden), F32, pltpu.VMEM),
        "g_b_out": ((cols, width), F32, pltpu.VMEM),
        "win_all": ((groups * width, hidden), BF16, pl.ANY),
        "z_all": ((zs * 64, width), BF16, pl.ANY),
    }
    line = (PAD, tokens)
    scratch = {
        "xy": ((tokens, width), BF16),
        "cot": ((tokens, width), BF16),
        "n1": ((tokens, width), BF16),
        "low": ((3 * PAD, tokens), F32),
        "gate": (line, F32),
        "gated": ((3 * PAD, tokens), BF16),
        "wqkv": ((3 * groups * inner, width), BF16),
        "qkv": ((3 * groups * inner, tokens), BF16),
        "e": ((heads * seqs, seq, seq), BF16),
        "recip": ((heads, 1, tokens), F32),
        "ctx": ((groups * inner, tokens), BF16),
        "wsm": ((4 * PAD, width), BF16),
        "bq": ((groups, 3 * RANK_PAD, inner), BF16),
        "bh": ((heads_here, 3 * PAD, hd), BF16),
        "rb": ((groups, 16, NB), BF16),
        "bin": ((groups, PAD, hidden), BF16),
        "urow": ((heads, 1, 2 * seq), F32),
        "brow": ((2, 128, 2 * seq - 128), F32),
        "wo": ((groups * inner, width), BF16),
        "win": ((2, width, hidden), BF16),
        "wout": ((groups * hidden, width), BF16),
        "h1": ((tokens, width), F32),
        "n2": ((tokens, width), BF16),
        "acc": ((tokens, width), F32),
        "dn2": ((tokens, width), F32),
        "gin": (line, BF16),
        "dgo": (line, BF16),
        "low_o": (line, F32),
        "low_in": (line, F32),
        "low_out": (line, F32),
        "d_low_in": (line, F32),
        "d_low_out": (line, F32),
        "dctx": ((groups * inner, tokens), BF16),
        "part": ((groups, 128, width), F32),
        "ao": ((PAD, width), BF16),
        "bo": ((PAD, width), BF16),
        "ain": ((PAD, width), BF16),
        "bout": ((PAD, width), BF16),
        "aout": ((groups, PAD, hidden), BF16),
        "core_in": ((256, width), BF16),
        "y_in": ((128, width), BF16),
        "x_in": ((64, width), BF16),
        "full": ((groups, 128, width), BF16),
        "small_out": ((896, 128), BF16),
        "small_in": ((8, 112, 128), BF16),
        "small_z": ((zs, 112, 128), BF16),
        "small_full": ((8, 112, 128), BF16),
        "b_all": ((groups, 128, inner), BF16),
        "b_in_sum": ((8, 64, inner), BF16),
        "b_z": ((zs, 64, inner), BF16),
        "b_full": ((2, 64, inner), BF16),
    }
    copies = 9 * 8 + 40 + 3 * zs
    shapes = [pltpu.VMEM(*v) for v in scratch.values()]
    shapes += [pltpu.SemaphoreType.DMA((copies,)), pltpu.SemaphoreType.DMA((copies,)), pltpu.SemaphoreType.DMA((40,))]
    names = list(ins) + list(outs) + list(scratch) + ["send", "recv", "local"]
    flops = 2 * tokens * (8 * width * hidden * groups + 24 * width * width)
    results = pl.pallas_call(
        lambda *refs: layer(names, sizes, *refs),
        name="encoder_layer",
        out_shape=[jax.ShapeDtypeStruct(o[0], o[1]) for o in outs.values()],
        in_specs=[pl.BlockSpec(memory_space=i[1]) for i in ins.values()],
        out_specs=[pl.BlockSpec(memory_space=o[2]) for o in outs.values()],
        scratch_shapes=shapes,
        cost_estimate=pl.CostEstimate(flops=flops, bytes_accessed=30 * 2**20, transcendentals=0),
        compiler_params=pltpu.CompilerParams(
            vmem_limit_bytes=VMEM_LIMIT, collective_id=0, has_side_effects=True
        ),
    )(*[i[0] for i in ins.values()])
    y, gx, g_router, g_in, g_ao, g_aout, g_bqkv, g_bo, g_bin, g_bout = results[:10]
    return (
        y.reshape(layer_inputs.shape),
        gx.reshape(layer_inputs.shape),
        g_router.T,
        jnp.swapaxes(g_in, 1, 2),
        g_ao.T,
        g_aout.T,
        g_bqkv,
        g_bo,
        g_bin,
        g_bout,
    )


def solution(mesh):
    rows = P(("dp", "tensor"), None, None)
    placed = (
        rows, P(("dp", "tensor")), P(), P(), P(), P(None, None, "tensor"), P(None, "tensor"), P("tensor", None),
        P(None, "tensor"), P("tensor", None), P(), P(), P(), P(None, None, "tensor"), P(), P(None, "tensor"), P(), rows,
    )
    return jax.shard_map(
        shards,
        mesh=mesh,
        in_specs=placed,
        out_specs=(rows, rows, P(), P(), P(), P(), P(None, None, "tensor"), P(), P(None, "tensor"), P()),
        check_vma=False,
    )
```

time: 407 us -> 144 us (0.35)
  waiting for transfers between devices: 163 us -> 0 us
  blocking collectives: 61.4 us -> 0 us
  between operations: 14 us -> 0.7 us
  local copies, waits for them, and re-layouts: 22.3 us -> 9.93 us
  Pallas kernels: 144 us -> 133 us
    psum x1 -> x0, waiting for transfers between devices: 97 us -> none  [shards(): lax.psum((g_router, g_in, gao[:cols], gaout[:, :cols], gbqkv[:, :, :cols]...]
    all_gather x4 -> x0, waiting for transfers between devices: 63.9 us -> none  [gather(): return lax.all_gather(v, 'tensor', axis=0)]
    psum x1 -> x0, blocking collectives: 40.6 us -> none  [shards(): lax.psum((g_router, g_in, gao[:cols], gaout[:, :cols], gbqkv[:, :, :cols]...]
    all_gather x3 -> x0, blocking collectives: 20.9 us -> none  [gather(): return lax.all_gather(v, 'tensor', axis=0)]
    pallas_call x3 -> x1, Pallas kernels: 144 us -> 133 us  [shards(): pl.pallas_call(lambda *refs: layer(names, sizes, *refs), name='encoder_la...]
    slice x7 -> x0, local copies, waits for them, and re-layouts: 6.09 us -> none  [the longest x1 1.91 us: shards(): gbqkv[:, :, :cols]]
    pad x8 -> x0, local copies, waits for them, and re-layouts: 5.54 us -> none  [the longest x7 4.94 us: pad_rows(): return jnp.pad(a, width)]
    unnamed x49 -> x28, local copies, waits for them, and re-layouts: 4.69 us -> 9.93 us
  transfers between devices with their start and end apart: 5 -> 0, of which waited for: 4 -> 0; matrix products, arithmetic and copies ran while one was open for 2% -> 0% of each run, Pallas kernels for 10% -> 0%
where the time goes in v4:
time: 144 us; the launch traced here: 143 us
  Pallas kernels  133 us (92%)
  local copies, waits for them, and re-layouts  9.93 us (7%)
    pallas_call x1, Pallas kernels, shards(): pl.pallas_call(lambda *refs: layer(names, sizes, *refs), name='encoder_la...  133 us
    unnamed x28, local copies, waits for them, and re-layouts  9.93 us

profile of v4, /device:TPU:0, one launch (start us, length us, event | category | flops | bytes accessed | tf_op | source)
XLA Modules:
  0.0 143.4 jit_solution(18109746784174816467)
XLA Ops:
  0.7 132.8 %encoder_layer.1 = (bf16[1024,768]{1,0:T(8,128)(2,1)}, f32[1024,768]{1,0:T(8,128)}, f32[10,768]{1,0:T(8,128)}, f32[4,40,768]{2,1,0:T(8,128)}, f32[40,768]{1,0:T(...) custom-call(s32[2]{0:T(128)} %refs_0_.1, ...), custom_call_target="tpu_custom_call" | custom-call | flops 67645734912 | bytes 31457280 | tf_op jit(solution)/shard_map/encoder_layer/pallas_call | solution.py:942
  133.4 0.0 copy-start
  133.4 2.8 %copy.39 = bf16[2,512,768]{2,1,0:T(8,128)(2,1)} copy(bf16[2,512,768]{2,1,0:T(8,128)(2,1)} %bitcast.15) | data formatting | bytes 3145728
  136.2 0.0 copy-done
  136.2 0.0 copy-start.8
  136.2 0.0 copy-start.2
  136.2 0.0 copy-start.7
  136.2 1.7 %copy.40 = f32[2,512,768]{2,1,0:T(8,128)} copy(f32[2,512,768]{2,1,0:T(8,128)S(1)} %bitcast.14) | data formatting | bytes 6291456
  137.9 0.0 copy-done.8
  137.9 0.0 copy-start.1
  137.9 0.0 copy-start.6
  137.9 0.0 copy-start.5
  137.9 0.0 copy-start.4
  137.9 0.0 copy-start.3
  137.9 0.6 copy.41
  138.6 0.0 copy-done.2
  138.6 0.8 copy.42
  139.3 0.0 copy-done.7
  139.3 0.6 copy.43
  140.0 0.0 copy-done.1
  140.0 0.8 copy.44
  140.8 0.0 copy-done.6
  140.8 0.6 copy.45
  141.4 0.0 copy-done.5
  141.4 0.6 copy.46
  142.1 0.0 copy-done.4
  142.1 0.6 copy.47
  142.7 0.0 copy-done.3
  142.7 0.6 copy.48
Async XLA Ops:
  133.4 2.8 %copy-start = (f32[1024,768]{1,0:T(8,128)S(1)}, f32[1024,768]{1,0:T(8,128)}, u32[]{:S(2)}) copy-start(f32[1024,768]{1,0:T(8,128)} %get-tuple-element.21) | copy-start | bytes 9437188
  136.2 1.7 %copy-start.8 = (f32[10,768]{1,0:T(8,128)S(1)}, f32[10,768]{1,0:T(8,128)}, u32[]{:S(2)}) copy-start(f32[10,768]{1,0:T(8,128)} %get-tuple-element.22) | copy-start | bytes 92164
  136.2 2.3 %copy-start.2 = (f32[4,40,768]{2,1,0:T(8,128)S(1)}, f32[4,40,768]{2,1,0:T(8,128)}, u32[]{:S(2)}) copy-start(f32[4,40,768]{2,1,0:T(8,128)} %get-tuple-element.23) | copy-start | bytes 1474564
  136.2 3.1 %copy-start.7 = (f32[40,768]{1,0:T(8,128)S(1)}, f32[40,768]{1,0:T(8,128)}, u32[]{:S(2)}) copy-start(f32[40,768]{1,0:T(8,128)} %get-tuple-element.24) | copy-start | bytes 368644
  137.9 2.1 %copy-start.1 = (f32[40,3072]{1,0:T(8,128)S(1)}, f32[40,3072]{1,0:T(8,128)}, u32[]{:S(2)}) copy-start(f32[40,3072]{1,0:T(8,128)} %get-tuple-element.25) | copy-start | bytes 1474564
  137.9 2.9 %copy-start.6 = (f32[3,40,192]{2,1,0:T(8,128)S(1)}, f32[3,40,192]{2,1,0:T(8,128)}, u32[]{:S(2)}) copy-start(f32[3,40,192]{2,1,0:T(8,128)} %get-tuple-element.46) | copy-start | bytes 276484
  137.9 3.5 %copy-start.5 = (f32[40,768]{1,0:T(8,128)S(1)}, f32[40,768]{1,0:T(8,128)}, u32[]{:S(2)}) copy-start(f32[40,768]{1,0:T(8,128)} %get-tuple-element.47) | copy-start | bytes 368644
  137.9 4.2 %copy-start.4 = (f32[40,768]{1,0:T(8,128)S(1)}, f32[40,768]{1,0:T(8,128)}, u32[]{:S(2)}) copy-start(f32[40,768]{1,0:T(8,128)} %get-tuple-element.48) | copy-start | bytes 368644
  137.9 4.8 %copy-start.3 = (f32[40,768]{1,0:T(8,128)S(1)}, f32[40,768]{1,0:T(8,128)}, u32[]{:S(2)}) copy-start(f32[40,768]{1,0:T(8,128)} %get-tuple-element.49) | copy-start | bytes 368644

commit v5 on v4

--- a/solution.py
+++ b/solution.py
@@ -227,7 +227,6 @@
     small_far = [links(a.at[places.y_t], a.at[places.y_t], places.core) for a in small]
     keep = [
         here(r.wo_own, quarter_of(r.wo, t, inner)),
-        here(r.win_own, quarter_of(r.win_all, t, width)),
         here(r.wout_own, quarter_of(r.wout, t, hidden)),
     ]
 
@@ -245,12 +244,12 @@
     small_core[0].start()
     small_core[1].start()
     qkv_chunks[1].start()
+    qkv_chunks[2].start()
+    o_chunk.start()
     small_y[0].start()
     small_y[1].start()
-    qkv_chunks[2].start()
     get_c.start()
     keep[0].start()
-    keep[1].start()
     for p in range(3):
         r.wsm[p * PAD : (p + 1) * PAD, :] = filled(r.at[p], PAD)
     spots = lax.broadcasted_iota(jnp.int32, (PAD, experts), 0) // rank
@@ -322,141 +321,152 @@
     def score_place(i):
         return slice((i % 2) * seq, (i % 2 + 1) * seq), slice((i // 2 % 3) * qb, (i // 2 % 3 + 1) * qb)
 
-    def attend(n):
+    blocks = [(s, b) for s in range(seqs) for b in range(parts)]
+
+    def keys_of(n, s):
         row = head_row(n)
-        full = ds(row // 3, hd)
-        blocks = [(s, b) for s in range(seqs) for b in range(parts)]
-        made, tops = {}, {}
-
-        def score(i):
-            s, b = blocks[i]
-            token = slice(s * seq, (s + 1) * seq)
-            if b == 0:
-                q = r.qkv[ds(row, hd), token]
-                k = r.qkv[ds(row + hd, hd), token].astype(F32) * LOG2E
-                high = k.astype(BF16)
-                keys = [high, (k - high.astype(F32)).astype(BF16)]
-                queries = [q, q]
-                if s > 0:
-                    keys.append(maskrow)
-                    queries.append(onerow)
-                v = jnp.concatenate([r.qkv[ds(row + 2 * hd, hd), token], onerow], axis=0)
-                made[s] = jnp.concatenate(keys, axis=0), jnp.concatenate(queries, axis=0), v
-            keys, queries, v = made[s]
-            top = None
-            rows, lanes = score_place(i)
-            for kc in range(seq // 256):
-                st = tn(keys[:, kc * 256 : (kc + 1) * 256], queries[:, b * qb : (b + 1) * qb])
-                for kk in range(2):
-                    kb = kc * 2 + kk
-                    shift = seq - 128 - 128 * kb + b * qb
-                    st_b = st[kk * 128 : (kk + 1) * 128] + r.brow[n % 2, :, shift : shift + qb]
-                    r.acc[rows.start + kb * 128 : rows.start + (kb + 1) * 128, lanes] = st_b
-                    peak = jnp.max(st_b, axis=0, keepdims=True)
-                    top = peak if top is None else jnp.maximum(top, peak)
-            tops[i] = top
-
-        def soft(i):
-            s, b = blocks[i]
-            v = made[s][2]
-            rows, lanes = score_place(i)
-            token = slice(s * seq + b * qb, s * seq + (b + 1) * qb)
-            for kb in range(seq // 128):
-                st = r.acc[rows.start + kb * 128 : rows.start + (kb + 1) * 128, lanes]
-                r.e[n * seqs + s, kb * 128 : (kb + 1) * 128, b * qb : (b + 1) * qb] = jnp.exp2(st - tops[i]).astype(
-                    BF16
-                )
-            o = nn(v, r.e[n * seqs + s, :, b * qb : (b + 1) * qb])
-            recip = 1.0 / o[hd : hd + 1]
-            r.recip[n, :, token] = recip
-            r.ctx[full, token] = (o[:hd] * recip).astype(BF16)
-
-        ahead = 3
-        for i in range(ahead):
-            score(i)
-        for i in range(len(blocks)):
-            if i + ahead < len(blocks):
-                score(i + ahead)
-            soft(i)
+        token = slice(s * seq, (s + 1) * seq)
+        q = r.qkv[ds(row, hd), token]
+        k = r.qkv[ds(row + hd, hd), token].astype(F32) * LOG2E
+        high = k.astype(BF16)
+        keys = [high, (k - high.astype(F32)).astype(BF16)]
+        queries = [q, q]
+        if s > 0:
+            keys.append(maskrow)
+            queries.append(onerow)
+        return jnp.concatenate(keys, axis=0), jnp.concatenate(queries, axis=0)
+
+    def values_of(n):
+        row = head_row(n)
+        return [
+            jnp.concatenate([r.qkv[ds(row + 2 * hd, hd), s * seq : (s + 1) * seq], onerow], axis=0)
+            for s in range(seqs)
+        ]
+
+    def score(n, i, made):
+        s, b = blocks[i]
+        if b == 0:
+            made[s] = keys_of(n, s)
+        keys, queries = made[s]
+        top = None
+        rows, lanes = score_place(i)
+        for kc in range(seq // 256):
+            st = tn(keys[:, kc * 256 : (kc + 1) * 256], queries[:, b * qb : (b + 1) * qb])
+            for kk in range(2):
+                kb = kc * 2 + kk
+                shift = seq - 128 - 128 * kb + b * qb
+                st_b = st[kk * 128 : (kk + 1) * 128] + r.brow[n % 2, :, shift : shift + qb]
+                r.acc[rows.start + kb * 128 : rows.start + (kb + 1) * 128, lanes] = st_b
+                peak = jnp.max(st_b, axis=0, keepdims=True)
+                top = peak if top is None else jnp.maximum(top, peak)
+        return top
+
+    def soft(n, i, top, values):
+        s, b = blocks[i]
+        rows, lanes = score_place(i)
+        token = slice(s * seq + b * qb, s * seq + (b + 1) * qb)
+        for kb in range(seq // 128):
+            st = r.acc[rows.start + kb * 128 : rows.start + (kb + 1) * 128, lanes]
+            r.e[n * seqs + s, kb * 128 : (kb + 1) * 128, b * qb : (b + 1) * qb] = jnp.exp2(st - top).astype(BF16)
+        o = nn(values[s], r.e[n * seqs + s, :, b * qb : (b + 1) * qb])
+        recip = 1.0 / o[hd : hd + 1]
+        r.recip[n, :, token] = recip
+        r.ctx[ds(head_row(n) // 3, hd), token] = (o[:hd] * recip).astype(BF16)
 
     def forward_step(step):
+        if step == 0:
+            qkv_chunks[0].relay()
         if step == 1:
-            qkv_chunks[0].relay()
+            in_chunks[0].start()
         if step == 2:
+            qkv_chunks[1].relay()
             core_qkv.wait_recv()
             small_core[0].wait_recv()
             small_core[1].wait_recv()
-            o_chunk.start()
             core_o.start()
         if step == 3:
+            qkv_chunks[2].relay()
             qkv_chunks[0].forward()
-            qkv_chunks[1].relay()
+            in_chunks[1].start()
+        if step == 4:
+            qkv_chunks[1].forward()
+        if step == 5:
+            qkv_chunks[0].close()
+            qkv_chunks[2].forward()
             small_y[0].wait_recv()
             small_y[1].wait_recv()
             small_far[0].start()
             small_far[1].start()
-        if step == 4:
-            in_chunks[0].start()
-            core_in.start()
-            qkv_chunks[2].relay()
-        if step == 5:
-            qkv_chunks[0].close()
-            qkv_chunks[1].forward()
+            o_chunk.relay()
         if step == 6:
             qkv_chunks[1].close()
-            qkv_chunks[2].forward()
+            out_chunks[0].start()
         if step == 7:
             qkv_chunks[2].close()
-            o_chunk.relay()
-            in_chunks[1].start()
+            o_chunk.forward()
+            in_chunks[0].relay()
+            core_in.start()
+            small_y[2].start()
+            small_core[2].start()
         if step == 8:
             small_far[0].wait_recv()
             small_far[1].wait_recv()
-            for chunk in qkv_chunks:
-                chunk.whole_here()
+            qkv_chunks[0].whole_here()
+            out_chunks[1].start()
         if step == 9:
-            in_chunks[0].relay()
-            o_chunk.forward()
-            out_chunks[0].start()
+            qkv_chunks[1].whole_here()
+            o_chunk.close()
+            in_chunks[1].relay()
+        if step == 10:
+            qkv_chunks[2].whole_here()
             core_out.start()
-            keep[2].start()
-            small_y[2].start()
-            small_core[2].start()
+            keep[1].start()
         if step == 11:
-            in_chunks[1].relay()
-            o_chunk.close()
-            out_chunks[1].start()
+            in_chunks[0].forward()
+            out_chunks[0].relay()
+
+    def first_step(step):
+        if step == 1:
+            in_chunks[1].forward()
+            out_chunks[1].relay()
+
+    def forward_head(n, tops):
+        for step in range(12):
+            pl.when(n == step)(lambda step=step: forward_step(step))
+        follow = jnp.minimum(n + 1, heads - 1)
+
+        @pl.when(jnp.logical_and(follow % heads_here == 0, n < heads - 1))
+        def _():
+            next_group(follow // heads_here)
+
+        values = values_of(n)
+        project(follow)
+        spread_bias(follow)
+        made, fresh = {}, []
+        behind = 2
+        for i in range(len(blocks)):
+            soft(n, i, tops[i], values)
+            if i + 1 >= behind:
+                fresh.append(score(follow, i + 1 - behind, made))
+        for i in range(len(fresh), len(blocks)):
+            fresh.append(score(follow, i, made))
+        return tuple(fresh)
 
     next_group(0)
     project(0)
     spread_bias(0)
-
-    def forward_head(n, c):
-        for step in (1, 2, 3, 4, 5, 6, 7, 8, 9, 11):
-            pl.when(n == step)(lambda step=step: forward_step(step))
-        last = heads - 1
-        follow = jnp.minimum(n + 1, last)
-
-        @pl.when(jnp.logical_and((n + 1) % heads_here == 0, n < last))
-        def _():
-            next_group((n + 1) // heads_here)
-
-        attend(n)
-        project(follow)
-        spread_bias(follow)
-        return c
-
-    lax.fori_loop(0, heads, forward_head, 0)
+    made = {}
+    lax.fori_loop(0, heads, forward_head, tuple(score(0, i, made) for i in range(len(blocks))))
 
     core_o.wait_recv()
     keep[0].wait()
     o_chunk.whole_here()
     get_c.wait()
-    keep[1].wait()
-    win_first = here(quarter_of(r.win_all, t, width), r.win.at[0])
+    win_first = here(r.win_own, r.win.at[0])
     win_first.start()
 
     def first(i, c):
+        pl.when(i == 1)(lambda: first_step(1))
         for j in range(2):
             rows = ds((2 * i + j) * tb, tb)
             gate = r.gate[:, rows]
@@ -484,42 +494,37 @@
     r.part[...] = jnp.zeros_like(r.part)
 
     wide = 512
-    blocks = tokens // wide
+    steps = tokens // wide
     win_next = [here(quarter_of(r.win_all, group_at(t, k), width), r.win.at[k % 2]) for k in range(1, groups)]
 
     def feed_step(step):
         if step == 0:
-            keep[2].wait()
-            out_chunks[0].relay()
-            in_chunks[0].forward()
+            keep[1].wait()
             win_first.wait()
-        if step == 1:
-            in_chunks[1].forward()
-            out_chunks[1].relay()
+            in_chunks[0].close()
+            out_chunks[0].forward()
+            core_in.wait_recv()
+            win_next[0].start()
             small_y[2].wait_recv()
             small_far[2].start()
-            core_in.wait_recv()
-            win_next[0].start()
+        if step == 1:
+            in_chunks[1].close()
+            out_chunks[1].forward()
         if step == 2:
-            in_chunks[0].close()
-            out_chunks[0].forward()
+            out_chunks[0].close()
             core_out.wait_recv()
             small_core[2].wait_recv()
             win_next[0].wait()
+            win_next[1].start()
         if step == 3:
-            in_chunks[1].close()
-            out_chunks[1].forward()
-            win_next[1].start()
+            out_chunks[1].close()
         if step == 4:
-            out_chunks[0].close()
-            out_chunks[1].close()
-            win_next[1].wait()
-        if step == 5:
             for chunk in in_chunks:
                 chunk.whole_here()
-            small_far[2].wait_recv()
+            win_next[1].wait()
             win_next[2].start()
         if step == 6:
+            small_far[2].wait_recv()
             for chunk in out_chunks:
                 chunk.whole_here()
             win_next[2].wait()
@@ -530,8 +535,8 @@
     def chunk(step, c):
         for point in range(7):
             pl.when(step == point)(lambda point=point: feed_step(point))
-        n = step // blocks
-        rows = ds((step % blocks) * wide, wide)
+        n = step // steps
+        rows = ds((step % steps) * wide, wide)
         g = group_at(t, n)
         slot = n % 2
         gin, dgo = r.gin[:, rows], r.dgo[:, rows]
@@ -551,7 +556,7 @@
         r.part[g, 2 * cols : 3 * cols] += nn(gin, d_pre[...])[:cols]
         return c
 
-    lax.fori_loop(0, groups * blocks, chunk, 0)
+    lax.fori_loop(0, groups * steps, chunk, 0)
 
     def last(i, c):
         for j in range(2):
@@ -805,28 +810,62 @@
         copy.start()
     for copy in all_core:
         copy.wait_recv()
-    r.g_b_in[...] = r.full[t].astype(F32)[2 * cols : 3 * cols]
-    for j in range(groups):
-        block = r.full[j].astype(F32)
-        r.g_a_out[:, j * hidden : (j + 1) * hidden] = block[:cols]
-        target = (r.g_a_o, r.g_b_o, r.g_b_out, r.g_a_in.at[3])[j]
-        target[...] = block[cols : 2 * cols]
+    results = [here(r.full, r.full_out), here(r.full.at[t, 2 * cols :], r.own_out)]
+    for copy in results:
+        copy.start()
     for copy in back:
         copy.wait_recv()
-    flat = r.small_full[...].reshape(8 * share, 128)
-    for i in range(strips):
-        block = flat[i * tall : (i + 1) * tall].astype(F32)
-        lanes = slice(i * 128, (i + 1) * 128)
-        for p in range(3):
-            r.g_a_in[p, :, lanes] = block[p * cols : (p + 1) * cols]
-        r.g_router[:, lanes] = block[3 * cols : 3 * cols + experts]
-    block = r.b_full[...].reshape(2 * b_share, inner).astype(F32)
-    for p in range(3):
-        r.g_b_qkv[p] = block[p * cols : (p + 1) * cols]
+    late = [here(r.small_full, r.small_res), here(r.b_full, r.b_res)]
+    for copy in late:
+        copy.start()
+    for copy in results + late:
+        copy.wait()
     for copy in put_x:
         copy.wait()
     for copy in links.made:
         copy.wait_send()
+
+
+def hand_out(cols, experts, *refs):
+    y, gx, full, own, small, b_full = refs[:6]
+    y_out, gx_out, g_router, g_a_in, g_a_o, g_a_out, g_b_qkv, g_b_o, g_b_in, g_b_out = refs[6:16]
+    y_buf, x_buf, sems = refs[16:]
+    pieces = [(y, y_buf, y_out, 0, y.shape[0])]
+    part = gx.shape[0] // 4
+    pieces += [(gx, x_buf, gx_out, i * part, (i + 1) * part) for i in range(4)]
+    get = [
+        pltpu.make_async_copy(a.at[lo:hi], b.at[lo:hi], sems.at[i]) for i, (a, b, _, lo, hi) in enumerate(pieces)
+    ]
+    put = [
+        pltpu.make_async_copy(b.at[lo:hi], c.at[lo:hi], sems.at[5 + i]) for i, (_, b, c, lo, hi) in enumerate(pieces)
+    ]
+    for copy in get:
+        copy.start()
+    for one, two in zip(get, put):
+        one.wait()
+        two.start()
+    groups = full.shape[0]
+    hidden = g_a_out.shape[1] // groups
+    g_b_in[...] = own[...].astype(F32)[:cols]
+    for j in range(groups):
+        block = full[j].astype(F32)
+        g_a_out[:, j * hidden : (j + 1) * hidden] = block[:cols]
+        target = (g_a_o, g_b_o, g_b_out, g_a_in.at[3])[j]
+        target[...] = block[cols : 2 * cols]
+    count = 3 * cols + 16
+    tall = -(-count // 16) * 16
+    flat = small[...].reshape(small.shape[0] * small.shape[1], 128)
+    for i in range(g_router.shape[1] // 128):
+        block = flat[i * tall : (i + 1) * tall].astype(F32)
+        lanes = slice(i * 128, (i + 1) * 128)
+        for p in range(3):
+            g_a_in[p, :, lanes] = block[p * cols : (p + 1) * cols]
+        g_router[:, lanes] = block[3 * cols : 3 * cols + experts]
+    block = b_full[...].reshape(b_full.shape[0] * b_full.shape[1], b_full.shape[2]).astype(F32)
+    for p in range(3):
+        g_b_qkv[p] = block[p * cols : (p + 1) * cols]
+    for copy in put:
+        copy.wait()
 
 
 def shards(
@@ -869,17 +908,25 @@
     outs = {
         "y": ((tokens, width), BF16, pl.ANY),
         "gx": ((tokens, width), F32, pl.ANY),
-        "g_router": ((experts, width), F32, pltpu.VMEM),
-        "g_a_in": ((4, cols, width), F32, pltpu.VMEM),
-        "g_a_o": ((cols, width), F32, pltpu.VMEM),
-        "g_a_out": ((cols, groups * hidden), F32, pltpu.VMEM),
-        "g_b_qkv": ((3, cols, inner), F32, pltpu.VMEM),
-        "g_b_o": ((cols, width), F32, pltpu.VMEM),
-        "g_b_in": ((cols, hidden), F32, pltpu.VMEM),
-        "g_b_out": ((cols, width), F32, pltpu.VMEM),
+        "full_out": ((groups, 128, width), BF16, pl.ANY),
+        "own_out": ((128 - 2 * cols, width), BF16, pl.ANY),
+        "small_res": ((8, 112, 128), BF16, pl.ANY),
+        "b_res": ((2, 64, inner), BF16, pl.ANY),
         "win_all": ((groups * width, hidden), BF16, pl.ANY),
         "z_all": ((zs * 64, width), BF16, pl.ANY),
     }
+    given = [
+        ((tokens, width), BF16, pl.ANY),
+        ((tokens, width), F32, pl.ANY),
+        ((experts, width), F32, pltpu.VMEM),
+        ((4, cols, width), F32, pltpu.VMEM),
+        ((cols, width), F32, pltpu.VMEM),
+        ((cols, groups * hidden), F32, pltpu.VMEM),
+        ((3, cols, inner), F32, pltpu.VMEM),
+        ((cols, width), F32, pltpu.VMEM),
+        ((cols, hidden), F32, pltpu.VMEM),
+        ((cols, width), F32, pltpu.VMEM),
+    ]
     line = (PAD, tokens)
     scratch = {
         "xy": ((tokens, width), BF16),
@@ -951,7 +998,19 @@
             vmem_limit_bytes=VMEM_LIMIT, collective_id=0, has_side_effects=True
         ),
     )(*[i[0] for i in ins.values()])
-    y, gx, g_router, g_in, g_ao, g_aout, g_bqkv, g_bo, g_bin, g_bout = results[:10]
+    y, gx, g_router, g_in, g_ao, g_aout, g_bqkv, g_bo, g_bin, g_bout = pl.pallas_call(
+        lambda *refs: hand_out(cols, experts, *refs),
+        name="hand_out",
+        out_shape=[jax.ShapeDtypeStruct(o[0], o[1]) for o in given],
+        in_specs=[pl.BlockSpec(memory_space=pl.ANY)] * 2 + [pl.BlockSpec(memory_space=pltpu.VMEM)] * 4,
+        out_specs=[pl.BlockSpec(memory_space=o[2]) for o in given],
+        scratch_shapes=[
+            pltpu.VMEM((tokens, width), BF16),
+            pltpu.VMEM((tokens, width), F32),
+            pltpu.SemaphoreType.DMA((10,)),
+        ],
+        compiler_params=pltpu.CompilerParams(vmem_limit_bytes=VMEM_LIMIT),
+    )(*results[:6])
     return (
         y.reshape(layer_inputs.shape),
         gx.reshape(layer_inputs.shape),

time: 144 us -> 132 us (0.917)
  local copies, waits for them, and re-layouts: 9.93 us -> 0 us
  Pallas kernels: 133 us -> 130 us
    unnamed x28 -> x0, local copies, waits for them, and re-layouts: 9.93 us -> none
    pallas_call x1, Pallas kernels: 133 us -> 124 us  [shards(): pl.pallas_call(lambda *refs: layer(names, sizes, *refs), name='encoder_la...]
    pallas_call x0 -> x1, Pallas kernels: none -> 6.04 us  [shards(): pl.pallas_call(lambda *refs: hand_out(cols, experts, *refs), name='hand_o...]
where the time goes in v5:
time: 132 us; the launch traced here: 131 us
  Pallas kernels  130 us (98%)
    pallas_call x1, Pallas kernels, shards(): pl.pallas_call(lambda *refs: layer(names, sizes, *refs), name='encoder_la...  124 us
    pallas_call x1, Pallas kernels, shards(): pl.pallas_call(lambda *refs: hand_out(cols, experts, *refs), name='hand_o...  6.04 us

profile of v5, /device:TPU:0, one launch (start us, length us, event | category | flops | bytes accessed | tf_op | source)
XLA Modules:
  0.0 130.7 jit_solution(5611487761774263965)
XLA Ops:
  0.7 123.9 %encoder_layer.1 = (bf16[1024,768]{1,0:T(8,128)(2,1)}, f32[1024,768]{1,0:T(8,128)}, bf16[4,128,768]{2,1,0:T(8,128)(2,1)}, bf16[48,768]{1,0:T(8,128)(2,1)}, bf16[...) custom-call(s32[2]{0:T(128)} %refs_0_.1, ...), custom_call_target="tpu_custom_call" | custom-call | flops 67645734912 | bytes 31457280 | tf_op jit(solution)/shard_map/encoder_layer/pallas_call | solution.py:989
  124.5 6.0 %hand_out.1 = (bf16[1024,768]{1,0:T(8,128)(2,1)}, f32[1024,768]{1,0:T(8,128)}, f32[10,768]{1,0:T(8,128)}, f32[4,40,768]{2,1,0:T(8,128)}, f32[40,768]{1,0:T(8,128...) custom-call(bf16[1024,768]{1,0:T(8,128)(2,1)} %get-tuple-element.26., ...), custom_call_target="tpu_custom_call" | custom-call | tf_op jit(solution)/shard_map/hand_out/pallas_call | solution.py:1001

commit v6 on v5

--- a/solution.py
+++ b/solution.py
@@ -140,6 +140,9 @@
     return (ids[None, :] == np.arange(NB)[:, None]).astype(np.float32)
 
 
+SMALL = ("b_qkv", "table", "b_in", "g1", "g2", "at", "router", "onehot", "a_o", "b_o", "a_out", "b_out")
+
+
 class Names:
     def __init__(self, **refs):
         self.__dict__.update(refs)
@@ -156,9 +159,6 @@
     z = d // 2
     links = Links(r.send, r.recv)
 
-    def gb_rows(g, p):
-        return ds(4 * PAD + (g * 3 + p) * PAD, PAD)
-
     r.zed = r.low_in
     r.dsmall = r.dctx.at[: 4 * PAD]
     r.d_low = [r.low_out, r.d_low_in, r.d_low_out]
@@ -173,6 +173,7 @@
         local[0] += 1
         return pltpu.make_async_copy(src, dst, r.local.at[local[0] - 1])
 
+    get_small = [here(getattr(r, n + "_far"), getattr(r, n)) for n in SMALL]
     get_x = here(r.x, r.xy)
     get_c = here(r.c, r.cot)
     get_qkv = [
@@ -183,9 +184,11 @@
         for h in range(heads_here)
         for p in range(3)
     ]
-    get_x.start()
     for copy in get_qkv:
         copy.start()
+    for copy in get_small:
+        copy.start()
+    get_x.start()
 
     z_peers = [((z + i) % zs * 2 + half, t) for i in range(1, zs)]
     same_x = [(half * 4 + j, (d, j)) for j in (places.core_t, places.y_t, places.far_t)]
@@ -230,6 +233,8 @@
         here(r.wout_own, quarter_of(r.wout, t, hidden)),
     ]
 
+    for copy in get_small:
+        copy.wait()
     for p in range(3):
         r.bq[t, p * RANK_PAD : (p + 1) * RANK_PAD] = filled(r.b_qkv[p], RANK_PAD)
     pick = lax.broadcasted_iota(jnp.int32, (16, heads_here), 0)
@@ -607,13 +612,16 @@
     give = []
     for j, dev in block_peers:
         give.append(links(r.small_out.at[ds(j * share, share)], r.small_in.at[me], dev))
-        give.append(links(r.b_all.at[j % 4, ds(j // 4 * b_share, b_share)], r.b_in_sum.at[me], dev))
-    cross = []
-    for dev in z_peers:
-        cross.append(links(r.small_z.at[z], r.small_z.at[z], dev))
-        cross.append(links(r.b_z.at[z], r.b_z.at[z], dev))
+    b_give = []
+    for g in (t, places.core_t, places.y_t, places.far_t):
+        there = [(1 - half, (flip(d, 1), g))] + ([(half, (d, g))] if b_give else [])
+        b_give.append(
+            [links(r.b_all.at[g, ds(h * b_share, b_share)], r.b_in_sum.at[me], dev) for h, dev in there]
+        )
+    cross = [links(r.small_z.at[z], r.small_z.at[z], dev) for dev in z_peers]
+    b_cross = [links(r.b_z.at[z], r.b_z.at[z], dev) for dev in z_peers]
     back = [links(r.small_full.at[me], r.small_full.at[me], dev) for _, dev in block_peers]
-    back.append(links(r.b_full.at[half], r.b_full.at[half], places.x))
+    b_back = links(r.b_full.at[half], r.b_full.at[half], places.x)
 
     def sum_step(step):
         if step == 0:
@@ -627,12 +635,12 @@
             r.part[t] += r.core_in[:128].astype(F32)
             put_y.wait()
             get_x_again.start()
-        if step == 5:
+        if step == 6:
             to_y.wait_recv()
             r.part[t] += r.y_in[...].astype(F32)
             r.x_out[...] = r.part[t, other, :].astype(BF16)
             to_x.start()
-        if step == 7:
+        if step == 9:
             to_x.wait_recv()
             r.z_out[...] = (r.part[t, mine, :] + r.x_in[...].astype(F32)).astype(BF16)
             keep_z.start()
@@ -704,31 +712,37 @@
                 score(i + ahead)
             grads(i)
 
-    def backward_head(n, c):
-        for step in (0, 2, 5, 7):
-            pl.when(n == step)(lambda step=step: sum_step(step))
-        attend_back(n)
-        return c
-
-    lax.fori_loop(0, heads, backward_head, 0)
-    sum_z()
-
-    gsm = r.acc.at[: 4 * PAD]
-
-    def adapters(g, c):
+    def adapters(k):
+        g = group_at(t, k)
+        block = []
         for p in range(3):
             dp = [
                 r.qkv[ds((g * heads_here + h) * span + p * hd, hd), :] for h in range(heads_here)
             ]
             dp = jnp.concatenate(dp, axis=0)
-            low = nn(r.bq[g, p * RANK_PAD : (p + 1) * RANK_PAD], dp)
-            r.d_low[p][:RANK_PAD, :] += low
-            r.acc[gb_rows(g, p), :inner] = nt(r.gated[p * PAD : (p + 1) * PAD, :], dp)
-        return c
+            r.d_low[p][:RANK_PAD, :] += nn(r.bq[g, p * RANK_PAD : (p + 1) * RANK_PAD], dp)
+            block.append(nt(r.gated[p * PAD : (p + 1) * PAD, :], dp)[:cols])
+        block.append(jnp.zeros((r.b_all.shape[1] - 3 * cols, inner), F32))
+        r.b_all[g] = jnp.concatenate(block, axis=0).astype(BF16)
+        if k < groups - 1:
+            for copy in b_give[k]:
+                copy.start()
 
     for p in range(3):
         r.d_low[p][...] = jnp.zeros(r.d_low[p].shape, F32)
-    lax.fori_loop(0, groups, adapters, 0)
+
+    def backward_head(n, c):
+        for k in range(groups - 1):
+            pl.when(n == (k + 1) * heads_here)(lambda k=k: adapters(k))
+        for step in (0, 2, 6, 9):
+            pl.when(n == step)(lambda step=step: sum_step(step))
+        attend_back(n)
+        return c
+
+    lax.fori_loop(0, heads, backward_head, 0)
+    adapters(groups - 1)
+
+    gsm = r.acc.at[: 4 * PAD]
     gate = r.gate[...]
     prod = r.zed[...]
     for p in range(3):
@@ -756,15 +770,8 @@
     for i in range(strips):
         r.small_out[i * tall : (i + 1) * tall, :] = lines[:, i * 128 : (i + 1) * 128]
     r.small_out[strips * tall :, :] = jnp.zeros((r.small_out.shape[0] - strips * tall, 128), BF16)
-    for j in range(groups):
-        block = [r.acc[gb_rows(j, p), :inner][:cols] for p in range(3)]
-        block.append(jnp.zeros((r.b_all.shape[1] - 3 * cols, inner), F32))
-        r.b_all[j] = jnp.concatenate(block, axis=0).astype(BF16)
-    for copy in give:
+    for copy in give + b_give[groups - 1]:
         copy.start()
-    all_x.wait_recv()
-    all_y.start()
-    all_core[0].start()
     get_x_again.wait()
 
     def finish(i, c):
@@ -780,40 +787,54 @@
     put_x = [here(r.h1.at[i * part_rows : (i + 1) * part_rows], r.gx.at[i * part_rows : (i + 1) * part_rows]) for i in range(2)]
     lax.fori_loop(0, tokens // tb // 2, finish, 0)
     put_x[0].start()
-    all_y.wait_recv()
-    all_core[1].start()
+    sum_z()
     for copy in give:
         copy.wait_recv()
     r.small_in[me] = r.small_out[ds(me * share, share), :]
-    r.b_in_sum[me] = r.b_all[t, ds(half * b_share, b_share), :]
     total = r.small_in[0].astype(F32)
-    total_b = r.b_in_sum[0].astype(F32)
     for i in range(1, 8):
         total = total + r.small_in[i].astype(F32)
-        total_b = total_b + r.b_in_sum[i].astype(F32)
     r.small_z[z] = total.astype(BF16)
-    r.b_z[z] = total_b.astype(BF16)
     for copy in cross:
+        copy.start()
+    for copies in b_give:
+        for copy in copies:
+            copy.wait_recv()
+    r.b_in_sum[me] = r.b_all[t, ds(half * b_share, b_share), :]
+    total = r.b_in_sum[0].astype(F32)
+    for i in range(1, 8):
+        total = total + r.b_in_sum[i].astype(F32)
+    r.b_z[z] = total.astype(BF16)
+    for copy in b_cross:
         copy.start()
     lax.fori_loop(tokens // tb // 2, tokens // tb, finish, 0)
     put_x[1].start()
+    all_x.wait_recv()
+    all_y.start()
+    all_core[0].start()
     for copy in cross:
         copy.wait_recv()
     total = r.small_z[0].astype(F32)
-    total_b = r.b_z[0].astype(F32)
     for i in range(1, zs):
         total = total + r.small_z[i].astype(F32)
-        total_b = total_b + r.b_z[i].astype(F32)
     r.small_full[me] = total.astype(BF16)
-    r.b_full[half] = total_b.astype(BF16)
     for copy in back:
         copy.start()
+    for copy in b_cross:
+        copy.wait_recv()
+    total = r.b_z[0].astype(F32)
+    for i in range(1, zs):
+        total = total + r.b_z[i].astype(F32)
+    r.b_full[half] = total.astype(BF16)
+    b_back.start()
+    all_y.wait_recv()
+    all_core[1].start()
     for copy in all_core:
         copy.wait_recv()
     results = [here(r.full, r.full_out), here(r.full.at[t, 2 * cols :], r.own_out)]
     for copy in results:
         copy.start()
-    for copy in back:
+    for copy in back + [b_back]:
         copy.wait_recv()
     late = [here(r.small_full, r.small_res), here(r.b_full, r.b_res)]
     for copy in late:
@@ -886,18 +907,18 @@
     sizes = (tokens, width, seq, seqs, groups, inner, heads_here, hd, hidden, cols, experts, zs)
     ins = {
         "lens": (lengths, pltpu.SMEM),
-        "g1": (first_gain, pltpu.VMEM),
-        "g2": (second_gain, pltpu.VMEM),
-        "at": (jnp.swapaxes(a_in, 1, 2), pltpu.VMEM),
-        "router": (router.T, pltpu.VMEM),
-        "onehot": (jnp.asarray(bucket_lines(seq), BF16), pltpu.VMEM),
-        "b_qkv": (b_qkv, pltpu.VMEM),
-        "table": (bias_table.T, pltpu.VMEM),
-        "b_in": (b_in, pltpu.VMEM),
-        "a_o": (a_o.T, pltpu.VMEM),
-        "b_o": (b_o, pltpu.VMEM),
-        "a_out": (a_out.T, pltpu.VMEM),
-        "b_out": (b_out, pltpu.VMEM),
+        "g1": (first_gain, pl.ANY),
+        "g2": (second_gain, pl.ANY),
+        "at": (jnp.swapaxes(a_in, 1, 2), pl.ANY),
+        "router": (router.T, pl.ANY),
+        "onehot": (jnp.asarray(bucket_lines(seq), BF16), pl.ANY),
+        "b_qkv": (b_qkv, pl.ANY),
+        "table": (bias_table.T, pl.ANY),
+        "b_in": (b_in, pl.ANY),
+        "a_o": (a_o.T, pl.ANY),
+        "b_o": (b_o, pl.ANY),
+        "a_out": (a_out.T, pl.ANY),
+        "b_out": (b_out, pl.ANY),
         "x": (layer_inputs.reshape(tokens, width), pl.ANY),
         "c": (cotangent.reshape(tokens, width), pl.ANY),
         "wqkv_own": (jnp.swapaxes(wqkv, 1, 2), pl.ANY),
@@ -905,6 +926,8 @@
         "win_own": (win, pl.ANY),
         "wout_own": (wout, pl.ANY),
     }
+    landing = {n: (ins[n][0].shape, ins[n][0].dtype) for n in SMALL}
+    ins = {n + "_far" if n in SMALL else n: v for n, v in ins.items()}
     outs = {
         "y": ((tokens, width), BF16, pl.ANY),
         "gx": ((tokens, width), F32, pl.ANY),
@@ -981,9 +1004,10 @@
         "b_z": ((zs, 64, inner), BF16),
         "b_full": ((2, 64, inner), BF16),
     }
+    scratch.update(landing)
     copies = 9 * 8 + 40 + 3 * zs
     shapes = [pltpu.VMEM(*v) for v in scratch.values()]
-    shapes += [pltpu.SemaphoreType.DMA((copies,)), pltpu.SemaphoreType.DMA((copies,)), pltpu.SemaphoreType.DMA((40,))]
+    shapes += [pltpu.SemaphoreType.DMA((copies,)), pltpu.SemaphoreType.DMA((copies,)), pltpu.SemaphoreType.DMA((64,))]
     names = list(ins) + list(outs) + list(scratch) + ["send", "recv", "local"]
     flops = 2 * tokens * (8 * width * hidden * groups + 24 * width * width)
     results = pl.pallas_call(

time: 132 us -> 124 us (0.939)
  Pallas kernels: 130 us -> 123 us
    pallas_call x1, Pallas kernels: 124 us -> 117 us  [shards(): pl.pallas_call(lambda *refs: layer(names, sizes, *refs), name='encoder_la...]
where the time goes in v6:
time: 124 us
  Pallas kernels  123 us (99%)
    pallas_call x1, Pallas kernels, shards(): pl.pallas_call(lambda *refs: layer(names, sizes, *refs), name='encoder_la...  117 us
    pallas_call x1, Pallas kernels, shards(): pl.pallas_call(lambda *refs: hand_out(cols, experts, *refs), name='hand_o...  6.04 us

profile of v6, /device:TPU:0, one launch (start us, length us, event | category | flops | bytes accessed | tf_op | source)
XLA Modules:
  0.0 124.1 jit_solution(14443527110449949608)
XLA Ops:
  0.7 117.2 %encoder_layer.1 = (bf16[1024,768]{1,0:T(8,128)(2,1)}, f32[1024,768]{1,0:T(8,128)}, bf16[4,128,768]{2,1,0:T(8,128)(2,1)}, bf16[48,768]{1,0:T(8,128)(2,1)}, bf16[...) custom-call(s32[2]{0:T(128)} %refs_0_.1, ...), custom_call_target="tpu_custom_call" | custom-call | flops 67645734912 | bytes 31457280 | tf_op jit(solution)/shard_map/encoder_layer/pallas_call | solution.py:1013
  117.9 6.0 %hand_out.1 = (bf16[1024,768]{1,0:T(8,128)(2,1)}, f32[1024,768]{1,0:T(8,128)}, f32[10,768]{1,0:T(8,128)}, f32[4,40,768]{2,1,0:T(8,128)}, f32[40,768]{1,0:T(8,128...) custom-call(bf16[1024,768]{1,0:T(8,128)(2,1)} %get-tuple-element.26., ...), custom_call_target="tpu_custom_call" | custom-call | tf_op jit(solution)/shard_map/hand_out/pallas_call | solution.py:1025

commit v7 on v6

--- a/solution.py
+++ b/solution.py
@@ -382,15 +382,15 @@
         if step == 0:
             qkv_chunks[0].relay()
         if step == 1:
+            qkv_chunks[1].relay()
             in_chunks[0].start()
         if step == 2:
-            qkv_chunks[1].relay()
+            qkv_chunks[2].relay()
             core_qkv.wait_recv()
             small_core[0].wait_recv()
             small_core[1].wait_recv()
             core_o.start()
         if step == 3:
-            qkv_chunks[2].relay()
             qkv_chunks[0].forward()
             in_chunks[1].start()
         if step == 4:
@@ -481,6 +481,8 @@
             gated = (low * gate).astype(BF16)
             h1 = r.xy[rows, :].astype(F32) + tn(ctx, r.wo[...]) + tn(gated, r.bo[...])
             r.h1[rows, :] = h1
+            r.acc[rows, :] = h1
+            r.dn2[rows, :] = jnp.zeros_like(h1)
             n2 = (h1 * lax.rsqrt(jnp.mean(h1 * h1, axis=1, keepdims=True) + EPS) * g2).astype(BF16)
             r.n2[rows, :] = n2
             low = nt(r.ain[...], n2)
@@ -492,8 +494,6 @@
         return c
 
     lax.fori_loop(0, tokens // tb // 2, first, 0)
-    r.acc[...] = jnp.zeros_like(r.acc)
-    r.dn2[...] = jnp.zeros_like(r.dn2)
     r.low_out[...] = jnp.zeros_like(r.low_out)
     r.d_low_in[...] = jnp.zeros_like(r.d_low_in)
     r.part[...] = jnp.zeros_like(r.part)
@@ -570,7 +570,7 @@
             cot, n2, ctx, h1 = r.cot[rows, :], r.n2[rows, :], r.ctx[:, rows], r.h1[rows, :]
             low_out, d_low_in = r.low_out[:, rows], r.d_low_in[:, rows]
             go = (low_out * gate).astype(BF16)
-            r.xy[rows, :] = (h1 + r.acc[rows, :] + tn(go, r.bout[...])).astype(BF16)
+            r.xy[rows, :] = (r.acc[rows, :] + tn(go, r.bout[...])).astype(BF16)
             dgi = (d_low_in * gate).astype(BF16)
             up = (r.dn2[rows, :] + tn(dgi, r.ain[...])) * g2
             r.part[2, cols : 2 * cols] += nn(go, cot)[:cols]
@@ -812,6 +812,10 @@
     all_x.wait_recv()
     all_y.start()
     all_core[0].start()
+    late_sends = cross + b_cross + back + [b_back, all_x, all_y] + all_core
+    for copy in links.made:
+        if not any(copy is x for x in late_sends):
+            copy.wait_send()
     for copy in cross:
         copy.wait_recv()
     total = r.small_z[0].astype(F32)
@@ -843,14 +847,21 @@
         copy.wait()
     for copy in put_x:
         copy.wait()
-    for copy in links.made:
+    for copy in late_sends:
         copy.wait_send()
 
 
 def hand_out(cols, experts, *refs):
-    y, gx, full, own, small, b_full = refs[:6]
-    y_out, gx_out, g_router, g_a_in, g_a_o, g_a_out, g_b_qkv, g_b_o, g_b_in, g_b_out = refs[6:16]
-    y_buf, x_buf, sems = refs[16:]
+    y, gx = refs[:2]
+    y_out, gx_out = refs[6:8]
+    y_buf, x_buf = refs[16:18]
+    full, own, small, b_full = refs[18:22]
+    g_router, g_a_in, g_a_o, g_a_out, g_b_qkv, g_b_o, g_b_in, g_b_out = refs[22:30]
+    sems = refs[30]
+    load = [pltpu.make_async_copy(a, b, sems.at[20 + i]) for i, (a, b) in enumerate(zip(refs[2:6], refs[18:22]))]
+    store = [pltpu.make_async_copy(b, a, sems.at[24 + i]) for i, (a, b) in enumerate(zip(refs[8:16], refs[22:30]))]
+    for copy in load:
+        copy.start()
     pieces = [(y, y_buf, y_out, 0, y.shape[0])]
     part = gx.shape[0] // 4
     pieces += [(gx, x_buf, gx_out, i * part, (i + 1) * part) for i in range(4)]
@@ -858,13 +869,12 @@
         pltpu.make_async_copy(a.at[lo:hi], b.at[lo:hi], sems.at[i]) for i, (a, b, _, lo, hi) in enumerate(pieces)
     ]
     put = [
-        pltpu.make_async_copy(b.at[lo:hi], c.at[lo:hi], sems.at[5 + i]) for i, (_, b, c, lo, hi) in enumerate(pieces)
+        pltpu.make_async_copy(b.at[lo:hi], c.at[lo:hi], sems.at[10 + i]) for i, (_, b, c, lo, hi) in enumerate(pieces)
     ]
     for copy in get:
         copy.start()
-    for one, two in zip(get, put):
-        one.wait()
-        two.start()
+    for copy in load:
+        copy.wait()
     groups = full.shape[0]
     hidden = g_a_out.shape[1] // groups
     g_b_in[...] = own[...].astype(F32)[:cols]
@@ -885,7 +895,12 @@
     block = b_full[...].reshape(b_full.shape[0] * b_full.shape[1], b_full.shape[2]).astype(F32)
     for p in range(3):
         g_b_qkv[p] = block[p * cols : (p + 1) * cols]
-    for copy in put:
+    for copy in store:
+        copy.start()
+    for one, two in zip(get, put):
+        one.wait()
+        two.start()
+    for copy in put + store:
         copy.wait()
 
 
@@ -941,7 +956,7 @@
     given = [
         ((tokens, width), BF16, pl.ANY),
         ((tokens, width), F32, pl.ANY),
-        ((experts, width), F32, pltpu.VMEM),
+        ((experts, width), F32, pl.ANY),
         ((4, cols, width), F32, pltpu.VMEM),
         ((cols, width), F32, pltpu.VMEM),
         ((cols, groups * hidden), F32, pltpu.VMEM),
@@ -950,6 +965,8 @@
         ((cols, hidden), F32, pltpu.VMEM),
         ((cols, width), F32, pltpu.VMEM),
     ]
+    moved = [given[0][:2], given[1][:2]] + [outs[n][:2] for n in ("full_out", "own_out", "small_res", "b_res")]
+    moved += [g[:2] for g in given[2:]]
     line = (PAD, tokens)
     scratch = {
         "xy": ((tokens, width), BF16),
@@ -1026,13 +1043,9 @@
         lambda *refs: hand_out(cols, experts, *refs),
         name="hand_out",
         out_shape=[jax.ShapeDtypeStruct(o[0], o[1]) for o in given],
-        in_specs=[pl.BlockSpec(memory_space=pl.ANY)] * 2 + [pl.BlockSpec(memory_space=pltpu.VMEM)] * 4,
-        out_specs=[pl.BlockSpec(memory_space=o[2]) for o in given],
-        scratch_shapes=[
-            pltpu.VMEM((tokens, width), BF16),
-            pltpu.VMEM((tokens, width), F32),
-            pltpu.SemaphoreType.DMA((10,)),
-        ],
+        in_specs=[pl.BlockSpec(memory_space=pl.ANY)] * 6,
+        out_specs=[pl.BlockSpec(memory_space=pl.ANY)] * len(given),
+        scratch_shapes=[pltpu.VMEM(*v) for v in moved] + [pltpu.SemaphoreType.DMA((32,))],
         compiler_params=pltpu.CompilerParams(vmem_limit_bytes=VMEM_LIMIT),
     )(*results[:6])
     return (

time: 124 us -> 122 us (0.984)
  Pallas kernels: 123 us -> 121 us
where the time goes in v7:
time: 122 us
  Pallas kernels  121 us (99%)
    pallas_call x1, Pallas kernels, shards(): pl.pallas_call(lambda *refs: layer(names, sizes, *refs), name='encoder_la...  116 us
    pallas_call x1, Pallas kernels, shards(): pl.pallas_call(lambda *refs: hand_out(cols, experts, *refs), name='hand_o...  5.17 us

profile of v7, /device:TPU:0, one launch (start us, length us, event | category | flops | bytes accessed | tf_op | source)
XLA Modules:
  0.0 122.2 jit_solution(11641066237235390532)
XLA Ops:
  0.7 116.2 %encoder_layer.1 = (bf16[1024,768]{1,0:T(8,128)(2,1)}, f32[1024,768]{1,0:T(8,128)}, bf16[4,128,768]{2,1,0:T(8,128)(2,1)}, bf16[48,768]{1,0:T(8,128)(2,1)}, bf16[...) custom-call(s32[2]{0:T(128)} %refs_0_.1, ...), custom_call_target="tpu_custom_call" | custom-call | flops 67645734912 | bytes 31457280 | tf_op jit(solution)/shard_map/encoder_layer/pallas_call | solution.py:1030
  116.9 5.2 %hand_out.1 = (bf16[1024,768]{1,0:T(8,128)(2,1)}, f32[1024,768]{1,0:T(8,128)}, f32[10,768]{1,0:T(8,128)}, f32[4,40,768]{2,1,0:T(8,128)}, f32[40,768]{1,0:T(8,128...) custom-call(bf16[1024,768]{1,0:T(8,128)(2,1)} %get-tuple-element.26., ...), custom_call_target="tpu_custom_call" | custom-call | tf_op jit(solution)/shard_map/hand_out/pallas_call | solution.py:1042

commit v8 on v7

--- a/solution.py
+++ b/solution.py
@@ -787,7 +787,6 @@
     put_x = [here(r.h1.at[i * part_rows : (i + 1) * part_rows], r.gx.at[i * part_rows : (i + 1) * part_rows]) for i in range(2)]
     lax.fori_loop(0, tokens // tb // 2, finish, 0)
     put_x[0].start()
-    sum_z()
     for copy in give:
         copy.wait_recv()
     r.small_in[me] = r.small_out[ds(me * share, share), :]
@@ -797,6 +796,7 @@
     r.small_z[z] = total.astype(BF16)
     for copy in cross:
         copy.start()
+    sum_z()
     for copies in b_give:
         for copy in copies:
             copy.wait_recv()

time: 122 us -> 124 us (1.016); the launches traced: 122 us -> 123 us
  no operation moved by 1% of the time
where the time goes in v8:
time: 124 us; the launch traced here: 123 us
  Pallas kernels  122 us (98%)
    pallas_call x1, Pallas kernels, shards(): pl.pallas_call(lambda *refs: layer(names, sizes, *refs), name='encoder_la...  117 us
    pallas_call x1, Pallas kernels, shards(): pl.pallas_call(lambda *refs: hand_out(cols, experts, *refs), name='hand_o...  5.17 us

profile of v8, /device:TPU:0, one launch (start us, length us, event | category | flops | bytes accessed | tf_op | source)
XLA Modules:
  0.0 122.7 jit_solution(11729933586012490676)
XLA Ops:
  0.7 116.7 %encoder_layer.1 = (bf16[1024,768]{1,0:T(8,128)(2,1)}, f32[1024,768]{1,0:T(8,128)}, bf16[4,128,768]{2,1,0:T(8,128)(2,1)}, bf16[48,768]{1,0:T(8,128)(2,1)}, bf16[...) custom-call(s32[2]{0:T(128)} %refs_0_.1, ...), custom_call_target="tpu_custom_call" | custom-call | flops 67645734912 | bytes 31457280 | tf_op jit(solution)/shard_map/encoder_layer/pallas_call | solution.py:1030
  117.3 5.2 %hand_out.1 = (bf16[1024,768]{1,0:T(8,128)(2,1)}, f32[1024,768]{1,0:T(8,128)}, f32[10,768]{1,0:T(8,128)}, f32[4,40,768]{2,1,0:T(8,128)}, f32[40,768]{1,0:T(8,128...) custom-call(bf16[1024,768]{1,0:T(8,128)(2,1)} %get-tuple-element.26., ...), custom_call_target="tpu_custom_call" | custom-call | tf_op jit(solution)/shard_map/hand_out/pallas_call | solution.py:1042
